TPU v7x, 32 devices: a whole 2x2x4 slice. The times are simulated.
32 devices in a mesh: groups: 2 (over y), tm: 4 (over z), rows: 4 (over x, core).
Axes of the slice: x: 2, y: 2, z: 4, core: 2. Of those that a mesh axis runs over, the one named last changes fastest.
Arguments:
- latents: bfloat16 [16, 16, 128, 256], P(('groups', 'tm'), 'rows'), parts along dimension 0, may hold values from -6 to 6
- weight_in: bfloat16 [3, 3, 256, 256], replicated, may hold values from -0.125 to 0.125
- weight_out: bfloat16 [3, 3, 256, 256], replicated, may hold values from -0.0234375 to 0.0234375
- decay_table: float32 [16], replicated, may hold values from 0.99 to 0.999
- decay_index: int32 [256], replicated, may hold values from 0 to 15
Outputs:
- updated: bfloat16 [16, 16, 128, 256], P(('groups', 'tm'), 'rows'), parts along dimension 0
There are 2 independent parts, one for each index of `groups`. A program takes and returns all parts, laid end to end along the dimension named above; an argument that names none is the same for every part. Nothing has to cross between parts.
All inputs are finite; a program needn't handle non-finite values.
Results may differ from a plain program's by a relative error of at most 0.0032.
Values may be sent and summed in bfloat16 or wider, within the bound.
No kernel may reach another device: no remote copies, remote signals or barrier semaphores. Data moves between devices by JAX's collectives and lax.ppermute only.
A program may use at most 64 MiB of HBM per device.

v0:
```python
import jax
import jax.numpy as jnp
from jax import lax
from jax.sharding import PartitionSpec as P


def extended(block, sides, width):
    for axis, dim in sides:
        count = lax.axis_size(axis)
        forward = [(i, i + 1) for i in range(count - 1)]
        backward = [(target, source) for source, target in forward]
        low = lax.ppermute(
            lax.slice_in_dim(block, block.shape[dim] - width, None, axis=dim), axis, forward
        )
        high = lax.ppermute(lax.slice_in_dim(block, 0, width, axis=dim), axis, backward)
        block = jnp.concatenate([low, block, high], axis=dim)
    return block


def carried_in(value, axis, join, neutral):
    count, mine = (lax.axis_size(axis), lax.axis_index(axis))
    pieces = jax.tree.map(lambda part: lax.all_gather(part, axis), value)
    so_far = jax.tree.map(
        lambda part, zero: jnp.full_like(part, 0) + jnp.asarray(zero, part.dtype), value, neutral
    )

    def hop(position, so_far):
        longer = join(so_far, jax.tree.map(lambda part: part[position], pieces))
        return jax.tree.map(lambda new, old: jnp.where(position < mine, new, old), longer, so_far)

    return lax.fori_loop(0, count - 1, hop, so_far)


def convolve(padded, weight, count):
    frames = padded.shape[0]
    width = padded.shape[2]
    depth = weight.shape[2]
    widened = jnp.pad(padded, ((0, 0), (0, 0), (1, 1), (0, 0)))
    total = jnp.zeros((frames * count * width, weight.shape[3]), jnp.float32)
    for tap_row in range(3):
        for tap_col in range(3):
            window = widened[:, tap_row : tap_row + count, tap_col : tap_col + width, :].reshape(
                -1, depth
            )
            total = total + jnp.dot(
                window, weight[tap_row, tap_col], preferred_element_type=jnp.float32
            )
    return total.reshape(frames, count, width, weight.shape[3])


def combine(earlier, later):
    return (earlier[0] * later[0], later[0] * earlier[1] + later[1])


def local_states(driven, decays):
    running = jnp.zeros(driven.shape[1:], jnp.float32)
    gathered = []
    for moment in range(driven.shape[0]):
        running = decays * running + driven[moment]
        gathered.append(running)
    return (jnp.stack(gathered), running)


def finish(partial_value, carried_state, decays):
    frames = partial_value.shape[0]
    growth = decays[None, :] ** jnp.arange(1, frames + 1, dtype=jnp.float32)[:, None]
    return partial_value + growth[:, None, None, :] * carried_state[None]


def local(latents, weight_in, weight_out, decay_table, decay_index):
    frames, strip, width, channels = latents.shape
    levels = decay_table.shape[0]
    onehot = decay_index[:, None] == jnp.arange(levels, dtype=jnp.int32)[None, :]
    decays = jnp.sum(jnp.where(onehot, decay_table[None, :], 0.0), axis=1)
    powers = decays ** float(frames)
    padded = extended(latents, (("rows", 1),), 1)
    driven = convolve(padded, weight_in, strip)
    partial_value, last_state = local_states(driven, decays)
    identity = (jnp.ones_like(decays), jnp.zeros(last_state.shape, jnp.float32))
    _, carried = carried_in((powers, last_state), "tm", combine, identity)
    rounded = finish(partial_value, carried, decays).astype(jnp.bfloat16)
    padded_states = extended(rounded, (("rows", 1),), 1)
    mixed = convolve(padded_states, weight_out, strip)
    return (latents.astype(jnp.float32) + jax.nn.gelu(mixed)).astype(jnp.bfloat16)


def solution(mesh):
    in_specs = (P(("groups", "tm"), "rows", None, None), P(), P(), P(), P())
    out_specs = P(("groups", "tm"), "rows", None, None)
    return jax.shard_map(local, mesh=mesh, in_specs=in_specs, out_specs=out_specs, check_vma=False)
```

profile of v0, /device:TPU:1, one launch (start us, length us, event | category | flops | bytes accessed | tf_op | source)
XLA Modules:
  0.0 98.3 jit_solution(2424338155233784217)
XLA Ops:
  6.5 1.0 %fusion.63 = (bf16[2,1,128,256]{3,2,1,0:T(8,128)(2,1)S(1)}, bf16[2,1,128,256]{3,2,1,0:T(8,128)(2,1)S(1)}) fusion(bf16[2,4,128,256]{3,2,1,0:T(8,128)(2,1)} %param.7), kind=kLoop, calls=%fused_computation.97 | loop fusion | bytes 524288 | tf_op jit(solution)/shard_map/slice | solution.py:13
  7.5 4.5 %collective-permute-start = (bf16[2,1,128,256]{3,2,1,0:T(8,128)(2,1)S(1)}, bf16[2,1,128,256]{3,2,1,0:T(8,128)(2,1)S(1)}, u32[]{:S(2)}, u32[]{:S(2)}) collective-permute-start(bf16[2,1,128,256]{3,2,1,0:T(8,128)(2,1)S(1)} %get-tuple-element.150), channel_id=1, source_target_pairs={{0,1},{1,2},{2,3},{4,5},{5,6},{6,7},{8,9},{9,10},{10,11},{12,13},{... | collective-permute-start | bytes 393224 | tf_op jit(solution)/shard_map/ppermute | solution.py:12
  12.0 1.9 %collective-permute-start.1 = (bf16[2,1,128,256]{3,2,1,0:T(8,128)(2,1)S(1)}, bf16[2,1,128,256]{3,2,1,0:T(8,128)(2,1)S(1)}, u32[]{:S(2)}, u32[]{:S(2)}) collective-permute-start(bf16[2,1,128,256]{3,2,1,0:T(8,128)(2,1)S(1)} %get-tuple-element.151), channel_id=1, source_target_pairs={{1,0},{2,1},{3,2},{5,4},{6,5},{7,6},{9,8},{10,9},{11,10},{13,12},{... | collective-permute-start | bytes 393224 | tf_op jit(solution)/shard_map/ppermute | solution.py:15
  14.0 0.8 select_reduce_fusion
  14.8 3.6 %collective-permute-done.1 = bf16[2,1,128,256]{3,2,1,0:T(8,128)(2,1)S(1)} collective-permute-done((bf16[2,1,128,256]{3,2,1,0:T(8,128)(2,1)S(1)}, bf16[2,1,128,256]{3,2,1,0:T(8,128)(2,1)S(1)}, u32[]{:S(2)}, u32[]{:S(2)}) %collective-permute-start.1) | collective-permute-done | bytes 131104 | tf_op jit(solution)/shard_map/ppermute | solution.py:15
  18.3 1.3 %fusion.18 = bf16[2,6,130,256]{3,2,1,0:T(8,128)(2,1)S(1)} fusion(bf16[2,1,128,256]{3,2,1,0:T(8,128)(2,1)S(1)} %collective-permute-done.1, bf16[2,4,128,256]{3,2,1,0:T(8,128)(2,1)} %param.7, bf16[2,1,128,256]{3,2,1,0:T(8,128)(2,1)S(1)} %collective-permute-done), kind=kLoop, calls=%fused_computation.40 | loop fusion | flops 4792320 | bytes 1585152 | tf_op jit(solution)/shard_map/concatenate | solution.py:16
  19.6 0.4 fusion.61
  20.0 0.8 copy-done.2
  20.9 0.3 fusion.39
  21.2 0.3 fusion.30
  21.5 0.7 copy-done
  22.2 0.1 pad_maximum_fusion.2
  22.3 0.3 convolution_add_fusion.13
  22.6 0.3 convolution_add_fusion.12
  22.9 0.3 convolution_add_fusion.11
  23.2 0.3 convolution_add_fusion.10
  23.5 0.3 convolution_add_fusion.9
  23.8 0.3 convolution_add_fusion.8
  24.1 0.3 fusion.3
  24.4 0.1 fusion.59
  24.5 0.9 multiply_add_fusion
  25.4 0.0 all-gather.4.cloned.1.call-update
  25.4 9.2 %all-gather.1 = f32[4,1,256]{2,1,0:T(1,128)S(1)} all-gather(f32[1,1,256]{2,1,0:T(1,128)S(1)} %bitcast.129), channel_id=2, replica_groups=mesh['groups'=2,'tm'=4,'rows'=4] {'tm'}, dimensions={0}, use_global_device_ids=true | all-gather | bytes 5120 | tf_op jit(solution)/shard_map/all_gather | solution.py:22
  34.6 0.1 broadcast_power_fusion
  34.7 36.6 %all-gather.4.cloned.1.call-done = f32[4,4,128,256]{3,2,1,0:T(8,128)} async-done(((f32[1,4,128,256]{3,2,1,0:T(8,128)}), f32[4,4,128,256]{3,2,1,0:T(8,128)}) %all-gather.4.cloned.1.call-update) | async-done | bytes 2097168 | tf_op jit(solution)/shard_map/all_gather | solution.py:22
  71.3 4.6 %while.14 = (s32[]{:T(128)}, f32[4,128,256]{2,1,0:T(8,128)S(1)}, s32[]{:T(128)}, f32[4,256]{1,0:T(4,128)S(1)}, f32[4,4,128,256]{3,2,1,0:T(8,128)}, /*index=5*/s32[]{:T(128)}, s32[]{:T(128)}) while((s32[]{:T(128)}, f32[4,128,256]{2,1,0:T(8,128)S(1)}, s32[]{:T(128)}, f32[4,256]{1,0:T(4,128)S(1)}, f32[4,4,128,256]{3,2,1,0:T(8,128)}, ...), condition=%wide.region_2.3_spmd.clone, body=%wide.region_1.2_spmd.clone.sunk | while | flops 524292 | bytes 1576041 | solution.py:31
  71.3 1.5 %fusion.83 = f32[4,128,256]{2,1,0:T(8,128)S(1)} fusion(f32[4,4,128,256]{3,2,1,0:T(8,128)} %get-tuple-element.203, s32[]{:T(128)} %get-tuple-element.192, f32[4,128,256]{2,1,0:T(8,128)S(1)} %get-tuple-element.193, f32[256]{0:T(256)S(1)} %bitcast.127, pred[]{:T(512)S(6)} %compare.55, pred[]{:T(512)S(6)} %lt.22), kind=kLoop, calls=%fused_computation.1.clone.1 | loop fusion | flops 524288 | bytes 1573894 | tf_op jit(solution)/shard_map/while/body/eval_jaxpr/jit(_where)/select_n | solution.py:29
  72.9 1.5 %fusion.83 = f32[4,128,256]{2,1,0:T(8,128)S(1)} fusion(f32[4,4,128,256]{3,2,1,0:T(8,128)} %get-tuple-element.203, s32[]{:T(128)} %get-tuple-element.192, f32[4,128,256]{2,1,0:T(8,128)S(1)} %get-tuple-element.193, f32[256]{0:T(256)S(1)} %bitcast.127, pred[]{:T(512)S(6)} %compare.55, pred[]{:T(512)S(6)} %lt.22), kind=kLoop, calls=%fused_computation.1.clone.1 | loop fusion | flops 524288 | bytes 1573894 | tf_op jit(solution)/shard_map/while/body/eval_jaxpr/jit(_where)/select_n | solution.py:29
  74.4 1.5 %fusion.83 = f32[4,128,256]{2,1,0:T(8,128)S(1)} fusion(f32[4,4,128,256]{3,2,1,0:T(8,128)} %get-tuple-element.203, s32[]{:T(128)} %get-tuple-element.192, f32[4,128,256]{2,1,0:T(8,128)S(1)} %get-tuple-element.193, f32[256]{0:T(256)S(1)} %bitcast.127, pred[]{:T(512)S(6)} %compare.55, pred[]{:T(512)S(6)} %lt.22), kind=kLoop, calls=%fused_computation.1.clone.1 | loop fusion | flops 524288 | bytes 1573894 | tf_op jit(solution)/shard_map/while/body/eval_jaxpr/jit(_where)/select_n | solution.py:29
  75.9 0.1 fusion.13
  76.1 3.7 %collective-permute-start.2 = (bf16[2,1,128,256]{3,2,1,0:T(8,128)(2,1)S(1)}, bf16[2,1,128,256]{3,2,1,0:T(8,128)(2,1)S(1)}, u32[]{:S(2)}, u32[]{:S(2)}) collective-permute-start(bf16[2,1,128,256]{3,2,1,0:T(8,128)(2,1)S(1)} %get-tuple-element.146), channel_id=1, source_target_pairs={{0,1},{1,2},{2,3},{4,5},{5,6},{6,7},{8,9},{9,10},{10,11},{12,13},{... | collective-permute-start | bytes 393224 | tf_op jit(solution)/shard_map/ppermute | solution.py:12
  79.7 1.9 %collective-permute-start.3 = (bf16[2,1,128,256]{3,2,1,0:T(8,128)(2,1)S(1)}, bf16[2,1,128,256]{3,2,1,0:T(8,128)(2,1)S(1)}, u32[]{:S(2)}, u32[]{:S(2)}) collective-permute-start(bf16[2,1,128,256]{3,2,1,0:T(8,128)(2,1)S(1)} %get-tuple-element.147), channel_id=1, source_target_pairs={{1,0},{2,1},{3,2},{5,4},{6,5},{7,6},{9,8},{10,9},{11,10},{13,12},{... | collective-permute-start | bytes 393224 | tf_op jit(solution)/shard_map/ppermute | solution.py:15
  81.7 4.3 %collective-permute-done.3 = bf16[2,1,128,256]{3,2,1,0:T(8,128)(2,1)S(1)} collective-permute-done((bf16[2,1,128,256]{3,2,1,0:T(8,128)(2,1)S(1)}, bf16[2,1,128,256]{3,2,1,0:T(8,128)(2,1)S(1)}, u32[]{:S(2)}, u32[]{:S(2)}) %collective-permute-start.3) | collective-permute-done | bytes 131104 | tf_op jit(solution)/shard_map/ppermute | solution.py:15
  86.0 0.2 select_maximum_fusion
  86.3 0.0 copy-start.3
  86.3 0.4 fusion.60
  86.7 0.8 copy-done.3
  87.5 0.3 fusion.28
  87.8 0.3 fusion.19
  88.1 0.1 pad_maximum_fusion
  88.2 0.3 convolution_add_fusion.6
  88.5 0.3 convolution_add_fusion.5
  88.8 0.3 convolution_add_fusion.4
  89.1 0.3 convolution_add_fusion.3
  89.4 0.3 convolution_add_fusion.2
  89.7 0.3 convolution_add_fusion.1
  90.0 0.3 fusion.2
  90.3 1.2 %fusion.12 = bf16[2,4,128,256]{3,2,1,0:T(8,128)(2,1)} fusion(f32[2,4,128,256]{3,2,1,0:T(8,128)S(1)} %bitcast.108, bf16[2,4,128,256]{3,2,1,0:T(8,128)(2,1)S(1)} %copy-done), kind=kLoop, calls=%fused_computation.31 | loop fusion | flops 2883584 | bytes 2097152 | tf_op jit(solution)/shard_map/convert_element_type | solution.py:84
  (15 shorter events, 0.1 us)
Async XLA Ops:
  6.5 64.8 %all-gather.4.cloned.1.call-start = ((), (), s32[]{:S(2)}) async-start(), calls=%async_computation | async-start | bytes 2621440 | tf_op jit(solution)/shard_map/all_gather | solution.py:22
  7.5 7.2 %collective-permute-start = (bf16[2,1,128,256]{3,2,1,0:T(8,128)(2,1)S(1)}, bf16[2,1,128,256]{3,2,1,0:T(8,128)(2,1)S(1)}, u32[]{:S(2)}, u32[]{:S(2)}) collective-permute-start(bf16[2,1,128,256]{3,2,1,0:T(8,128)(2,1)S(1)} %get-tuple-element.150), channel_id=1, source_target_pairs={{0,1},{1,2},{2,3},{4,5},{5,6},{6,7},{8,9},{9,10},{10,11},{12,13},{... | collective-permute-start | bytes 393224 | tf_op jit(solution)/shard_map/ppermute | solution.py:12
  12.0 6.3 %collective-permute-start.1 = (bf16[2,1,128,256]{3,2,1,0:T(8,128)(2,1)S(1)}, bf16[2,1,128,256]{3,2,1,0:T(8,128)(2,1)S(1)}, u32[]{:S(2)}, u32[]{:S(2)}) collective-permute-start(bf16[2,1,128,256]{3,2,1,0:T(8,128)(2,1)S(1)} %get-tuple-element.151), channel_id=1, source_target_pairs={{1,0},{2,1},{3,2},{5,4},{6,5},{7,6},{9,8},{10,9},{11,10},{13,12},{... | collective-permute-start | bytes 393224 | tf_op jit(solution)/shard_map/ppermute | solution.py:15
  19.6 1.3 %copy-start.2 = (bf16[3,3,256,256]{3,2,1,0:T(8,128)(2,1)S(1)}, bf16[3,3,256,256]{3,2,1,0:T(8,128)(2,1)}, u32[]{:S(2)}) copy-start(bf16[3,3,256,256]{3,2,1,0:T(8,128)(2,1)} %param.8) | copy-start | bytes 3538948
  21.2 1.0 %copy-start = (bf16[2,4,128,256]{3,2,1,0:T(8,128)(2,1)S(1)}, bf16[2,4,128,256]{3,2,1,0:T(8,128)(2,1)}, u32[]{:S(2)}) copy-start(bf16[2,4,128,256]{3,2,1,0:T(8,128)(2,1)} %param.7) | copy-start | bytes 1572868
  71.3 4.6 %copy-start.1 = (f32[1,4,128,256]{3,2,1,0:T(8,128)S(1)}, f32[1,4,128,256]{3,2,1,0:T(8,128)}, u32[]{:S(2)}) copy-start(f32[1,4,128,256]{3,2,1,0:T(8,128)} %get-tuple-element.128) | copy-start | bytes 1572868
  76.1 5.6 %collective-permute-start.2 = (bf16[2,1,128,256]{3,2,1,0:T(8,128)(2,1)S(1)}, bf16[2,1,128,256]{3,2,1,0:T(8,128)(2,1)S(1)}, u32[]{:S(2)}, u32[]{:S(2)}) collective-permute-start(bf16[2,1,128,256]{3,2,1,0:T(8,128)(2,1)S(1)} %get-tuple-element.146), channel_id=1, source_target_pairs={{0,1},{1,2},{2,3},{4,5},{5,6},{6,7},{8,9},{9,10},{10,11},{12,13},{... | collective-permute-start | bytes 393224 | tf_op jit(solution)/shard_map/ppermute | solution.py:12
  79.7 6.3 %collective-permute-start.3 = (bf16[2,1,128,256]{3,2,1,0:T(8,128)(2,1)S(1)}, bf16[2,1,128,256]{3,2,1,0:T(8,128)(2,1)S(1)}, u32[]{:S(2)}, u32[]{:S(2)}) collective-permute-start(bf16[2,1,128,256]{3,2,1,0:T(8,128)(2,1)S(1)} %get-tuple-element.147), channel_id=1, source_target_pairs={{1,0},{2,1},{3,2},{5,4},{6,5},{7,6},{9,8},{10,9},{11,10},{13,12},{... | collective-permute-start | bytes 393224 | tf_op jit(solution)/shard_map/ppermute | solution.py:15
  86.3 1.3 %copy-start.3 = (bf16[3,3,256,256]{3,2,1,0:T(8,128)(2,1)S(1)}, bf16[3,3,256,256]{3,2,1,0:T(8,128)(2,1)}, u32[]{:S(2)}) copy-start(bf16[3,3,256,256]{3,2,1,0:T(8,128)(2,1)} %param.9) | copy-start | bytes 3538948
Sparse Core Ops, SparseCore 0:
  25.5 45.7 all-gather.3
where the time goes:
time: 98.8 us; the launch traced here: 98.3 us
  waiting for transfers between devices  44.6 us (45%)
  between operations  13.7 us (14%)
  starting transfers between devices  12 us (12%)
  other arithmetic  9.16 us (9%)
  blocking collectives  9.15 us (9%)
  matrix products  5.3 us (5%)
  local copies, waits for them, and re-layouts  4.43 us (4%)
    all_gather x1, waiting for transfers between devices, carried_in(): pieces = jax.tree.map(lambda part: lax.all_gather(part, axis), value)  36.6 us
    all_gather x1, blocking collectives, carried_in(): pieces = jax.tree.map(lambda part: lax.all_gather(part, axis), value)  9.15 us
    ppermute x2, starting transfers between devices, extended(): lax.ppermute(lax.slice_in_dim(block, block.shape[dim] - width, None, axis...  8.17 us
    ppermute x2, waiting for transfers between devices, extended(): lax.ppermute(lax.slice_in_dim(block, 0, width, axis=dim), axis, backward)  7.91 us
    dot_general x18, matrix products, convolve(): jnp.dot(window, weight[tap_row, tap_col], preferred_element_type=jnp.floa...  5.3 us
    select_n x3, other arithmetic, hop(): jnp.where(position < mine, new, old)  4.49 us
    ppermute x2, starting transfers between devices, extended(): lax.ppermute(lax.slice_in_dim(block, 0, width, axis=dim), axis, backward)  3.84 us
    unnamed x9, local copies, waits for them, and re-layouts  2.39 us
  transfers between devices with their start and end apart: 5, of which 3 were waited for; matrix products, arithmetic and copies ran while one was open for 1% of the time, Pallas kernels for 0%

commit v1 on v0

v1 whole, which is shorter than its diff:
```python
import functools

import jax
import jax.numpy as jnp
from jax import lax
from jax.experimental import pallas as pl
from jax.experimental.pallas import tpu as pltpu
from jax.sharding import PartitionSpec as P

VMEM = pl.BlockSpec(memory_space=pltpu.VMEM)
ANY = pl.BlockSpec(memory_space=pl.ANY)
LIMIT = 24 * 1024 * 1024


def matmul(rows, weight):
    lead, depth = rows.shape[:-1], rows.shape[-1]
    flat = jnp.dot(rows.reshape(-1, depth), weight, preferred_element_type=jnp.float32)
    return flat.reshape(*lead, weight.shape[-1])


def join_columns(left, middle, right):
    width = middle.shape[-2]
    axis = middle.ndim - 2
    column = lax.broadcasted_iota(jnp.int32, middle.shape, axis)
    left = jnp.where(column == 0, 0.0, pltpu.roll(left, 1, axis))
    right = jnp.where(column == width - 1, 0.0, pltpu.roll(right, width - 1, axis))
    return left + middle + right


def own_rows(x_ref, w_ref, taps):
    frames, strip = x_ref.shape[:2]
    for q in range(3):
        for f in range(frames):
            taps[q, f] = matmul(x_ref[f], w_ref[1, q])
            taps[q, f, 1:] += matmul(x_ref[f, : strip - 1], w_ref[0, q])
            taps[q, f, : strip - 1] += matmul(x_ref[f, 1:], w_ref[2, q])


def edge_rows(low_ref, high_ref, w_ref, axis):
    mine, count = lax.axis_index(axis), lax.axis_size(axis)
    low, high = low_ref[...], high_ref[...]
    low = jnp.where(mine > 0, low, jnp.zeros_like(low))
    high = jnp.where(mine < count - 1, high, jnp.zeros_like(high))
    first = join_columns(*[matmul(low, w_ref[0, q]) for q in range(3)])
    last = join_columns(*[matmul(high, w_ref[2, q]) for q in range(3)])
    return first, last


def drive_kernel(x_ref, w_ref, decay_ref, inner_ref, outer_ref, sent_ref, taps):
    frames, strip = x_ref.shape[:2]
    own_rows(x_ref, w_ref, taps)
    decay = decay_ref[...].reshape(1, 1, -1)
    state = None
    for f in range(frames):
        driven = join_columns(taps[0, f], taps[1, f], taps[2, f])
        state = driven if state is None else decay * state + driven
        inner_ref[f] = state[1 : strip - 1]
        outer_ref[f, 0] = state[0]
        outer_ref[f, 1] = state[strip - 1]
    sent_ref[...] = state[1 : strip - 1].astype(sent_ref.dtype)


def drive_edge_kernel(low_ref, high_ref, w_ref, decay_ref, outer_ref, result_ref, sent_ref):
    frames = outer_ref.shape[0]
    first, last = edge_rows(low_ref, high_ref, w_ref, "rows")
    decay = decay_ref[...]
    for side, driven in ((0, first), (1, last)):
        more = None
        for f in range(frames):
            now = driven[f, 0]
            more = now if more is None else decay * more + now
            state = outer_ref[f, side] + more
            result_ref[f, side] = state
        sent_ref[side] = state.astype(sent_ref.dtype)


def residual(x, mixed):
    return (x.astype(jnp.float32) + jax.nn.gelu(mixed)).astype(jnp.bfloat16)


def mix_kernel(inner_ref, carried_ref, growth_ref, outer_ref, w_ref, x_ref, out_ref, edge_ref, states, taps, ready, sem):
    frames, strip = states.shape[:2]
    carried = carried_ref[...]
    for f in range(frames):
        growth = growth_ref[f].reshape(1, 1, -1)
        states[f, 1 : strip - 1] = (inner_ref[f] + growth * carried).astype(jnp.bfloat16)
        states[f, 0] = outer_ref[f, 0]
        states[f, strip - 1] = outer_ref[f, 1]
    own_rows(states, w_ref, taps)
    for f in range(frames):
        mixed = join_columns(taps[0, f], taps[1, f], taps[2, f])
        ready[f] = residual(x_ref[f, 1 : strip - 1], mixed[1 : strip - 1])
        edge_ref[f, 0] = mixed[0]
        edge_ref[f, 1] = mixed[strip - 1]
    copy = pltpu.make_async_copy(ready, out_ref.at[:, 1 : strip - 1], sem)
    copy.start()
    copy.wait()


def mix_edge_kernel(low_ref, high_ref, w_ref, edge_ref, x_ref, before_ref, out_ref, ready, sems):
    frames, strip = x_ref.shape[:2]
    first, last = edge_rows(low_ref, high_ref, w_ref, "rows")
    copies = []
    for side, row, more in ((0, 0, first), (1, strip - 1, last)):
        ready[side] = residual(x_ref[:, row], edge_ref[:, side] + more[:, 0])
        copy = pltpu.make_async_copy(ready.at[side], out_ref.at[:, row], sems.at[side])
        copy.start()
        copies.append(copy)
    for copy in copies:
        copy.wait()


def kernel_call(kernel, out_shape, in_specs, out_specs, scratch, flops, aliases=None):
    return pl.pallas_call(
        kernel,
        out_shape=out_shape,
        in_specs=in_specs,
        out_specs=out_specs,
        scratch_shapes=scratch,
        input_output_aliases=aliases or {},
        compiler_params=pltpu.CompilerParams(vmem_limit_bytes=LIMIT),
        cost_estimate=pl.CostEstimate(flops=flops, bytes_accessed=1 << 20, transcendentals=0),
    )


def ring_halo(first, last, axis):
    count = lax.axis_size(axis)
    up = [(i, (i + 1) % count) for i in range(count)]
    down = [(target, source) for source, target in up]
    return lax.ppermute(last, axis, up), lax.ppermute(first, axis, down)


def swapped(value, axis, distance):
    return lax.ppermute(value, axis, [(i, i ^ distance) for i in range(lax.axis_size(axis))])


def butterfly(value, decay, axis):
    count, mine = lax.axis_size(axis), lax.axis_index(axis)
    total, carried, distance = value, None, 1
    before = jnp.ones_like(decay)
    while distance < count:
        other = swapped(total, axis, distance).astype(jnp.float32)
        after = (mine & distance) != 0
        own = total.astype(jnp.float32)
        here = jnp.where(after, before * other, 0.0)
        carried = here if carried is None else carried + here
        if 2 * distance < count:
            earlier, later = jnp.where(after, other, own), jnp.where(after, own, other)
            total = (decay * earlier + later).astype(value.dtype)
            before = jnp.where(after, decay * before, before)
            decay = decay * decay
        distance *= 2
    return carried


def far_first(value, decay, axis):
    mine = lax.axis_index(axis)
    far = swapped(value, axis, 2).astype(jnp.float32)
    far = jnp.where(mine >= 2, far, 0.0)
    message = jnp.where((mine & 1) != 0, far, decay * decay * far + value.astype(jnp.float32))
    near = swapped(message.astype(value.dtype), axis, 1).astype(jnp.float32)
    return jnp.where(mine >= 1, near, 0.0) + decay * far


def local(latents, weight_in, weight_out, decay_table, decay_index):
    frames, strip, width, channels = latents.shape
    levels = decay_table.shape[0]
    f32, bf16 = jnp.float32, jnp.bfloat16
    shaped = jax.ShapeDtypeStruct
    area = width * channels
    conv_flops = 2 * 9 * frames * strip * area * channels

    low, high = ring_halo(latents[:, :1], latents[:, strip - 1 :], "rows")
    onehot = decay_index[:, None] == jnp.arange(levels, dtype=jnp.int32)[None, :]
    decays = jnp.sum(jnp.where(onehot, decay_table[None, :], 0.0), axis=1)[None, :]
    growth = [decays]
    for _ in range(frames - 1):
        growth.append(growth[-1] * decays)
    over = growth[-1]
    growth = jnp.stack(growth)

    inner, outer, sent = kernel_call(
        drive_kernel,
        (shaped((frames, strip - 2, width, channels), f32), shaped((frames, 2, width, channels), f32), shaped((strip - 2, width, channels), bf16)),
        [VMEM] * 3,
        (VMEM,) * 3,
        [pltpu.VMEM((3, frames, strip, width, channels), f32)],
        conv_flops,
    )(latents, weight_in, decays)
    outer, edge_sent = kernel_call(
        drive_edge_kernel,
        (shaped((frames, 2, width, channels), f32), shaped((2, width, channels), bf16)),
        [VMEM] * 5,
        (VMEM,) * 2,
        [],
        conv_flops // 6,
        aliases={4: 0},
    )(low, high, weight_in, decays, outer)

    count = lax.axis_size("tm")
    scan = far_first if count == 4 else butterfly
    carried = scan(sent, over, "tm")
    edge_carried = butterfly(edge_sent, over, "tm")

    edge_states = (outer + growth[:, None] * edge_carried[None]).astype(bf16)
    low, high = ring_halo(edge_states[:, :1], edge_states[:, 1:], "rows")
    out, edge = kernel_call(
        mix_kernel,
        (shaped(latents.shape, bf16), shaped((frames, 2, width, channels), f32)),
        [VMEM] * 6,
        (ANY, VMEM),
        [
            pltpu.VMEM(latents.shape, bf16),
            pltpu.VMEM((3, frames, strip, width, channels), f32),
            pltpu.VMEM((frames, strip - 2, width, channels), bf16),
            pltpu.SemaphoreType.DMA,
        ],
        conv_flops,
    )(inner, carried, growth, edge_states, weight_out, latents)
    return kernel_call(
        mix_edge_kernel,
        shaped(latents.shape, bf16),
        [VMEM] * 5 + [ANY],
        ANY,
        [pltpu.VMEM((2, frames, width, channels), bf16), pltpu.SemaphoreType.DMA((2,))],
        conv_flops // 6,
        aliases={5: 0},
    )(low, high, weight_out, edge, latents, out)


def solution(mesh):
    in_specs = (P(("groups", "tm"), "rows", None, None), P(), P(), P(), P())
    out_specs = P(("groups", "tm"), "rows", None, None)
    return jax.shard_map(local, mesh=mesh, in_specs=in_specs, out_specs=out_specs, check_vma=False)
```

time: 98.8 us -> 39.2 us (0.40)
  the two profiles are of different devices: /device:TPU:1 before, /device:TPU:0 now
where the time goes in v1:
time: 39.2 us; the launch traced here: 39 us
  waiting for transfers between devices  19 us (48%)
  starting transfers between devices  10.5 us (27%)
  Pallas kernels  4.97 us (13%)
  local copies, waits for them, and re-layouts  3.34 us (9%)
  other arithmetic  1.09 us (3%)
    ppermute x4, waiting for transfers between devices, swapped(): lax.ppermute(value, axis, [(i, i ^ distance) for i in range(lax.axis_size...  15.9 us
    ppermute x4, starting transfers between devices, swapped(): lax.ppermute(value, axis, [(i, i ^ distance) for i in range(lax.axis_size...  7.5 us
    ppermute x4, waiting for transfers between devices, ring_halo(): return (lax.ppermute(last, axis, up), lax.ppermute(first, axis, down))  3.07 us
    ppermute x4, starting transfers between devices, ring_halo(): return (lax.ppermute(last, axis, up), lax.ppermute(first, axis, down))  2.99 us
    unnamed x11, local copies, waits for them, and re-layouts  2.33 us
    pallas_call x1, Pallas kernels, local(): kernel_call(mix_kernel, (shaped(latents.shape, bf16), shaped((frames, 2,...  2.1 us
    pallas_call x1, Pallas kernels, local(): kernel_call(mix_edge_kernel, shaped(latents.shape, bf16), [VMEM] * 5 + [A...  1.24 us
    pallas_call x1, Pallas kernels, local(): kernel_call(drive_kernel, (shaped((frames, strip - 2, width, channels), f...  1.2 us
  transfers between devices with their start and end apart: 8, of which 5 were waited for; matrix products, arithmetic and copies ran while one was open for 2% of the time, Pallas kernels for 10%

profile of v1, /device:TPU:0, one launch (start us, length us, event | category | flops | bytes accessed | tf_op | source)
XLA Modules:
  0.0 39.0 jit_solution(8852384729456984756)
XLA Ops:
  0.0 1.0 %fusion.4 = (bf16[2,1,128,256]{3,2,1,0:T(8,128)(2,1)S(1)}, bf16[2,1,128,256]{3,2,1,0:T(8,128)(2,1)S(1)}) fusion(bf16[2,4,128,256]{3,2,1,0:T(8,128)(2,1)} %x_ref.5), kind=kLoop, calls=%fused_computation.17 | loop fusion | bytes 524288 | tf_op jit(solution)/shard_map/slice | solution.py:173
  1.0 2.4 %collective-permute-start.1 = (bf16[2,1,128,256]{3,2,1,0:T(8,128)(2,1)S(1)}, bf16[2,1,128,256]{3,2,1,0:T(8,128)(2,1)S(1)}, u32[]{:S(2)}, u32[]{:S(2)}) collective-permute-start(bf16[2,1,128,256]{3,2,1,0:T(8,128)(2,1)S(1)} %get-tuple-element.19), channel_id=1, source_target_pairs={{1,0},{2,1},{3,2},{0,3},{5,4},{6,5},{7,6},{4,7},{9,8},{10,9},{11,1... | collective-permute-start | bytes 393224 | tf_op jit(solution)/shard_map/ppermute | solution.py:130
  3.4 0.0 collective-permute-start
  3.4 0.8 %select_reduce_fusion = f32[256]{0:T(256)S(1)} fusion(f32[16]{0:T(128)} %param.8, s32[256]{0:T(256)} %param.9), kind=kLoop, calls=%fused_computation.11 | loop fusion | flops 12032 | bytes 2112 | tf_op jit(solution)/shard_map/reduce_sum | solution.py:175
  4.2 0.0 copy-start.1
  4.2 1.0 %copy-done.1 = bf16[2,4,128,256]{3,2,1,0:T(8,128)(2,1)S(1)} copy-done((bf16[2,4,128,256]{3,2,1,0:T(8,128)(2,1)S(1)}, bf16[2,4,128,256]{3,2,1,0:T(8,128)(2,1)}, u32[]{:S(2)}) %copy-start.1) | copy-done | bytes 524312
  5.2 0.0 copy-start.3
  5.2 1.3 %copy-done.3 = bf16[3,3,256,256]{3,2,1,0:T(8,128)(2,1)S(1)} copy-done((bf16[3,3,256,256]{3,2,1,0:T(8,128)(2,1)S(1)}, bf16[3,3,256,256]{3,2,1,0:T(8,128)(2,1)}, u32[]{:S(2)}) %copy-start.3) | copy-done | bytes 1179672
  6.5 0.0 copy-start.4
  6.5 1.2 %shard_map.55 = (f32[2,2,128,256]{3,2,1,0:T(8,128)S(1)}, f32[2,2,128,256]{3,2,1,0:T(8,128)S(1)}, bf16[2,128,256]{2,1,0:T(8,128)(2,1)S(1)}) custom-call(bf16[2,4,128,256]{3,2,1,0:T(8,128)(2,1)S(1)} %copy-done.1, bf16[3,3,256,256]{3,2,1,0:T(8,128)(2,1)S(1)} %copy-done.3, f32[1,256]{1,0:T(1,128)S(1)} %bitcast.5), custom_call_target="tpu_custom_call" | custom-call | flops 1207959552 | bytes 1048576 | tf_op jit(solution)/shard_map/pallas_call | solution.py:182
  7.7 2.7 %collective-permute-start.6 = (bf16[2,128,256]{2,1,0:T(8,128)(2,1)S(1)}, bf16[2,128,256]{2,1,0:T(8,128)(2,1)S(1)}, u32[]{:S(2)}, u32[]{:S(2)}) collective-permute-start(bf16[2,128,256]{2,1,0:T(8,128)(2,1)S(1)} %get-tuple-element.16), channel_id=1, source_target_pairs={{0,8},{4,12},{8,0},{12,4},{1,9},{5,13},{9,1},{13,5},{2,10},{6,14},... | collective-permute-start | bytes 393224 | tf_op jit(solution)/shard_map/ppermute | solution.py:134
  10.4 0.0 collective-permute-done.1.high_ref
  10.4 0.0 collective-permute-done.low_ref
  10.4 0.0 copy-done.4
  10.4 0.4 %shard_map.56 = (f32[2,2,128,256]{3,2,1,0:T(8,128)S(1)}, bf16[2,128,256]{2,1,0:T(8,128)(2,1)S(1)}) custom-call(bf16[2,1,128,256]{3,2,1,0:T(8,128)(2,1)S(1)} %collective-permute-done.low_ref, bf16[2,1,128,256]{3,2,1,0:T(8,128)(2,1)S(1)} %collective-permute-done.1.high_ref, bf16[3,3,256,256]{3,2,1,0:T(8,128)(2,1)S(1)} %copy-done.4, ...), custom_call_target="tpu_custom_call", output_to_operand_aliasing={{0}: (4, {})} | custom-call | flops 201326592 | bytes 1048576 | tf_op jit(solution)/shard_map/pallas_call | solution.py:190
  10.8 1.6 %collective-permute-start.2 = (bf16[2,128,256]{2,1,0:T(8,128)(2,1)S(1)}, bf16[2,128,256]{2,1,0:T(8,128)(2,1)S(1)}, u32[]{:S(2)}, u32[]{:S(2)}) collective-permute-start(bf16[2,128,256]{2,1,0:T(8,128)(2,1)S(1)} %get-tuple-element.14), channel_id=1, source_target_pairs={{0,4},{4,0},{8,12},{12,8},{1,5},{5,1},{9,13},{13,9},{2,6},{6,2},{1... | collective-permute-start | bytes 393224 | tf_op jit(solution)/shard_map/ppermute | solution.py:134
  12.5 5.3 %collective-permute-done.6 = bf16[2,128,256]{2,1,0:T(8,128)(2,1)S(1)} collective-permute-done((bf16[2,128,256]{2,1,0:T(8,128)(2,1)S(1)}, bf16[2,128,256]{2,1,0:T(8,128)(2,1)S(1)}, u32[]{:S(2)}, u32[]{:S(2)}) %collective-permute-start.6) | collective-permute-done | bytes 131104 | tf_op jit(solution)/shard_map/ppermute | solution.py:134
  17.7 0.1 select_convert_fusion
  17.8 0.7 %collective-permute-start.7 = (bf16[2,128,256]{2,1,0:T(8,128)(2,1)S(1)}, bf16[2,128,256]{2,1,0:T(8,128)(2,1)S(1)}, u32[]{:S(2)}, u32[]{:S(2)}) collective-permute-start(bf16[2,128,256]{2,1,0:T(8,128)(2,1)S(1)} %select_convert_fusion), channel_id=1, source_target_pairs={{0,4},{4,0},{8,12},{12,8},{1,5},{5,1},{9,13},{13,9},{2,6},{6,2},{1... | collective-permute-start | bytes 393224 | tf_op jit(solution)/shard_map/ppermute | solution.py:134
  18.5 0.0 collective-permute-done.2
  18.5 4.6 %collective-permute-done.7 = bf16[2,128,256]{2,1,0:T(8,128)(2,1)S(1)} collective-permute-done((bf16[2,128,256]{2,1,0:T(8,128)(2,1)S(1)}, bf16[2,128,256]{2,1,0:T(8,128)(2,1)S(1)}, u32[]{:S(2)}, u32[]{:S(2)}) %collective-permute-start.7) | collective-permute-done | bytes 131104 | tf_op jit(solution)/shard_map/ppermute | solution.py:134
  23.1 0.1 multiply_add_fusion
  23.2 0.0 copy-start
  23.2 0.0 copy-start.2
  23.2 2.5 %collective-permute-start.3 = (bf16[2,128,256]{2,1,0:T(8,128)(2,1)S(1)}, bf16[2,128,256]{2,1,0:T(8,128)(2,1)S(1)}, u32[]{:S(2)}, u32[]{:S(2)}) collective-permute-start(bf16[2,128,256]{2,1,0:T(8,128)(2,1)S(1)} %get-tuple-element.26), channel_id=1, source_target_pairs={{0,8},{4,12},{8,0},{12,4},{1,9},{5,13},{9,1},{13,5},{2,10},{6,14},... | collective-permute-start | bytes 393224 | tf_op jit(solution)/shard_map/ppermute | solution.py:134
  25.8 6.0 %collective-permute-done.3 = bf16[2,128,256]{2,1,0:T(8,128)(2,1)S(1)} collective-permute-done((bf16[2,128,256]{2,1,0:T(8,128)(2,1)S(1)}, bf16[2,128,256]{2,1,0:T(8,128)(2,1)S(1)}, u32[]{:S(2)}, u32[]{:S(2)}) %collective-permute-start.3) | collective-permute-done | bytes 131104 | tf_op jit(solution)/shard_map/ppermute | solution.py:134
  31.8 0.1 fusion
  31.9 0.1 add_convert_fusion.outer_ref
  32.0 0.1 collective-permute-start.5
  32.1 0.5 %collective-permute-start.4 = (bf16[2,1,128,256]{3,2,1,0:T(8,128)(2,1)S(1)}, bf16[2,1,128,256]{3,2,1,0:T(8,128)(2,1)S(1)}, u32[]{:S(2)}, u32[]{:S(2)}) collective-permute-start(bf16[2,1,128,256]{3,2,1,0:T(8,128)(2,1)S(1)} %get-tuple-element.22), channel_id=1, source_target_pairs={{0,1},{1,2},{2,3},{3,0},{4,5},{5,6},{6,7},{7,4},{8,9},{9,10},{10,1... | collective-permute-start | bytes 393224 | tf_op jit(solution)/shard_map/ppermute | solution.py:130
  32.6 0.0 copy-done
  32.6 0.0 copy-done.2
  32.6 2.1 %shard_map.57 = (bf16[2,4,128,256]{3,2,1,0:T(8,128)(2,1)}, f32[2,2,128,256]{3,2,1,0:T(8,128)S(1)}) custom-call(f32[2,2,128,256]{3,2,1,0:T(8,128)S(1)} %get-tuple-element.15.inner_ref, f32[2,128,256]{2,1,0:T(8,128)S(1)} %get-tuple-element.25.carried_ref, f32[2,1,256]{2,1,0:T(1,128)S(1)} %pad_maximum_fusion.growth_ref, ...), custom_call_target="tpu_custom_call" | custom-call | flops 1207959552 | bytes 1048576 | tf_op jit(solution)/shard_map/pallas_call | solution.py:207
  34.7 0.5 %collective-permute-done.5.high_ref = bf16[2,1,128,256]{3,2,1,0:T(8,128)(2,1)S(1)} collective-permute-done((bf16[2,1,128,256]{3,2,1,0:T(8,128)(2,1)S(1)}, bf16[2,1,128,256]{3,2,1,0:T(8,128)(2,1)S(1)}, u32[]{:S(2)}, u32[]{:S(2)}) %collective-permute-start.5) | collective-permute-done | bytes 131104 | tf_op jit(solution)/shard_map/ppermute | solution.py:130
  35.2 2.5 %collective-permute-done.4.low_ref = bf16[2,1,128,256]{3,2,1,0:T(8,128)(2,1)S(1)} collective-permute-done((bf16[2,1,128,256]{3,2,1,0:T(8,128)(2,1)S(1)}, bf16[2,1,128,256]{3,2,1,0:T(8,128)(2,1)S(1)}, u32[]{:S(2)}, u32[]{:S(2)}) %collective-permute-start.4) | collective-permute-done | bytes 131104 | tf_op jit(solution)/shard_map/ppermute | solution.py:130
  37.7 1.2 %shard_map.58 = bf16[2,4,128,256]{3,2,1,0:T(8,128)(2,1)} custom-call(bf16[2,1,128,256]{3,2,1,0:T(8,128)(2,1)S(1)} %collective-permute-done.4.low_ref, bf16[2,1,128,256]{3,2,1,0:T(8,128)(2,1)S(1)} %collective-permute-done.5.high_ref, bf16[3,3,256,256]{3,2,1,0:T(8,128)(2,1)S(1)} %copy-done, ...), custom_call_target="tpu_custom_call", output_to_operand_aliasing={{}: (5, {})} | custom-call | flops 201326592 | bytes 1048576 | tf_op jit(solution)/shard_map/pallas_call | solution.py:220
  (5 shorter events, 0.0 us)
Async XLA Ops:
  1.0 9.4 %collective-permute-start.1 = (bf16[2,1,128,256]{3,2,1,0:T(8,128)(2,1)S(1)}, bf16[2,1,128,256]{3,2,1,0:T(8,128)(2,1)S(1)}, u32[]{:S(2)}, u32[]{:S(2)}) collective-permute-start(bf16[2,1,128,256]{3,2,1,0:T(8,128)(2,1)S(1)} %get-tuple-element.19), channel_id=1, source_target_pairs={{1,0},{2,1},{3,2},{0,3},{5,4},{6,5},{7,6},{4,7},{9,8},{10,9},{11,1... | collective-permute-start | bytes 393224 | tf_op jit(solution)/shard_map/ppermute | solution.py:130
  3.4 7.0 %collective-permute-start = (bf16[2,1,128,256]{3,2,1,0:T(8,128)(2,1)S(1)}, bf16[2,1,128,256]{3,2,1,0:T(8,128)(2,1)S(1)}, u32[]{:S(2)}, u32[]{:S(2)}) collective-permute-start(bf16[2,1,128,256]{3,2,1,0:T(8,128)(2,1)S(1)} %get-tuple-element.20), channel_id=1, source_target_pairs={{0,1},{1,2},{2,3},{3,0},{4,5},{5,6},{6,7},{7,4},{8,9},{9,10},{10,1... | collective-permute-start | bytes 393224 | tf_op jit(solution)/shard_map/ppermute | solution.py:130
  4.2 1.0 %copy-start.1 = (bf16[2,4,128,256]{3,2,1,0:T(8,128)(2,1)S(1)}, bf16[2,4,128,256]{3,2,1,0:T(8,128)(2,1)}, u32[]{:S(2)}) copy-start(bf16[2,4,128,256]{3,2,1,0:T(8,128)(2,1)} %x_ref.5) | copy-start | bytes 1572868
  5.2 1.3 %copy-start.3 = (bf16[3,3,256,256]{3,2,1,0:T(8,128)(2,1)S(1)}, bf16[3,3,256,256]{3,2,1,0:T(8,128)(2,1)}, u32[]{:S(2)}) copy-start(bf16[3,3,256,256]{3,2,1,0:T(8,128)(2,1)} %w_ref.5) | copy-start | bytes 3538948
  6.5 3.9 %copy-start.4 = (bf16[3,3,256,256]{3,2,1,0:T(8,128)(2,1)S(1)}, bf16[3,3,256,256]{3,2,1,0:T(8,128)(2,1)}, u32[]{:S(2)}) copy-start(bf16[3,3,256,256]{3,2,1,0:T(8,128)(2,1)} %w_ref.5) | copy-start | bytes 3538948
  7.7 10.0 %collective-permute-start.6 = (bf16[2,128,256]{2,1,0:T(8,128)(2,1)S(1)}, bf16[2,128,256]{2,1,0:T(8,128)(2,1)S(1)}, u32[]{:S(2)}, u32[]{:S(2)}) collective-permute-start(bf16[2,128,256]{2,1,0:T(8,128)(2,1)S(1)} %get-tuple-element.16), channel_id=1, source_target_pairs={{0,8},{4,12},{8,0},{12,4},{1,9},{5,13},{9,1},{13,5},{2,10},{6,14},... | collective-permute-start | bytes 393224 | tf_op jit(solution)/shard_map/ppermute | solution.py:134
  10.8 7.6 %collective-permute-start.2 = (bf16[2,128,256]{2,1,0:T(8,128)(2,1)S(1)}, bf16[2,128,256]{2,1,0:T(8,128)(2,1)S(1)}, u32[]{:S(2)}, u32[]{:S(2)}) collective-permute-start(bf16[2,128,256]{2,1,0:T(8,128)(2,1)S(1)} %get-tuple-element.14), channel_id=1, source_target_pairs={{0,4},{4,0},{8,12},{12,8},{1,5},{5,1},{9,13},{13,9},{2,6},{6,2},{1... | collective-permute-start | bytes 393224 | tf_op jit(solution)/shard_map/ppermute | solution.py:134
  17.8 5.3 %collective-permute-start.7 = (bf16[2,128,256]{2,1,0:T(8,128)(2,1)S(1)}, bf16[2,128,256]{2,1,0:T(8,128)(2,1)S(1)}, u32[]{:S(2)}, u32[]{:S(2)}) collective-permute-start(bf16[2,128,256]{2,1,0:T(8,128)(2,1)S(1)} %select_convert_fusion), channel_id=1, source_target_pairs={{0,4},{4,0},{8,12},{12,8},{1,5},{5,1},{9,13},{13,9},{2,6},{6,2},{1... | collective-permute-start | bytes 393224 | tf_op jit(solution)/shard_map/ppermute | solution.py:134
  23.2 9.3 %copy-start = (bf16[3,3,256,256]{3,2,1,0:T(8,128)(2,1)S(1)}, bf16[3,3,256,256]{3,2,1,0:T(8,128)(2,1)}, u32[]{:S(2)}) copy-start(bf16[3,3,256,256]{3,2,1,0:T(8,128)(2,1)} %w_ref.7) | copy-start | bytes 3538948
  23.2 9.3 %copy-start.2 = (bf16[2,4,128,256]{3,2,1,0:T(8,128)(2,1)S(1)}, bf16[2,4,128,256]{3,2,1,0:T(8,128)(2,1)}, u32[]{:S(2)}) copy-start(bf16[2,4,128,256]{3,2,1,0:T(8,128)(2,1)} %x_ref.5) | copy-start | bytes 1572868
  23.2 8.6 %collective-permute-start.3 = (bf16[2,128,256]{2,1,0:T(8,128)(2,1)S(1)}, bf16[2,128,256]{2,1,0:T(8,128)(2,1)S(1)}, u32[]{:S(2)}, u32[]{:S(2)}) collective-permute-start(bf16[2,128,256]{2,1,0:T(8,128)(2,1)S(1)} %get-tuple-element.26), channel_id=1, source_target_pairs={{0,8},{4,12},{8,0},{12,4},{1,9},{5,13},{9,1},{13,5},{2,10},{6,14},... | collective-permute-start | bytes 393224 | tf_op jit(solution)/shard_map/ppermute | solution.py:134
  32.0 3.2 %collective-permute-start.5 = (bf16[2,1,128,256]{3,2,1,0:T(8,128)(2,1)S(1)}, bf16[2,1,128,256]{3,2,1,0:T(8,128)(2,1)S(1)}, u32[]{:S(2)}, u32[]{:S(2)}) collective-permute-start(bf16[2,1,128,256]{3,2,1,0:T(8,128)(2,1)S(1)} %get-tuple-element.21), channel_id=1, source_target_pairs={{1,0},{2,1},{3,2},{0,3},{5,4},{6,5},{7,6},{4,7},{9,8},{10,9},{11,1... | collective-permute-start | bytes 393224 | tf_op jit(solution)/shard_map/ppermute | solution.py:130
  32.1 5.7 %collective-permute-start.4 = (bf16[2,1,128,256]{3,2,1,0:T(8,128)(2,1)S(1)}, bf16[2,1,128,256]{3,2,1,0:T(8,128)(2,1)S(1)}, u32[]{:S(2)}, u32[]{:S(2)}) collective-permute-start(bf16[2,1,128,256]{3,2,1,0:T(8,128)(2,1)S(1)} %get-tuple-element.22), channel_id=1, source_target_pairs={{0,1},{1,2},{2,3},{3,0},{4,5},{5,6},{6,7},{7,4},{8,9},{9,10},{10,1... | collective-permute-start | bytes 393224 | tf_op jit(solution)/shard_map/ppermute | solution.py:130

commit v2 on v1

v2 whole, which is shorter than its diff:
```python
import functools

import jax
import jax.numpy as jnp
from jax import lax
from jax.experimental import pallas as pl
from jax.experimental.pallas import tpu as pltpu
from jax.sharding import PartitionSpec as P

VMEM = pl.BlockSpec(memory_space=pltpu.VMEM)
ANY = pl.BlockSpec(memory_space=pl.ANY)
SMALL = 1000
LONG = 3000000000
LIMIT = 24 * 1024 * 1024
F32, BF16 = jnp.float32, jnp.bfloat16


def turned():
    return lax.axis_index("rows") % 2


def place(row, count):
    return jnp.where(turned() == 1, count - 1 - row, row)


def matmul(rows, weight):
    lead, depth = rows.shape[:-1], rows.shape[-1]
    flat = jnp.dot(rows.reshape(-1, depth), weight, preferred_element_type=F32)
    return flat.reshape(*lead, weight.shape[-1])


def join_columns(left, middle, right):
    width = middle.shape[-2]
    axis = middle.ndim - 2
    column = lax.broadcasted_iota(jnp.int32, middle.shape, axis)
    left = jnp.where(column == 0, 0.0, pltpu.roll(left, 1, axis))
    right = jnp.where(column == width - 1, 0.0, pltpu.roll(right, width - 1, axis))
    return left + middle + right


def own_rows(x_ref, w_ref, taps):
    frames, strip = x_ref.shape[:2]
    for q in range(3):
        for f in range(frames):
            taps[q, f] = matmul(x_ref[f], w_ref[1, q])
            taps[q, f, 1:] += matmul(x_ref[f, : strip - 1], w_ref[0, q])
            taps[q, f, : strip - 1] += matmul(x_ref[f, 1:], w_ref[2, q])


def from_outside(halo_ref, w_ref):
    mine, count = lax.axis_index("rows"), lax.axis_size("rows")
    halo = halo_ref[...]
    inside = jnp.logical_and(mine > 0, mine < count - 1)
    halo = jnp.where(inside, halo, jnp.zeros_like(halo))
    return join_columns(*[matmul(halo, w_ref[place(0, 3), q]) for q in range(3)])


def from_inside(halo_ref, w_ref):
    return join_columns(*[matmul(halo_ref[...], w_ref[place(2, 3), q]) for q in range(3)])


def rows_kernel(x_ref, outer_ref, inner_ref):
    frames, strip = x_ref.shape[:2]
    for f in range(frames):
        outer_ref[f] = x_ref[f, place(0, strip)]
        inner_ref[f] = x_ref[f, place(strip - 1, strip)]


def drive_kernel(x_ref, w_ref, table_ref, index_ref, outer_ref, middle_ref, inner_ref, sent_ref, growth_ref, taps, states):
    frames, strip = x_ref.shape[:2]
    own_rows(x_ref, w_ref, taps)
    index = index_ref[...]
    decay = jnp.zeros(index.shape, F32)
    for level in range(table_ref.shape[1]):
        decay = jnp.where(index == level, table_ref[:, level : level + 1], decay)
    growth = decay
    state = None
    for f in range(frames):
        growth_ref[f] = growth
        growth = growth * decay
        driven = join_columns(taps[0, f], taps[1, f], taps[2, f])
        state = driven if state is None else decay.reshape(1, 1, -1) * state + driven
        states[...] = state
        outer_ref[f] = states[place(0, strip)]
        middle_ref[f] = state[1 : strip - 1]
        inner_ref[f] = states[place(strip - 1, strip)]
    sent_ref[...] = state[1 : strip - 1].astype(BF16)


def drive_edge_kernel(beyond, halo_ref, w_ref, growth_ref, row_ref, result_ref, sent_ref, order_ref):
    frames = row_ref.shape[0]
    driven = beyond(halo_ref, w_ref)
    decay = growth_ref[0]
    more = None
    for f in range(frames):
        more = driven[f] if more is None else decay * more + driven[f]
        state = row_ref[f] + more
        result_ref[f] = state
    sent_ref[...] = state.astype(BF16)
    order_ref[...] = growth_ref[...]


def pair_kernel(own_ref, other_ref, growth_ref, total_ref, order_ref):
    over = growth_ref[growth_ref.shape[0] - 1]
    own, other = own_ref[...].astype(F32), other_ref[...].astype(F32)
    after = lax.axis_index("tm") % 2 == 1
    earlier, later = jnp.where(after, other, own), jnp.where(after, own, other)
    total_ref[...] = (over * earlier + later).astype(BF16)
    order_ref[...] = growth_ref[...]


def edge_states_kernel(row_ref, near_ref, far_ref, growth_ref, states_ref, order_ref):
    frames = row_ref.shape[0]
    over = growth_ref[frames - 1]
    mine = lax.axis_index("tm")
    near, far = near_ref[...].astype(F32), far_ref[...].astype(F32)
    far = jnp.where(mine >= 2, far, 0.0)
    carried = jnp.where(mine % 2 == 1, over * far + near, far)
    for f in range(frames):
        states_ref[f] = (row_ref[f] + growth_ref[f] * carried).astype(BF16)
    order_ref[...] = growth_ref[...]


def relay_kernel(own_ref, before_ref, growth_ref, message_ref, order_ref):
    over = growth_ref[growth_ref.shape[0] - 1]
    message_ref[...] = (over * before_ref[...].astype(F32) + own_ref[...].astype(F32)).astype(BF16)
    order_ref[...] = growth_ref[...]


def middle_states_kernel(middle_ref, first_ref, second_ref, third_ref, growth_ref, states_ref):
    frames = middle_ref.shape[0]
    mine = lax.axis_index("tm")
    carried = jnp.zeros(first_ref.shape, F32)
    for hop, ref in enumerate((first_ref, second_ref, third_ref)):
        carried = jnp.where(mine == hop + 1, ref[...].astype(F32), carried)
    for f in range(frames):
        states_ref[f] = (middle_ref[f] + growth_ref[f] * carried).astype(BF16)


def residual(x, mixed):
    return (x.astype(F32) + jax.nn.gelu(mixed)).astype(BF16)


def mix_kernel(outer_in, middle_in, inner_in, w_ref, x_ref, outer_ref, middle_ref, inner_ref, states, taps):
    frames, strip = x_ref.shape[:2]
    for f in range(frames):
        states[f, place(0, strip)] = outer_in[f]
        states[f, 1 : strip - 1] = middle_in[f]
        states[f, place(strip - 1, strip)] = inner_in[f]
    own_rows(states, w_ref, taps)
    for f in range(frames):
        mixed = join_columns(taps[0, f], taps[1, f], taps[2, f])
        middle_ref[f] = residual(x_ref[f, 1 : strip - 1], mixed[1 : strip - 1])
        first, last = mixed[0], mixed[strip - 1]
        outer_ref[f] = jnp.where(turned() == 1, last, first)
        inner_ref[f] = jnp.where(turned() == 1, first, last)


def finish_kernel(outer_halo, inner_halo, w_ref, outer_ref, inner_ref, middle_ref, x_ref, out_ref, ready, sems):
    frames, strip = x_ref.shape[:2]
    copies = []

    def send(source, target):
        copies.append(pltpu.make_async_copy(source, target, sems.at[len(copies)]))
        copies[-1].start()

    for f in range(frames):
        send(middle_ref.at[f], out_ref.at[f, 1 : strip - 1])
    edges = ((inner_ref, inner_halo, from_inside, strip - 1), (outer_ref, outer_halo, from_outside, 0))
    for side, (mixed_ref, halo_ref, beyond, row) in enumerate(edges):
        mixed = mixed_ref[...] + beyond(halo_ref, w_ref)
        for f in range(frames):
            ready[side, f] = residual(x_ref[f, place(row, strip)], mixed[f])
            send(ready.at[side, f], out_ref.at[f, place(row, strip)])
    for copy in copies:
        copy.wait()


def call(kernel, out_shape, in_specs, out_specs, scratch, flops, aliases=None):
    return pl.pallas_call(
        kernel,
        out_shape=out_shape,
        in_specs=in_specs,
        out_specs=out_specs,
        scratch_shapes=scratch,
        input_output_aliases=aliases or {},
        compiler_params=pltpu.CompilerParams(vmem_limit_bytes=LIMIT),
        cost_estimate=pl.CostEstimate(flops=flops, bytes_accessed=1 << 20, transcendentals=0),
    )


def swapped(value, axis, distance):
    return lax.ppermute(value, axis, [(i, i ^ distance) for i in range(lax.axis_size(axis))])


def swapped_between(value, lower):
    places, count = lax.axis_size("tm"), lax.axis_size("rows")
    pairs = []
    for place_in in range(places):
        for i in range(count):
            if place_in in (lower, lower + 1):
                pairs.append((place_in * count + i, (2 * lower + 1 - place_in) * count + i))
            else:
                pairs.append((place_in * count + i, place_in * count + (i ^ 1)))
    return lax.ppermute(value, ("tm", "rows"), pairs)


def across_chips(value):
    groups, count = lax.axis_size("groups"), lax.axis_size("rows")
    pairs = []
    for group in range(groups):
        for i in range(count):
            other = (i + 1 if i % 2 else i - 1) % count
            side = group
            if groups % 2 == 0 and i in (0, count - 1):
                other, side = i, group ^ 1
            pairs.append((group * count + i, side * count + other))
    return lax.ppermute(value, ("groups", "rows"), pairs)


def butterfly(value, decay, axis):
    count, mine = lax.axis_size(axis), lax.axis_index(axis)
    total, carried, distance = value, None, 1
    before = jnp.ones_like(decay)
    while distance < count:
        other = swapped(total, axis, distance).astype(F32)
        after = (mine & distance) != 0
        own = total.astype(F32)
        here = jnp.where(after, before * other, 0.0)
        carried = here if carried is None else carried + here
        if 2 * distance < count:
            earlier, later = jnp.where(after, other, own), jnp.where(after, own, other)
            total = (decay * earlier + later).astype(value.dtype)
            before = jnp.where(after, decay * before, before)
            decay = decay * decay
        distance *= 2
    return carried


def local(latents, weight_in, weight_out, decay_table, decay_index):
    frames, strip, width, channels = latents.shape
    shaped = jax.ShapeDtypeStruct
    row, last = (frames, width, channels), (width, channels)
    inside = (strip - 2, width, channels)
    row_f32, row_bf16, last_bf16 = shaped(row, F32), shaped(row, BF16), shaped(last, BF16)
    inside_bf16 = shaped(inside, BF16)
    order = shaped((frames, 1, channels), F32)
    conv_flops = 2 * 9 * frames * strip * width * channels * channels
    taps = pltpu.VMEM((3, frames, strip, width, channels), F32)

    x_outer, x_inner = call(rows_kernel, (row_bf16,) * 2, [VMEM], (VMEM,) * 2, [], 2 * conv_flops)(latents)
    halo_outer = across_chips(x_outer)
    halo_inner = swapped(x_inner, "rows", 1)
    outer, middle, inner, sent, growth = call(
        drive_kernel,
        (row_f32, shaped((frames,) + inside, F32), row_f32, inside_bf16, order),
        [VMEM] * 4,
        (VMEM,) * 5,
        [taps, pltpu.VMEM((strip, width, channels), F32)],
        SMALL,
    )(latents, weight_in, decay_table[None, :], decay_index[None, :])

    def edge(beyond, halo, mixed, growth):
        kernel = functools.partial(drive_edge_kernel, beyond)
        return call(kernel, (row_f32, last_bf16, order), [VMEM] * 4, (VMEM,) * 3, [], SMALL)(halo, weight_in, growth, mixed)

    if lax.axis_size("tm") == 4:
        first = swapped(sent, "tm", 1)
        inner, sent_inner, growth = edge(from_inside, halo_inner, inner, growth)
        outer, sent_outer, growth = edge(from_outside, halo_outer, outer, growth)
        near_outer = swapped(sent_outer, "tm", 1)
        near_inner = swapped(sent_inner, "tm", 1)
        total, growth = call(pair_kernel, (inside_bf16, order), [VMEM] * 3, (VMEM,) * 2, [], SMALL)(sent, first, growth)
        second = swapped_between(total, 1)
        total_outer, growth = call(pair_kernel, (last_bf16, order), [VMEM] * 3, (VMEM,) * 2, [], SMALL)(sent_outer, near_outer, growth)
        far_outer = swapped(total_outer, "tm", 2)
        total_inner, growth = call(pair_kernel, (last_bf16, order), [VMEM] * 3, (VMEM,) * 2, [], LONG)(sent_inner, near_inner, growth)
        far_inner = swapped(total_inner, "tm", 2)
        message, growth = call(relay_kernel, (inside_bf16, order), [VMEM] * 3, (VMEM,) * 2, [], SMALL)(sent, second, growth)
        third = swapped(message, "tm", 1)
        finish_states = call(edge_states_kernel, (row_bf16, order), [VMEM] * 4, (VMEM,) * 2, [], SMALL)
        states_outer, growth = finish_states(outer, near_outer, far_outer, growth)
        halo_outer = across_chips(states_outer)
        states_inner, growth = finish_states(inner, near_inner, far_inner, growth)
        halo_inner = swapped(states_inner, "rows", 1)
        states_middle = call(middle_states_kernel, shaped((frames,) + inside, BF16), [VMEM] * 5, VMEM, [], SMALL)(
            middle, first, second, third, growth
        )
    else:
        inner, sent_inner, growth = edge(from_inside, halo_inner, inner, growth)
        outer, sent_outer, growth = edge(from_outside, halo_outer, outer, growth)
        over = growth[frames - 1]
        states_outer = (outer + growth * butterfly(sent_outer, over, "tm")[None]).astype(BF16)
        states_inner = (inner + growth * butterfly(sent_inner, over, "tm")[None]).astype(BF16)
        states_middle = (middle + growth[:, None] * butterfly(sent, over, "tm")[None]).astype(BF16)
        halo_outer = across_chips(states_outer)
        halo_inner = swapped(states_inner, "rows", 1)

    outer, middle, inner = call(
        mix_kernel,
        (row_f32, shaped((frames,) + inside, BF16), row_f32),
        [VMEM] * 5,
        (VMEM,) * 3,
        [pltpu.VMEM(latents.shape, BF16), taps],
        SMALL,
    )(states_outer, states_middle, states_inner, weight_out, latents)
    return call(
        finish_kernel,
        shaped(latents.shape, BF16),
        [VMEM] * 7,
        ANY,
        [pltpu.VMEM((2,) + row, BF16), pltpu.SemaphoreType.DMA((3 * frames,))],
        SMALL,
    )(halo_outer, halo_inner, weight_out, outer, inner, middle, latents)


def solution(mesh):
    in_specs = (P(("groups", "tm"), "rows", None, None), P(), P(), P(), P())
    out_specs = P(("groups", "tm"), "rows", None, None)
    return jax.shard_map(local, mesh=mesh, in_specs=in_specs, out_specs=out_specs, check_vma=False)
```

time: 39.2 us -> 28.4 us (0.72)
  waiting for transfers between devices: 19 us -> 4.37 us
  starting transfers between devices: 10.5 us -> 17.6 us
  local copies, waits for them, and re-layouts: 3.34 us -> 1.16 us
  other arithmetic: 1.09 us -> 0 us
    ppermute x4 -> x8, waiting for transfers between devices: 15.9 us -> 3.34 us  [swapped(): lax.ppermute(value, axis, [(i, i ^ distance) for i in range(lax.axis_size...]
    ppermute x4 -> x8, starting transfers between devices: 7.5 us -> 12.6 us  [swapped(): lax.ppermute(value, axis, [(i, i ^ distance) for i in range(lax.axis_size...]
    ppermute x4 -> x3, waiting for transfers between devices: 3.07 us -> 1.03 us  [the longest x2 1.02 us: across_chips(): return lax.ppermute(value, ('groups', 'rows'), pairs)]
    ppermute x4 -> x3, starting transfers between devices: 2.99 us -> 5.02 us  [the longest x2 4.95 us: across_chips(): return lax.ppermute(value, ('groups', 'rows'), pairs)]
    unnamed x11 -> x12, local copies, waits for them, and re-layouts: 2.33 us -> 1.16 us
    slice x2 -> x0, local copies, waits for them, and re-layouts: 1.01 us -> none  [the longest x1 0.99 us: local(): low, high = ring_halo(latents[:, :1], latents[:, strip - 1:], 'rows')]
    reduce_sum x1 -> x0, other arithmetic: 0.78 us -> none  [local(): jnp.sum(jnp.where(onehot, decay_table[None, :], 0.0), axis=1)[None, :]]
    pallas_call x4 -> x13, Pallas kernels: 4.97 us -> 4.99 us  [the longest x1 1.41 us: local(): call(mix_kernel, (row_f32, shaped((frames,) + inside, BF16), row_f32), [V...]
  transfers between devices with their start and end apart: 8 -> 11, of which waited for: 5 -> 4; matrix products, arithmetic and copies ran while one was open for 2% -> 0% of each run, Pallas kernels for 10% -> 13%
where the time goes in v2:
time: 28.4 us; the launch traced here: 28.3 us
  starting transfers between devices  17.6 us (62%)
  Pallas kernels  4.99 us (18%)
  waiting for transfers between devices  4.37 us (15%)
  local copies, waits for them, and re-layouts  1.16 us (4%)
    ppermute x8, starting transfers between devices, swapped(): lax.ppermute(value, axis, [(i, i ^ distance) for i in range(lax.axis_size...  12.6 us
    ppermute x2, starting transfers between devices, across_chips(): return lax.ppermute(value, ('groups', 'rows'), pairs)  4.95 us
    ppermute x8, waiting for transfers between devices, swapped(): lax.ppermute(value, axis, [(i, i ^ distance) for i in range(lax.axis_size...  3.34 us
    pallas_call x1, Pallas kernels, local(): call(mix_kernel, (row_f32, shaped((frames,) + inside, BF16), row_f32), [V...  1.41 us
    pallas_call x1, Pallas kernels, local(): call(drive_kernel, (row_f32, shaped((frames,) + inside, F32), row_f32, in...  1.31 us
    pallas_call x1, Pallas kernels, local(): call(finish_kernel, shaped(latents.shape, BF16), [VMEM] * 7, ANY, [pltpu....  1.25 us
    unnamed x12, local copies, waits for them, and re-layouts  1.16 us
    ppermute x2, waiting for transfers between devices, across_chips(): return lax.ppermute(value, ('groups', 'rows'), pairs)  1.02 us
  transfers between devices with their start and end apart: 11, of which 4 were waited for; matrix products, arithmetic and copies ran while one was open for 0% of the time, Pallas kernels for 13%

profile of v2, /device:TPU:0, one launch (start us, length us, event | category | flops | bytes accessed | tf_op | source)
XLA Modules:
  0.0 28.3 jit_solution(872959343036739982)
XLA Ops:
  0.0 0.0 copy-start
  0.0 0.0 copy-start.1
  0.0 1.1 %copy-done.1 = bf16[2,4,128,256]{3,2,1,0:T(8,128)(2,1)S(1)} copy-done((bf16[2,4,128,256]{3,2,1,0:T(8,128)(2,1)S(1)}, bf16[2,4,128,256]{3,2,1,0:T(8,128)(2,1)}, u32[]{:S(2)}) %copy-start.1) | copy-done | bytes 524312
  1.1 0.0 copy-start.4
  1.1 0.0 copy-start.5
  1.2 0.5 %collective-permute-start.1 = (bf16[2,128,256]{2,1,0:T(8,128)(2,1)S(1)}, bf16[2,128,256]{2,1,0:T(8,128)(2,1)S(1)}, u32[]{:S(2)}, u32[]{:S(2)}) collective-permute-start(bf16[2,128,256]{2,1,0:T(8,128)(2,1)S(1)} %get-tuple-element.34), channel_id=1, source_target_pairs={{0,1},{1,0},{2,3},{3,2},{4,5},{5,4},{6,7},{7,6},{8,9},{9,8},{10,11... | collective-permute-start | bytes 393224 | tf_op jit(solution)/shard_map/ppermute | solution.py:193
  1.7 2.6 %collective-permute-start = (bf16[2,128,256]{2,1,0:T(8,128)(2,1)S(1)}, bf16[2,128,256]{2,1,0:T(8,128)(2,1)S(1)}, u32[]{:S(2)}, u32[]{:S(2)}) collective-permute-start(bf16[2,128,256]{2,1,0:T(8,128)(2,1)S(1)} %get-tuple-element.33), channel_id=1, source_target_pairs={{0,16},{1,2},{2,1},{3,19},{16,0},{17,18},{18,17},{19,3},{4,20},{5,... | collective-permute-start | bytes 393224 | tf_op jit(solution)/shard_map/ppermute | solution.py:218
  4.3 0.0 copy-done
  4.3 0.0 copy-done.4
  4.3 0.0 copy-done.5
  4.3 1.3 %shard_map.56 = (f32[2,128,256]{2,1,0:T(8,128)S(1)}, f32[2,2,128,256]{3,2,1,0:T(8,128)S(1)}, f32[2,128,256]{2,1,0:T(8,128)S(1)}, bf16[2,128,256]{2,1,0:T(8,128)(2,1)S(1)}, f32[2,1,256]{2,1,0:T(1,128)S(1)}) custom-call(bf16[2,4,128,256]{3,2,1,0:T(8,128)(2,1)S(1)} %copy-done.1, bf16[3,3,256,256]{3,2,1,0:T(8,128)(2,1)S(1)} %copy-done, f32[1,16]{1,0:T(1,128)S(1)} %bitcast.3, ...), custom_call_target="tpu_custom_call" | custom-call | flops 1000 | bytes 1048576 | tf_op jit(solution)/shard_map/pallas_call | solution.py:254
  5.6 1.6 %collective-permute-start.3 = (bf16[2,128,256]{2,1,0:T(8,128)(2,1)S(1)}, bf16[2,128,256]{2,1,0:T(8,128)(2,1)S(1)}, u32[]{:S(2)}, u32[]{:S(2)}) collective-permute-start(bf16[2,128,256]{2,1,0:T(8,128)(2,1)S(1)} %get-tuple-element.41.own_ref), channel_id=1, source_target_pairs={{0,4},{4,0},{8,12},{12,8},{1,5},{5,1},{9,13},{13,9},{2,6},{6,2},{1... | collective-permute-start | bytes 393224 | tf_op jit(solution)/shard_map/ppermute | solution.py:193
  7.2 0.0 collective-permute-done.1.halo_ref
  7.2 0.3 shard_map.57
  7.5 0.0 collective-permute-done.halo_ref
  7.5 0.3 %shard_map.58 = (f32[2,128,256]{2,1,0:T(8,128)S(1)}, bf16[128,256]{1,0:T(8,128)(2,1)S(1)}, f32[2,1,256]{2,1,0:T(1,128)S(1)}) custom-call(bf16[2,128,256]{2,1,0:T(8,128)(2,1)S(1)} %collective-permute-done.halo_ref, bf16[3,3,256,256]{3,2,1,0:T(8,128)(2,1)S(1)} %copy-done, f32[2,1,256]{2,1,0:T(1,128)S(1)} %get-tuple-element.37.growth_ref, ...), custom_call_target="tpu_custom_call" | custom-call | flops 1000 | bytes 1048576 | tf_op jit(solution)/shard_map/pallas_call | solution.py:265
  7.8 1.8 %collective-permute-start.2 = (bf16[128,256]{1,0:T(8,128)(2,1)S(1)}, bf16[128,256]{1,0:T(8,128)(2,1)S(1)}, u32[]{:S(2)}, u32[]{:S(2)}) collective-permute-start(bf16[128,256]{1,0:T(8,128)(2,1)S(1)} %get-tuple-element.40.own_ref), channel_id=1, source_target_pairs={{0,4},{4,0},{8,12},{12,8},{1,5},{5,1},{9,13},{13,9},{2,6},{6,2},{1... | collective-permute-start | bytes 196616 | tf_op jit(solution)/shard_map/ppermute | solution.py:193
  9.6 0.3 collective-permute-start.6
  9.9 1.7 %collective-permute-done.3.other_ref.first_ref = bf16[2,128,256]{2,1,0:T(8,128)(2,1)S(1)} collective-permute-done((bf16[2,128,256]{2,1,0:T(8,128)(2,1)S(1)}, bf16[2,128,256]{2,1,0:T(8,128)(2,1)S(1)}, u32[]{:S(2)}, u32[]{:S(2)}) %collective-permute-start.3) | collective-permute-done | bytes 131104 | tf_op jit(solution)/shard_map/ppermute | solution.py:193
  11.6 0.1 shard_map.59
  11.7 0.1 collective-permute-start.5
  11.8 1.2 %collective-permute-done.2.other_ref.near_ref = bf16[128,256]{1,0:T(8,128)(2,1)S(1)} collective-permute-done((bf16[128,256]{1,0:T(8,128)(2,1)S(1)}, bf16[128,256]{1,0:T(8,128)(2,1)S(1)}, u32[]{:S(2)}, u32[]{:S(2)}) %collective-permute-start.2) | collective-permute-done | bytes 65568 | tf_op jit(solution)/shard_map/ppermute | solution.py:193
  13.0 2.7 %collective-permute-start.4 = (bf16[128,256]{1,0:T(8,128)(2,1)S(1)}, bf16[128,256]{1,0:T(8,128)(2,1)S(1)}, u32[]{:S(2)}, u32[]{:S(2)}) collective-permute-start(bf16[128,256]{1,0:T(8,128)(2,1)S(1)} %get-tuple-element.44), channel_id=1, source_target_pairs={{0,8},{4,12},{8,0},{12,4},{1,9},{5,13},{9,1},{13,5},{2,10},{6,14},... | collective-permute-start | bytes 196616 | tf_op jit(solution)/shard_map/ppermute | solution.py:193
  15.7 0.0 collective-permute-done.6.other_ref.near_ref
  15.8 0.0 copy-start.2
  15.8 0.0 copy-start.3
  15.8 0.9 %collective-permute-start.8 = (bf16[128,256]{1,0:T(8,128)(2,1)S(1)}, bf16[128,256]{1,0:T(8,128)(2,1)S(1)}, u32[]{:S(2)}, u32[]{:S(2)}) collective-permute-start(bf16[128,256]{1,0:T(8,128)(2,1)S(1)} %get-tuple-element.52), channel_id=1, source_target_pairs={{0,8},{4,12},{8,0},{12,4},{1,9},{5,13},{9,1},{13,5},{2,10},{6,14},... | collective-permute-start | bytes 196616 | tf_op jit(solution)/shard_map/ppermute | solution.py:193
  16.7 0.0 collective-permute-done.5.before_ref.second_ref
  16.7 4.4 %collective-permute-start.10 = (bf16[2,128,256]{2,1,0:T(8,128)(2,1)S(1)}, bf16[2,128,256]{2,1,0:T(8,128)(2,1)S(1)}, u32[]{:S(2)}, u32[]{:S(2)}) collective-permute-start(bf16[2,128,256]{2,1,0:T(8,128)(2,1)S(1)} %get-tuple-element.56), channel_id=1, source_target_pairs={{0,4},{4,0},{8,12},{12,8},{1,5},{5,1},{9,13},{13,9},{2,6},{6,2},{1... | collective-permute-start | bytes 393224 | tf_op jit(solution)/shard_map/ppermute | solution.py:193
  21.2 0.5 %collective-permute-done.4.far_ref = bf16[128,256]{1,0:T(8,128)(2,1)S(1)} collective-permute-done((bf16[128,256]{1,0:T(8,128)(2,1)S(1)}, bf16[128,256]{1,0:T(8,128)(2,1)S(1)}, u32[]{:S(2)}, u32[]{:S(2)}) %collective-permute-start.4) | collective-permute-done | bytes 65568 | tf_op jit(solution)/shard_map/ppermute | solution.py:193
  21.6 0.1 shard_map.63
  21.7 2.4 %collective-permute-start.7 = (bf16[2,128,256]{2,1,0:T(8,128)(2,1)S(1)}, bf16[2,128,256]{2,1,0:T(8,128)(2,1)S(1)}, u32[]{:S(2)}, u32[]{:S(2)}) collective-permute-start(bf16[2,128,256]{2,1,0:T(8,128)(2,1)S(1)} %get-tuple-element.50.outer_in), channel_id=1, source_target_pairs={{0,16},{1,2},{2,1},{3,19},{16,0},{17,18},{18,17},{19,3},{4,20},{5,... | collective-permute-start | bytes 393224 | tf_op jit(solution)/shard_map/ppermute | solution.py:218
  24.1 0.0 collective-permute-done.8.far_ref
  24.1 0.1 shard_map.64
  24.1 0.3 %collective-permute-start.9 = (bf16[2,128,256]{2,1,0:T(8,128)(2,1)S(1)}, bf16[2,128,256]{2,1,0:T(8,128)(2,1)S(1)}, u32[]{:S(2)}, u32[]{:S(2)}) collective-permute-start(bf16[2,128,256]{2,1,0:T(8,128)(2,1)S(1)} %get-tuple-element.54.inner_in), channel_id=1, source_target_pairs={{0,1},{1,0},{2,3},{3,2},{4,5},{5,4},{6,7},{7,6},{8,9},{9,8},{10,11... | collective-permute-start | bytes 393224 | tf_op jit(solution)/shard_map/ppermute | solution.py:193
  24.4 0.0 collective-permute-done.10.third_ref
  24.4 0.1 shard_map.65.middle_in
  24.6 0.0 copy-done.2
  24.6 0.0 copy-done.3
  24.6 1.4 %shard_map.66 = (f32[2,128,256]{2,1,0:T(8,128)S(1)}, bf16[2,2,128,256]{3,2,1,0:T(8,128)(2,1)S(1)}, f32[2,128,256]{2,1,0:T(8,128)S(1)}) custom-call(bf16[2,128,256]{2,1,0:T(8,128)(2,1)S(1)} %get-tuple-element.50.outer_in, bf16[2,2,128,256]{3,2,1,0:T(8,128)(2,1)S(1)} %shard_map.65.middle_in, bf16[2,128,256]{2,1,0:T(8,128)(2,1)S(1)} %get-tuple-element.54.inner_in, ...), custom_call_target="tpu_custom_call" | custom-call | flops 1000 | bytes 1048576 | tf_op jit(solution)/shard_map/pallas_call | solution.py:299
  26.0 1.0 %collective-permute-done.7.outer_halo = bf16[2,128,256]{2,1,0:T(8,128)(2,1)S(1)} collective-permute-done((bf16[2,128,256]{2,1,0:T(8,128)(2,1)S(1)}, bf16[2,128,256]{2,1,0:T(8,128)(2,1)S(1)}, u32[]{:S(2)}, u32[]{:S(2)}) %collective-permute-start.7) | collective-permute-done | bytes 131104 | tf_op jit(solution)/shard_map/ppermute | solution.py:218
  27.0 0.0 collective-permute-done.9.inner_halo
  27.0 1.2 %shard_map.67 = bf16[2,4,128,256]{3,2,1,0:T(8,128)(2,1)} custom-call(bf16[2,128,256]{2,1,0:T(8,128)(2,1)S(1)} %collective-permute-done.7.outer_halo, bf16[2,128,256]{2,1,0:T(8,128)(2,1)S(1)} %collective-permute-done.9.inner_halo, bf16[3,3,256,256]{3,2,1,0:T(8,128)(2,1)S(1)} %copy-done.3, f32[2,128,256]{2,1,0:T(8,128)S(1)} %get-tuple-element.58.outer_ref, ...), custom_call_target="tpu_custom_call" | custom-call | flops 1000 | bytes 1048576 | tf_op jit(solution)/shard_map/pallas_call | solution.py:307
  (4 shorter events, 0.2 us)
Async XLA Ops:
  0.0 4.3 %copy-start = (bf16[3,3,256,256]{3,2,1,0:T(8,128)(2,1)S(1)}, bf16[3,3,256,256]{3,2,1,0:T(8,128)(2,1)}, u32[]{:S(2)}) copy-start(bf16[3,3,256,256]{3,2,1,0:T(8,128)(2,1)} %w_ref.7) | copy-start | bytes 3538948
  0.0 1.1 %copy-start.1 = (bf16[2,4,128,256]{3,2,1,0:T(8,128)(2,1)S(1)}, bf16[2,4,128,256]{3,2,1,0:T(8,128)(2,1)}, u32[]{:S(2)}) copy-start(bf16[2,4,128,256]{3,2,1,0:T(8,128)(2,1)} %x_ref.7) | copy-start | bytes 1572868
  1.1 3.1 %copy-start.4 = (s32[256]{0:T(256)S(1)}, s32[256]{0:T(256)}, u32[]{:S(2)}) copy-start(s32[256]{0:T(256)} %param.9) | copy-start | bytes 3076
  1.1 3.1 %copy-start.5 = (f32[16]{0:T(128)S(1)}, f32[16]{0:T(128)}, u32[]{:S(2)}) copy-start(f32[16]{0:T(128)} %param.8) | copy-start | bytes 196
  1.2 6.1 %collective-permute-start.1 = (bf16[2,128,256]{2,1,0:T(8,128)(2,1)S(1)}, bf16[2,128,256]{2,1,0:T(8,128)(2,1)S(1)}, u32[]{:S(2)}, u32[]{:S(2)}) collective-permute-start(bf16[2,128,256]{2,1,0:T(8,128)(2,1)S(1)} %get-tuple-element.34), channel_id=1, source_target_pairs={{0,1},{1,0},{2,3},{3,2},{4,5},{5,4},{6,7},{7,6},{8,9},{9,8},{10,11... | collective-permute-start | bytes 393224 | tf_op jit(solution)/shard_map/ppermute | solution.py:193
  1.7 5.8 %collective-permute-start = (bf16[2,128,256]{2,1,0:T(8,128)(2,1)S(1)}, bf16[2,128,256]{2,1,0:T(8,128)(2,1)S(1)}, u32[]{:S(2)}, u32[]{:S(2)}) collective-permute-start(bf16[2,128,256]{2,1,0:T(8,128)(2,1)S(1)} %get-tuple-element.33), channel_id=1, source_target_pairs={{0,16},{1,2},{2,1},{3,19},{16,0},{17,18},{18,17},{19,3},{4,20},{5,... | collective-permute-start | bytes 393224 | tf_op jit(solution)/shard_map/ppermute | solution.py:218
  5.6 6.0 %collective-permute-start.3 = (bf16[2,128,256]{2,1,0:T(8,128)(2,1)S(1)}, bf16[2,128,256]{2,1,0:T(8,128)(2,1)S(1)}, u32[]{:S(2)}, u32[]{:S(2)}) collective-permute-start(bf16[2,128,256]{2,1,0:T(8,128)(2,1)S(1)} %get-tuple-element.41.own_ref), channel_id=1, source_target_pairs={{0,4},{4,0},{8,12},{12,8},{1,5},{5,1},{9,13},{13,9},{2,6},{6,2},{1... | collective-permute-start | bytes 393224 | tf_op jit(solution)/shard_map/ppermute | solution.py:193
  7.8 5.1 %collective-permute-start.2 = (bf16[128,256]{1,0:T(8,128)(2,1)S(1)}, bf16[128,256]{1,0:T(8,128)(2,1)S(1)}, u32[]{:S(2)}, u32[]{:S(2)}) collective-permute-start(bf16[128,256]{1,0:T(8,128)(2,1)S(1)} %get-tuple-element.40.own_ref), channel_id=1, source_target_pairs={{0,4},{4,0},{8,12},{12,8},{1,5},{5,1},{9,13},{13,9},{2,6},{6,2},{1... | collective-permute-start | bytes 196616 | tf_op jit(solution)/shard_map/ppermute | solution.py:193
  9.6 6.1 %collective-permute-start.6 = (bf16[128,256]{1,0:T(8,128)(2,1)S(1)}, bf16[128,256]{1,0:T(8,128)(2,1)S(1)}, u32[]{:S(2)}, u32[]{:S(2)}) collective-permute-start(bf16[128,256]{1,0:T(8,128)(2,1)S(1)} %get-tuple-element.46.own_ref), channel_id=1, source_target_pairs={{0,4},{4,0},{8,12},{12,8},{1,5},{5,1},{9,13},{13,9},{2,6},{6,2},{1... | collective-permute-start | bytes 196616 | tf_op jit(solution)/shard_map/ppermute | solution.py:193
  11.7 5.0 %collective-permute-start.5 = (bf16[2,128,256]{2,1,0:T(8,128)(2,1)S(1)}, bf16[2,128,256]{2,1,0:T(8,128)(2,1)S(1)}, u32[]{:S(2)}, u32[]{:S(2)}) collective-permute-start(bf16[2,128,256]{2,1,0:T(8,128)(2,1)S(1)} %get-tuple-element.45), channel_id=1, source_target_pairs={{0,1},{1,0},{2,3},{3,2},{4,8},{5,9},{6,10},{7,11},{8,4},{9,5},{10,... | collective-permute-start | bytes 393224 | tf_op jit(solution)/shard_map/ppermute | solution.py:205
  13.0 8.6 %collective-permute-start.4 = (bf16[128,256]{1,0:T(8,128)(2,1)S(1)}, bf16[128,256]{1,0:T(8,128)(2,1)S(1)}, u32[]{:S(2)}, u32[]{:S(2)}) collective-permute-start(bf16[128,256]{1,0:T(8,128)(2,1)S(1)} %get-tuple-element.44), channel_id=1, source_target_pairs={{0,8},{4,12},{8,0},{12,4},{1,9},{5,13},{9,1},{13,5},{2,10},{6,14},... | collective-permute-start | bytes 196616 | tf_op jit(solution)/shard_map/ppermute | solution.py:193
  15.8 8.8 %copy-start.2 = (bf16[2,4,128,256]{3,2,1,0:T(8,128)(2,1)S(1)}, bf16[2,4,128,256]{3,2,1,0:T(8,128)(2,1)}, u32[]{:S(2)}) copy-start(bf16[2,4,128,256]{3,2,1,0:T(8,128)(2,1)} %x_ref.7) | copy-start | bytes 1572868
  15.8 8.8 %copy-start.3 = (bf16[3,3,256,256]{3,2,1,0:T(8,128)(2,1)S(1)}, bf16[3,3,256,256]{3,2,1,0:T(8,128)(2,1)}, u32[]{:S(2)}) copy-start(bf16[3,3,256,256]{3,2,1,0:T(8,128)(2,1)} %w_ref.9) | copy-start | bytes 3538948
  15.8 8.3 %collective-permute-start.8 = (bf16[128,256]{1,0:T(8,128)(2,1)S(1)}, bf16[128,256]{1,0:T(8,128)(2,1)S(1)}, u32[]{:S(2)}, u32[]{:S(2)}) collective-permute-start(bf16[128,256]{1,0:T(8,128)(2,1)S(1)} %get-tuple-element.52), channel_id=1, source_target_pairs={{0,8},{4,12},{8,0},{12,4},{1,9},{5,13},{9,1},{13,5},{2,10},{6,14},... | collective-permute-start | bytes 196616 | tf_op jit(solution)/shard_map/ppermute | solution.py:193
  16.7 7.7 %collective-permute-start.10 = (bf16[2,128,256]{2,1,0:T(8,128)(2,1)S(1)}, bf16[2,128,256]{2,1,0:T(8,128)(2,1)S(1)}, u32[]{:S(2)}, u32[]{:S(2)}) collective-permute-start(bf16[2,128,256]{2,1,0:T(8,128)(2,1)S(1)} %get-tuple-element.56), channel_id=1, source_target_pairs={{0,4},{4,0},{8,12},{12,8},{1,5},{5,1},{9,13},{13,9},{2,6},{6,2},{1... | collective-permute-start | bytes 393224 | tf_op jit(solution)/shard_map/ppermute | solution.py:193
  21.7 5.3 %collective-permute-start.7 = (bf16[2,128,256]{2,1,0:T(8,128)(2,1)S(1)}, bf16[2,128,256]{2,1,0:T(8,128)(2,1)S(1)}, u32[]{:S(2)}, u32[]{:S(2)}) collective-permute-start(bf16[2,128,256]{2,1,0:T(8,128)(2,1)S(1)} %get-tuple-element.50.outer_in), channel_id=1, source_target_pairs={{0,16},{1,2},{2,1},{3,19},{16,0},{17,18},{18,17},{19,3},{4,20},{5,... | collective-permute-start | bytes 393224 | tf_op jit(solution)/shard_map/ppermute | solution.py:218
  24.1 2.9 %collective-permute-start.9 = (bf16[2,128,256]{2,1,0:T(8,128)(2,1)S(1)}, bf16[2,128,256]{2,1,0:T(8,128)(2,1)S(1)}, u32[]{:S(2)}, u32[]{:S(2)}) collective-permute-start(bf16[2,128,256]{2,1,0:T(8,128)(2,1)S(1)} %get-tuple-element.54.inner_in), channel_id=1, source_target_pairs={{0,1},{1,0},{2,3},{3,2},{4,5},{5,4},{6,7},{7,6},{8,9},{9,8},{10,11... | collective-permute-start | bytes 393224 | tf_op jit(solution)/shard_map/ppermute | solution.py:193

commit v3 on v2

--- a/solution.py
+++ b/solution.py
@@ -121,42 +121,89 @@
     order_ref[...] = growth_ref[...]
 
 
+def far_relay_kernel(own_ref, far_ref, growth_ref, message_ref, order_ref):
+    over = growth_ref[growth_ref.shape[0] - 1]
+    mine = lax.axis_index("tm")
+    far = jnp.where(mine >= 2, far_ref[...].astype(F32), 0.0)
+    message = jnp.where(mine % 2 == 1, far, over * over * far + own_ref[...].astype(F32))
+    message_ref[...] = message.astype(BF16)
+    order_ref[...] = growth_ref[...]
+
+
+def far_states_kernel(row_ref, far_ref, near_ref, growth_ref, states_ref, order_ref):
+    frames = row_ref.shape[0]
+    mine = lax.axis_index("tm")
+    far = jnp.where(mine >= 2, far_ref[...].astype(F32), 0.0)
+    near = jnp.where(mine >= 1, near_ref[...].astype(F32), 0.0)
+    carried = near + growth_ref[frames - 1] * far
+    for f in range(frames):
+        states_ref[f] = (row_ref[f] + growth_ref[f] * carried).astype(BF16)
+    order_ref[...] = growth_ref[...]
+
+
 def relay_kernel(own_ref, before_ref, growth_ref, message_ref, order_ref):
     over = growth_ref[growth_ref.shape[0] - 1]
     message_ref[...] = (over * before_ref[...].astype(F32) + own_ref[...].astype(F32)).astype(BF16)
     order_ref[...] = growth_ref[...]
 
 
-def middle_states_kernel(middle_ref, first_ref, second_ref, third_ref, growth_ref, states_ref):
-    frames = middle_ref.shape[0]
-    mine = lax.axis_index("tm")
-    carried = jnp.zeros(first_ref.shape, F32)
-    for hop, ref in enumerate((first_ref, second_ref, third_ref)):
-        carried = jnp.where(mine == hop + 1, ref[...].astype(F32), carried)
-    for f in range(frames):
-        states_ref[f] = (middle_ref[f] + growth_ref[f] * carried).astype(BF16)
-
-
 def residual(x, mixed):
     return (x.astype(F32) + jax.nn.gelu(mixed)).astype(BF16)
 
 
-def mix_kernel(outer_in, middle_in, inner_in, w_ref, x_ref, outer_ref, middle_ref, inner_ref, states, taps):
-    frames, strip = x_ref.shape[:2]
-    for f in range(frames):
-        states[f, place(0, strip)] = outer_in[f]
-        states[f, 1 : strip - 1] = middle_in[f]
-        states[f, place(strip - 1, strip)] = inner_in[f]
-    own_rows(states, w_ref, taps)
-    for f in range(frames):
-        mixed = join_columns(taps[0, f], taps[1, f], taps[2, f])
-        middle_ref[f] = residual(x_ref[f, 1 : strip - 1], mixed[1 : strip - 1])
-        first, last = mixed[0], mixed[strip - 1]
-        outer_ref[f] = jnp.where(turned() == 1, last, first)
-        inner_ref[f] = jnp.where(turned() == 1, first, last)
-
-
-def finish_kernel(outer_halo, inner_halo, w_ref, outer_ref, inner_ref, middle_ref, x_ref, out_ref, ready, sems):
+def mix_ends_kernel(outer_in, inner_in, w_ref, outer_ref, middle_ref, inner_ref):
+    frames, inside = middle_ref.shape[:2]
+    outer, inner = outer_in[...], inner_in[...]
+    first = jnp.where(turned() == 1, inner, outer)
+    last = jnp.where(turned() == 1, outer, inner)
+    parts = [[[] for _ in range(inside)] for _ in range(3)]
+    ends = []
+    for q in range(3):
+        ends.append(matmul(jnp.concatenate([outer, inner]), w_ref[1, q]))
+        parts[q][0].append(matmul(first, w_ref[0, q]))
+        parts[q][inside - 1].append(matmul(last, w_ref[2, q]))
+    for row in range(inside):
+        if parts[0][row]:
+            middle_ref[:, row] = join_columns(*[sum(parts[q][row]) for q in range(3)])
+        else:
+            middle_ref[:, row] = jnp.zeros(first.shape, F32)
+    ends = join_columns(*ends)
+    outer_ref[...] = ends[:frames]
+    inner_ref[...] = ends[frames:]
+
+
+def mix_inside_kernel(
+    first_ref, second_ref, third_ref, growth_ref, states_ref, w_ref, outer_in, middle_in, inner_in, x_ref,
+    outer_ref, middle_ref, inner_ref, taps, mixed,
+):
+    frames, strip = x_ref.shape[:2]
+    mine = lax.axis_index("tm")
+    carried = third_ref[...].astype(F32)
+    for hop, ref in enumerate((first_ref, second_ref)):
+        carried = jnp.where(mine == hop + 1, ref[...].astype(F32), carried)
+    carried = jnp.where(mine == 0, 0.0, carried)
+    states = (states_ref[...] + growth_ref[...][:, None] * carried[None]).astype(BF16)
+    for q in range(3):
+        above, level, below = (matmul(states, w_ref[tap, q]) for tap in (2, 1, 0))
+        for f in range(frames):
+            taps[q, f, 1 : strip - 1] = level[f]
+            taps[q, f, 0] = above[f, 0]
+            taps[q, f, strip - 1] = below[f, strip - 3]
+            if strip > 3:
+                taps[q, f, 1 : strip - 2] += above[f, 1:]
+                taps[q, f, 2 : strip - 1] += below[f, : strip - 3]
+    for f in range(frames):
+        mixed[...] = join_columns(taps[0, f], taps[1, f], taps[2, f])
+        outer_ref[f] = outer_in[f] + mixed[place(0, strip)]
+        inner_ref[f] = inner_in[f] + mixed[place(strip - 1, strip)]
+        middle_ref[f] = residual(x_ref[f, 1 : strip - 1], middle_in[f] + mixed[1 : strip - 1])
+
+
+def mix_beyond_kernel(halo_ref, w_ref, outer_in, outer_ref):
+    outer_ref[...] = outer_in[...] + from_outside(halo_ref, w_ref)
+
+
+def finish_kernel(halo_ref, w_ref, outer_ref, inner_ref, middle_ref, x_ref, out_ref, ready, sems):
     frames, strip = x_ref.shape[:2]
     copies = []
 
@@ -166,9 +213,8 @@
 
     for f in range(frames):
         send(middle_ref.at[f], out_ref.at[f, 1 : strip - 1])
-    edges = ((inner_ref, inner_halo, from_inside, strip - 1), (outer_ref, outer_halo, from_outside, 0))
-    for side, (mixed_ref, halo_ref, beyond, row) in enumerate(edges):
-        mixed = mixed_ref[...] + beyond(halo_ref, w_ref)
+    for side, row in ((0, 0), (1, strip - 1)):
+        mixed = inner_ref[...] + from_inside(halo_ref, w_ref) if side else outer_ref[...]
         for f in range(frames):
             ready[side, f] = residual(x_ref[f, place(row, strip)], mixed[f])
             send(ready.at[side, f], out_ref.at[f, place(row, strip)])
@@ -243,7 +289,7 @@
     row, last = (frames, width, channels), (width, channels)
     inside = (strip - 2, width, channels)
     row_f32, row_bf16, last_bf16 = shaped(row, F32), shaped(row, BF16), shaped(last, BF16)
-    inside_bf16 = shaped(inside, BF16)
+    inside_bf16, middle_f32 = shaped(inside, BF16), shaped((frames,) + inside, F32)
     order = shaped((frames, 1, channels), F32)
     conv_flops = 2 * 9 * frames * strip * width * channels * channels
     taps = pltpu.VMEM((3, frames, strip, width, channels), F32)
@@ -253,7 +299,7 @@
     halo_inner = swapped(x_inner, "rows", 1)
     outer, middle, inner, sent, growth = call(
         drive_kernel,
-        (row_f32, shaped((frames,) + inside, F32), row_f32, inside_bf16, order),
+        (row_f32, middle_f32, row_f32, inside_bf16, order),
         [VMEM] * 4,
         (VMEM,) * 5,
         [taps, pltpu.VMEM((strip, width, channels), F32)],
@@ -268,50 +314,54 @@
         first = swapped(sent, "tm", 1)
         inner, sent_inner, growth = edge(from_inside, halo_inner, inner, growth)
         outer, sent_outer, growth = edge(from_outside, halo_outer, outer, growth)
-        near_outer = swapped(sent_outer, "tm", 1)
+        far_outer = swapped(sent_outer, "tm", 2)
         near_inner = swapped(sent_inner, "tm", 1)
         total, growth = call(pair_kernel, (inside_bf16, order), [VMEM] * 3, (VMEM,) * 2, [], SMALL)(sent, first, growth)
         second = swapped_between(total, 1)
-        total_outer, growth = call(pair_kernel, (last_bf16, order), [VMEM] * 3, (VMEM,) * 2, [], SMALL)(sent_outer, near_outer, growth)
-        far_outer = swapped(total_outer, "tm", 2)
+        relayed, growth = call(far_relay_kernel, (last_bf16, order), [VMEM] * 3, (VMEM,) * 2, [], SMALL)(sent_outer, far_outer, growth)
+        near_outer = swapped(relayed, "tm", 1)
         total_inner, growth = call(pair_kernel, (last_bf16, order), [VMEM] * 3, (VMEM,) * 2, [], LONG)(sent_inner, near_inner, growth)
         far_inner = swapped(total_inner, "tm", 2)
         message, growth = call(relay_kernel, (inside_bf16, order), [VMEM] * 3, (VMEM,) * 2, [], SMALL)(sent, second, growth)
         third = swapped(message, "tm", 1)
-        finish_states = call(edge_states_kernel, (row_bf16, order), [VMEM] * 4, (VMEM,) * 2, [], SMALL)
-        states_outer, growth = finish_states(outer, near_outer, far_outer, growth)
+        states_outer, growth = call(far_states_kernel, (row_bf16, order), [VMEM] * 4, (VMEM,) * 2, [], SMALL)(
+            outer, far_outer, near_outer, growth
+        )
         halo_outer = across_chips(states_outer)
-        states_inner, growth = finish_states(inner, near_inner, far_inner, growth)
+        states_inner, growth = call(edge_states_kernel, (row_bf16, order), [VMEM] * 4, (VMEM,) * 2, [], SMALL)(
+            inner, near_inner, far_inner, growth
+        )
         halo_inner = swapped(states_inner, "rows", 1)
-        states_middle = call(middle_states_kernel, shaped((frames,) + inside, BF16), [VMEM] * 5, VMEM, [], SMALL)(
-            middle, first, second, third, growth
-        )
     else:
         inner, sent_inner, growth = edge(from_inside, halo_inner, inner, growth)
         outer, sent_outer, growth = edge(from_outside, halo_outer, outer, growth)
         over = growth[frames - 1]
         states_outer = (outer + growth * butterfly(sent_outer, over, "tm")[None]).astype(BF16)
         states_inner = (inner + growth * butterfly(sent_inner, over, "tm")[None]).astype(BF16)
-        states_middle = (middle + growth[:, None] * butterfly(sent, over, "tm")[None]).astype(BF16)
+        first = second = third = butterfly(sent, over, "tm").astype(BF16)
         halo_outer = across_chips(states_outer)
         halo_inner = swapped(states_inner, "rows", 1)
 
+    ends = call(mix_ends_kernel, (row_f32, middle_f32, row_f32), [VMEM] * 3, (VMEM,) * 3, [], SMALL)(
+        states_outer, states_inner, weight_out
+    )
     outer, middle, inner = call(
-        mix_kernel,
+        mix_inside_kernel,
         (row_f32, shaped((frames,) + inside, BF16), row_f32),
-        [VMEM] * 5,
+        [VMEM] * 10,
         (VMEM,) * 3,
-        [pltpu.VMEM(latents.shape, BF16), taps],
+        [taps, pltpu.VMEM((strip, width, channels), F32)],
         SMALL,
-    )(states_outer, states_middle, states_inner, weight_out, latents)
+    )(first, second, third, growth, middle, weight_out, *ends, latents)
+    outer = call(mix_beyond_kernel, row_f32, [VMEM] * 3, VMEM, [], SMALL)(halo_outer, weight_out, outer)
     return call(
         finish_kernel,
         shaped(latents.shape, BF16),
-        [VMEM] * 7,
+        [VMEM] * 6,
         ANY,
         [pltpu.VMEM((2,) + row, BF16), pltpu.SemaphoreType.DMA((3 * frames,))],
         SMALL,
-    )(halo_outer, halo_inner, weight_out, outer, inner, middle, latents)
+    )(halo_inner, weight_out, outer, inner, middle, latents)
 
 
 def solution(mesh):

time: 28.4 us -> 26.9 us (0.947)
  starting transfers between devices: 17.6 us -> 16.4 us
  waiting for transfers between devices: 4.37 us -> 3.72 us
  Pallas kernels: 4.99 us -> 5.31 us
    ppermute x2, waiting for transfers between devices: 1.02 us -> 0.01 us  [across_chips(): return lax.ppermute(value, ('groups', 'rows'), pairs)]
    ppermute x2, starting transfers between devices: 4.95 us -> 4.18 us  [across_chips(): return lax.ppermute(value, ('groups', 'rows'), pairs)]
    ppermute x8, starting transfers between devices: 12.6 us -> 12.2 us  [swapped(): lax.ppermute(value, axis, [(i, i ^ distance) for i in range(lax.axis_size...]
    ppermute x8, waiting for transfers between devices: 3.34 us -> 3.72 us  [swapped(): lax.ppermute(value, axis, [(i, i ^ distance) for i in range(lax.axis_size...]
    pallas_call x7 -> x8, Pallas kernels: 4.22 us -> 4.54 us  [the longest x1 1.31 us: local(): call(drive_kernel, (row_f32, middle_f32, row_f32, inside_bf16, order), [V...]
  transfers between devices with their start and end apart: 11 -> 11, of which waited for: 4 -> 3; matrix products, arithmetic and copies ran while one was open for 0% -> 0% of each run, Pallas kernels for 13% -> 15%
where the time goes in v3:
time: 26.9 us; the launch traced here: 26.8 us
  starting transfers between devices  16.4 us (61%)
  Pallas kernels  5.31 us (20%)
  waiting for transfers between devices  3.72 us (14%)
  local copies, waits for them, and re-layouts  1.16 us (4%)
    ppermute x8, starting transfers between devices, swapped(): lax.ppermute(value, axis, [(i, i ^ distance) for i in range(lax.axis_size...  12.2 us
    ppermute x2, starting transfers between devices, across_chips(): return lax.ppermute(value, ('groups', 'rows'), pairs)  4.18 us
    ppermute x8, waiting for transfers between devices, swapped(): lax.ppermute(value, axis, [(i, i ^ distance) for i in range(lax.axis_size...  3.72 us
    pallas_call x1, Pallas kernels, local(): call(drive_kernel, (row_f32, middle_f32, row_f32, inside_bf16, order), [V...  1.31 us
    unnamed x12, local copies, waits for them, and re-layouts  1.16 us
    pallas_call x1, Pallas kernels, local(): call(finish_kernel, shaped(latents.shape, BF16), [VMEM] * 6, ANY, [pltpu....  1.15 us
    pallas_call x1, Pallas kernels, local(): call(mix_inside_kernel, (row_f32, shaped((frames,) + inside, BF16), row_f...  1.05 us
    pallas_call x1, Pallas kernels, local(): call(mix_ends_kernel, (row_f32, middle_f32, row_f32), [VMEM] * 3, (VMEM,)...  0.59 us
  transfers between devices with their start and end apart: 11, of which 3 were waited for; matrix products, arithmetic and copies ran while one was open for 0% of the time, Pallas kernels for 15%

profile of v3, /device:TPU:0, one launch (start us, length us, event | category | flops | bytes accessed | tf_op | source)
XLA Modules:
  0.0 26.8 jit_solution(8342947287508377374)
XLA Ops:
  0.0 0.0 copy-start.1
  0.0 0.0 copy-start.2
  0.0 1.1 %copy-done.2 = bf16[2,4,128,256]{3,2,1,0:T(8,128)(2,1)S(1)} copy-done((bf16[2,4,128,256]{3,2,1,0:T(8,128)(2,1)S(1)}, bf16[2,4,128,256]{3,2,1,0:T(8,128)(2,1)}, u32[]{:S(2)}) %copy-start.2) | copy-done | bytes 524312
  1.1 0.0 copy-start.4
  1.1 0.0 copy-start.5
  1.2 0.5 %collective-permute-start = (bf16[2,128,256]{2,1,0:T(8,128)(2,1)S(1)}, bf16[2,128,256]{2,1,0:T(8,128)(2,1)S(1)}, u32[]{:S(2)}, u32[]{:S(2)}) collective-permute-start(bf16[2,128,256]{2,1,0:T(8,128)(2,1)S(1)} %get-tuple-element.36), channel_id=1, source_target_pairs={{0,1},{1,0},{2,3},{3,2},{4,5},{5,4},{6,7},{7,6},{8,9},{9,8},{10,11... | collective-permute-start | bytes 393224 | tf_op jit(solution)/shard_map/ppermute | solution.py:239
  1.7 2.6 %collective-permute-start.2 = (bf16[2,128,256]{2,1,0:T(8,128)(2,1)S(1)}, bf16[2,128,256]{2,1,0:T(8,128)(2,1)S(1)}, u32[]{:S(2)}, u32[]{:S(2)}) collective-permute-start(bf16[2,128,256]{2,1,0:T(8,128)(2,1)S(1)} %get-tuple-element.41), channel_id=1, source_target_pairs={{0,16},{1,2},{2,1},{3,19},{16,0},{17,18},{18,17},{19,3},{4,20},{5,... | collective-permute-start | bytes 393224 | tf_op jit(solution)/shard_map/ppermute | solution.py:264
  4.3 0.0 copy-done.1
  4.3 0.0 copy-done.4
  4.3 0.0 copy-done.5
  4.3 1.3 %shard_map.56 = (f32[2,128,256]{2,1,0:T(8,128)S(1)}, f32[2,2,128,256]{3,2,1,0:T(8,128)S(1)}, f32[2,128,256]{2,1,0:T(8,128)S(1)}, bf16[2,128,256]{2,1,0:T(8,128)(2,1)S(1)}, f32[2,1,256]{2,1,0:T(1,128)S(1)}) custom-call(bf16[2,4,128,256]{3,2,1,0:T(8,128)(2,1)S(1)} %copy-done.2, bf16[3,3,256,256]{3,2,1,0:T(8,128)(2,1)S(1)} %copy-done.1, f32[1,16]{1,0:T(1,128)S(1)} %bitcast.3, ...), custom_call_target="tpu_custom_call" | custom-call | flops 1000 | bytes 1048576 | tf_op jit(solution)/shard_map/pallas_call | solution.py:300
  5.6 1.6 %collective-permute-start.4 = (bf16[2,128,256]{2,1,0:T(8,128)(2,1)S(1)}, bf16[2,128,256]{2,1,0:T(8,128)(2,1)S(1)}, u32[]{:S(2)}, u32[]{:S(2)}) collective-permute-start(bf16[2,128,256]{2,1,0:T(8,128)(2,1)S(1)} %get-tuple-element.45.own_ref), channel_id=1, source_target_pairs={{0,4},{4,0},{8,12},{12,8},{1,5},{5,1},{9,13},{13,9},{2,6},{6,2},{1... | collective-permute-start | bytes 393224 | tf_op jit(solution)/shard_map/ppermute | solution.py:239
  7.2 0.0 collective-permute-done.halo_ref
  7.2 0.3 %shard_map.57 = (f32[2,128,256]{2,1,0:T(8,128)S(1)}, bf16[128,256]{1,0:T(8,128)(2,1)S(1)}, f32[2,1,256]{2,1,0:T(1,128)S(1)}) custom-call(bf16[2,128,256]{2,1,0:T(8,128)(2,1)S(1)} %collective-permute-done.halo_ref, bf16[3,3,256,256]{3,2,1,0:T(8,128)(2,1)S(1)} %copy-done.1, f32[2,1,256]{2,1,0:T(1,128)S(1)} %get-tuple-element.37.growth_ref, ...), custom_call_target="tpu_custom_call" | custom-call | flops 1000 | bytes 1048576 | tf_op jit(solution)/shard_map/pallas_call | solution.py:311
  7.5 0.0 collective-permute-done.2.halo_ref
  7.5 0.3 %shard_map.58 = (f32[2,128,256]{2,1,0:T(8,128)S(1)}, bf16[128,256]{1,0:T(8,128)(2,1)S(1)}, f32[2,1,256]{2,1,0:T(1,128)S(1)}) custom-call(bf16[2,128,256]{2,1,0:T(8,128)(2,1)S(1)} %collective-permute-done.2.halo_ref, bf16[3,3,256,256]{3,2,1,0:T(8,128)(2,1)S(1)} %copy-done.1, f32[2,1,256]{2,1,0:T(1,128)S(1)} %get-tuple-element.42.growth_ref, ...), custom_call_target="tpu_custom_call" | custom-call | flops 1000 | bytes 1048576 | tf_op jit(solution)/shard_map/pallas_call | solution.py:311
  7.8 2.8 %collective-permute-start.3 = (bf16[128,256]{1,0:T(8,128)(2,1)S(1)}, bf16[128,256]{1,0:T(8,128)(2,1)S(1)}, u32[]{:S(2)}, u32[]{:S(2)}) collective-permute-start(bf16[128,256]{1,0:T(8,128)(2,1)S(1)} %get-tuple-element.44.own_ref), channel_id=1, source_target_pairs={{0,8},{4,12},{8,0},{12,4},{1,9},{5,13},{9,1},{13,5},{2,10},{6,14},... | collective-permute-start | bytes 196616 | tf_op jit(solution)/shard_map/ppermute | solution.py:239
  10.7 1.6 %collective-permute-start.1 = (bf16[128,256]{1,0:T(8,128)(2,1)S(1)}, bf16[128,256]{1,0:T(8,128)(2,1)S(1)}, u32[]{:S(2)}, u32[]{:S(2)}) collective-permute-start(bf16[128,256]{1,0:T(8,128)(2,1)S(1)} %get-tuple-element.40.own_ref), channel_id=1, source_target_pairs={{0,4},{4,0},{8,12},{12,8},{1,5},{5,1},{9,13},{13,9},{2,6},{6,2},{1... | collective-permute-start | bytes 196616 | tf_op jit(solution)/shard_map/ppermute | solution.py:239
  12.2 0.0 collective-permute-done.4.other_ref.first_ref
  12.2 0.1 shard_map.59
  12.3 0.1 collective-permute-start.7
  12.4 1.0 %collective-permute-done.3.far_ref = bf16[128,256]{1,0:T(8,128)(2,1)S(1)} collective-permute-done((bf16[128,256]{1,0:T(8,128)(2,1)S(1)}, bf16[128,256]{1,0:T(8,128)(2,1)S(1)}, u32[]{:S(2)}, u32[]{:S(2)}) %collective-permute-start.3) | collective-permute-done | bytes 65568 | tf_op jit(solution)/shard_map/ppermute | solution.py:239
  13.4 2.3 %collective-permute-start.6 = (bf16[128,256]{1,0:T(8,128)(2,1)S(1)}, bf16[128,256]{1,0:T(8,128)(2,1)S(1)}, u32[]{:S(2)}, u32[]{:S(2)}) collective-permute-start(bf16[128,256]{1,0:T(8,128)(2,1)S(1)} %get-tuple-element.51), channel_id=1, source_target_pairs={{0,4},{4,0},{8,12},{12,8},{1,5},{5,1},{9,13},{13,9},{2,6},{6,2},{1... | collective-permute-start | bytes 196616 | tf_op jit(solution)/shard_map/ppermute | solution.py:239
  15.7 0.0 collective-permute-done.1.other_ref.near_ref
  15.7 0.0 copy-start
  15.7 3.2 %collective-permute-start.5 = (bf16[128,256]{1,0:T(8,128)(2,1)S(1)}, bf16[128,256]{1,0:T(8,128)(2,1)S(1)}, u32[]{:S(2)}, u32[]{:S(2)}) collective-permute-start(bf16[128,256]{1,0:T(8,128)(2,1)S(1)} %get-tuple-element.49), channel_id=1, source_target_pairs={{0,8},{4,12},{8,0},{12,4},{1,9},{5,13},{9,1},{13,5},{2,10},{6,14},... | collective-permute-start | bytes 196616 | tf_op jit(solution)/shard_map/ppermute | solution.py:239
  18.9 0.0 collective-permute-done.7.before_ref.second_ref
  19.0 0.0 copy-start.3
  19.0 0.1 collective-permute-start.10
  19.1 0.0 collective-permute-done.6.near_ref
  19.1 0.1 shard_map.63
  19.2 1.6 %collective-permute-start.9 = (bf16[2,128,256]{2,1,0:T(8,128)(2,1)S(1)}, bf16[2,128,256]{2,1,0:T(8,128)(2,1)S(1)}, u32[]{:S(2)}, u32[]{:S(2)}) collective-permute-start(bf16[2,128,256]{2,1,0:T(8,128)(2,1)S(1)} %get-tuple-element.57.outer_in), channel_id=1, source_target_pairs={{0,16},{1,2},{2,1},{3,19},{16,0},{17,18},{18,17},{19,3},{4,20},{5,... | collective-permute-start | bytes 393224 | tf_op jit(solution)/shard_map/ppermute | solution.py:264
  20.7 1.4 %collective-permute-done.5.far_ref = bf16[128,256]{1,0:T(8,128)(2,1)S(1)} collective-permute-done((bf16[128,256]{1,0:T(8,128)(2,1)S(1)}, bf16[128,256]{1,0:T(8,128)(2,1)S(1)}, u32[]{:S(2)}, u32[]{:S(2)}) %collective-permute-start.5) | collective-permute-done | bytes 65568 | tf_op jit(solution)/shard_map/ppermute | solution.py:239
  22.1 0.1 shard_map.64
  22.2 0.1 collective-permute-start.8
  22.3 0.0 copy-done
  22.3 0.6 %shard_map.65 = (f32[2,128,256]{2,1,0:T(8,128)S(1)}, f32[2,2,128,256]{3,2,1,0:T(8,128)S(1)}, f32[2,128,256]{2,1,0:T(8,128)S(1)}) custom-call(bf16[2,128,256]{2,1,0:T(8,128)(2,1)S(1)} %get-tuple-element.57.outer_in, bf16[2,128,256]{2,1,0:T(8,128)(2,1)S(1)} %get-tuple-element.56.inner_in, bf16[3,3,256,256]{3,2,1,0:T(8,128)(2,1)S(1)} %copy-done), custom_call_target="tpu_custom_call" | custom-call | flops 1000 | bytes 1048576 | tf_op jit(solution)/shard_map/pallas_call | solution.py:345
  22.9 1.4 %collective-permute-done.10.third_ref = bf16[2,128,256]{2,1,0:T(8,128)(2,1)S(1)} collective-permute-done((bf16[2,128,256]{2,1,0:T(8,128)(2,1)S(1)}, bf16[2,128,256]{2,1,0:T(8,128)(2,1)S(1)}, u32[]{:S(2)}, u32[]{:S(2)}) %collective-permute-start.10) | collective-permute-done | bytes 131104 | tf_op jit(solution)/shard_map/ppermute | solution.py:239
  24.2 0.0 copy-done.3
  24.2 1.1 %shard_map.66 = (f32[2,128,256]{2,1,0:T(8,128)S(1)}, bf16[2,2,128,256]{3,2,1,0:T(8,128)(2,1)S(1)}, f32[2,128,256]{2,1,0:T(8,128)S(1)}) custom-call(bf16[2,128,256]{2,1,0:T(8,128)(2,1)S(1)} %collective-permute-done.4.other_ref.first_ref, bf16[2,128,256]{2,1,0:T(8,128)(2,1)S(1)} %collective-permute-done.7.before_ref.second_ref, ...), custom_call_target="tpu_custom_call" | custom-call | flops 1000 | bytes 1048576 | tf_op jit(solution)/shard_map/pallas_call | solution.py:348
  25.3 0.0 collective-permute-done.9.halo_ref
  25.3 0.3 %shard_map.67.outer_ref = f32[2,128,256]{2,1,0:T(8,128)S(1)} custom-call(bf16[2,128,256]{2,1,0:T(8,128)(2,1)S(1)} %collective-permute-done.9.halo_ref, bf16[3,3,256,256]{3,2,1,0:T(8,128)(2,1)S(1)} %copy-done, f32[2,128,256]{2,1,0:T(8,128)S(1)} %get-tuple-element.64.outer_in), custom_call_target="tpu_custom_call" | custom-call | flops 1000 | bytes 1048576 | tf_op jit(solution)/shard_map/pallas_call | solution.py:356
  25.6 0.0 collective-permute-done.8.halo_ref
  25.6 1.2 %shard_map.68 = bf16[2,4,128,256]{3,2,1,0:T(8,128)(2,1)} custom-call(bf16[2,128,256]{2,1,0:T(8,128)(2,1)S(1)} %collective-permute-done.8.halo_ref, bf16[3,3,256,256]{3,2,1,0:T(8,128)(2,1)S(1)} %copy-done, f32[2,128,256]{2,1,0:T(8,128)S(1)} %shard_map.67.outer_ref, f32[2,128,256]{2,1,0:T(8,128)S(1)} %get-tuple-element.65.inner_ref, ...), custom_call_target="tpu_custom_call" | custom-call | flops 1000 | bytes 1048576 | tf_op jit(solution)/shard_map/pallas_call | solution.py:357
  (4 shorter events, 0.1 us)
Async XLA Ops:
  0.0 4.3 %copy-start.1 = (bf16[3,3,256,256]{3,2,1,0:T(8,128)(2,1)S(1)}, bf16[3,3,256,256]{3,2,1,0:T(8,128)(2,1)}, u32[]{:S(2)}) copy-start(bf16[3,3,256,256]{3,2,1,0:T(8,128)(2,1)} %w_ref.9) | copy-start | bytes 3538948
  0.0 1.1 %copy-start.2 = (bf16[2,4,128,256]{3,2,1,0:T(8,128)(2,1)S(1)}, bf16[2,4,128,256]{3,2,1,0:T(8,128)(2,1)}, u32[]{:S(2)}) copy-start(bf16[2,4,128,256]{3,2,1,0:T(8,128)(2,1)} %x_ref.7) | copy-start | bytes 1572868
  1.1 3.1 %copy-start.4 = (s32[256]{0:T(256)S(1)}, s32[256]{0:T(256)}, u32[]{:S(2)}) copy-start(s32[256]{0:T(256)} %param.9) | copy-start | bytes 3076
  1.1 3.1 %copy-start.5 = (f32[16]{0:T(128)S(1)}, f32[16]{0:T(128)}, u32[]{:S(2)}) copy-start(f32[16]{0:T(128)} %param.8) | copy-start | bytes 196
  1.2 6.1 %collective-permute-start = (bf16[2,128,256]{2,1,0:T(8,128)(2,1)S(1)}, bf16[2,128,256]{2,1,0:T(8,128)(2,1)S(1)}, u32[]{:S(2)}, u32[]{:S(2)}) collective-permute-start(bf16[2,128,256]{2,1,0:T(8,128)(2,1)S(1)} %get-tuple-element.36), channel_id=1, source_target_pairs={{0,1},{1,0},{2,3},{3,2},{4,5},{5,4},{6,7},{7,6},{8,9},{9,8},{10,11... | collective-permute-start | bytes 393224 | tf_op jit(solution)/shard_map/ppermute | solution.py:239
  1.7 5.8 %collective-permute-start.2 = (bf16[2,128,256]{2,1,0:T(8,128)(2,1)S(1)}, bf16[2,128,256]{2,1,0:T(8,128)(2,1)S(1)}, u32[]{:S(2)}, u32[]{:S(2)}) collective-permute-start(bf16[2,128,256]{2,1,0:T(8,128)(2,1)S(1)} %get-tuple-element.41), channel_id=1, source_target_pairs={{0,16},{1,2},{2,1},{3,19},{16,0},{17,18},{18,17},{19,3},{4,20},{5,... | collective-permute-start | bytes 393224 | tf_op jit(solution)/shard_map/ppermute | solution.py:264
  5.6 6.6 %collective-permute-start.4 = (bf16[2,128,256]{2,1,0:T(8,128)(2,1)S(1)}, bf16[2,128,256]{2,1,0:T(8,128)(2,1)S(1)}, u32[]{:S(2)}, u32[]{:S(2)}) collective-permute-start(bf16[2,128,256]{2,1,0:T(8,128)(2,1)S(1)} %get-tuple-element.45.own_ref), channel_id=1, source_target_pairs={{0,4},{4,0},{8,12},{12,8},{1,5},{5,1},{9,13},{13,9},{2,6},{6,2},{1... | collective-permute-start | bytes 393224 | tf_op jit(solution)/shard_map/ppermute | solution.py:239
  7.8 5.5 %collective-permute-start.3 = (bf16[128,256]{1,0:T(8,128)(2,1)S(1)}, bf16[128,256]{1,0:T(8,128)(2,1)S(1)}, u32[]{:S(2)}, u32[]{:S(2)}) collective-permute-start(bf16[128,256]{1,0:T(8,128)(2,1)S(1)} %get-tuple-element.44.own_ref), channel_id=1, source_target_pairs={{0,8},{4,12},{8,0},{12,4},{1,9},{5,13},{9,1},{13,5},{2,10},{6,14},... | collective-permute-start | bytes 196616 | tf_op jit(solution)/shard_map/ppermute | solution.py:239
  10.7 5.0 %collective-permute-start.1 = (bf16[128,256]{1,0:T(8,128)(2,1)S(1)}, bf16[128,256]{1,0:T(8,128)(2,1)S(1)}, u32[]{:S(2)}, u32[]{:S(2)}) collective-permute-start(bf16[128,256]{1,0:T(8,128)(2,1)S(1)} %get-tuple-element.40.own_ref), channel_id=1, source_target_pairs={{0,4},{4,0},{8,12},{12,8},{1,5},{5,1},{9,13},{13,9},{2,6},{6,2},{1... | collective-permute-start | bytes 196616 | tf_op jit(solution)/shard_map/ppermute | solution.py:239
  12.3 6.6 %collective-permute-start.7 = (bf16[2,128,256]{2,1,0:T(8,128)(2,1)S(1)}, bf16[2,128,256]{2,1,0:T(8,128)(2,1)S(1)}, u32[]{:S(2)}, u32[]{:S(2)}) collective-permute-start(bf16[2,128,256]{2,1,0:T(8,128)(2,1)S(1)} %get-tuple-element.52), channel_id=1, source_target_pairs={{0,1},{1,0},{2,3},{3,2},{4,8},{5,9},{6,10},{7,11},{8,4},{9,5},{10,... | collective-permute-start | bytes 393224 | tf_op jit(solution)/shard_map/ppermute | solution.py:251
  13.4 5.7 %collective-permute-start.6 = (bf16[128,256]{1,0:T(8,128)(2,1)S(1)}, bf16[128,256]{1,0:T(8,128)(2,1)S(1)}, u32[]{:S(2)}, u32[]{:S(2)}) collective-permute-start(bf16[128,256]{1,0:T(8,128)(2,1)S(1)} %get-tuple-element.51), channel_id=1, source_target_pairs={{0,4},{4,0},{8,12},{12,8},{1,5},{5,1},{9,13},{13,9},{2,6},{6,2},{1... | collective-permute-start | bytes 196616 | tf_op jit(solution)/shard_map/ppermute | solution.py:239
  15.7 6.6 %copy-start = (bf16[3,3,256,256]{3,2,1,0:T(8,128)(2,1)S(1)}, bf16[3,3,256,256]{3,2,1,0:T(8,128)(2,1)}, u32[]{:S(2)}) copy-start(bf16[3,3,256,256]{3,2,1,0:T(8,128)(2,1)} %w_ref.13) | copy-start | bytes 3538948
  15.7 6.4 %collective-permute-start.5 = (bf16[128,256]{1,0:T(8,128)(2,1)S(1)}, bf16[128,256]{1,0:T(8,128)(2,1)S(1)}, u32[]{:S(2)}, u32[]{:S(2)}) collective-permute-start(bf16[128,256]{1,0:T(8,128)(2,1)S(1)} %get-tuple-element.49), channel_id=1, source_target_pairs={{0,8},{4,12},{8,0},{12,4},{1,9},{5,13},{9,1},{13,5},{2,10},{6,14},... | collective-permute-start | bytes 196616 | tf_op jit(solution)/shard_map/ppermute | solution.py:239
  19.0 5.3 %copy-start.3 = (bf16[2,4,128,256]{3,2,1,0:T(8,128)(2,1)S(1)}, bf16[2,4,128,256]{3,2,1,0:T(8,128)(2,1)}, u32[]{:S(2)}) copy-start(bf16[2,4,128,256]{3,2,1,0:T(8,128)(2,1)} %x_ref.7) | copy-start | bytes 1572868
  19.0 5.3 %collective-permute-start.10 = (bf16[2,128,256]{2,1,0:T(8,128)(2,1)S(1)}, bf16[2,128,256]{2,1,0:T(8,128)(2,1)S(1)}, u32[]{:S(2)}, u32[]{:S(2)}) collective-permute-start(bf16[2,128,256]{2,1,0:T(8,128)(2,1)S(1)} %get-tuple-element.58), channel_id=1, source_target_pairs={{0,4},{4,0},{8,12},{12,8},{1,5},{5,1},{9,13},{13,9},{2,6},{6,2},{1... | collective-permute-start | bytes 393224 | tf_op jit(solution)/shard_map/ppermute | solution.py:239
  19.2 6.1 %collective-permute-start.9 = (bf16[2,128,256]{2,1,0:T(8,128)(2,1)S(1)}, bf16[2,128,256]{2,1,0:T(8,128)(2,1)S(1)}, u32[]{:S(2)}, u32[]{:S(2)}) collective-permute-start(bf16[2,128,256]{2,1,0:T(8,128)(2,1)S(1)} %get-tuple-element.57.outer_in), channel_id=1, source_target_pairs={{0,16},{1,2},{2,1},{3,19},{16,0},{17,18},{18,17},{19,3},{4,20},{5,... | collective-permute-start | bytes 393224 | tf_op jit(solution)/shard_map/ppermute | solution.py:264
  22.2 3.4 %collective-permute-start.8 = (bf16[2,128,256]{2,1,0:T(8,128)(2,1)S(1)}, bf16[2,128,256]{2,1,0:T(8,128)(2,1)S(1)}, u32[]{:S(2)}, u32[]{:S(2)}) collective-permute-start(bf16[2,128,256]{2,1,0:T(8,128)(2,1)S(1)} %get-tuple-element.56.inner_in), channel_id=1, source_target_pairs={{0,1},{1,0},{2,3},{3,2},{4,5},{5,4},{6,7},{7,6},{8,9},{9,8},{10,11... | collective-permute-start | bytes 393224 | tf_op jit(solution)/shard_map/ppermute | solution.py:239

commit v4 on v3

--- a/solution.py
+++ b/solution.py
@@ -311,7 +311,7 @@
         return call(kernel, (row_f32, last_bf16, order), [VMEM] * 4, (VMEM,) * 3, [], SMALL)(halo, weight_in, growth, mixed)
 
     if lax.axis_size("tm") == 4:
-        first = swapped(sent, "tm", 1)
+        first = swapped_between(sent, 0)
         inner, sent_inner, growth = edge(from_inside, halo_inner, inner, growth)
         outer, sent_outer, growth = edge(from_outside, halo_outer, outer, growth)
         far_outer = swapped(sent_outer, "tm", 2)
@@ -323,7 +323,7 @@
         total_inner, growth = call(pair_kernel, (last_bf16, order), [VMEM] * 3, (VMEM,) * 2, [], LONG)(sent_inner, near_inner, growth)
         far_inner = swapped(total_inner, "tm", 2)
         message, growth = call(relay_kernel, (inside_bf16, order), [VMEM] * 3, (VMEM,) * 2, [], SMALL)(sent, second, growth)
-        third = swapped(message, "tm", 1)
+        third = swapped_between(message, 2)
         states_outer, growth = call(far_states_kernel, (row_bf16, order), [VMEM] * 4, (VMEM,) * 2, [], SMALL)(
             outer, far_outer, near_outer, growth
         )

time: 26.9 us -> 26.1 us (0.970); the launches traced: 26.8 us -> 25.6 us
  starting transfers between devices: 16.4 us -> 15.8 us
  waiting for transfers between devices: 3.72 us -> 3.23 us
    ppermute x8 -> x6, starting transfers between devices: 12.2 us -> 9.8 us  [swapped(): lax.ppermute(value, axis, [(i, i ^ distance) for i in range(lax.axis_size...]
    ppermute x1 -> x3, starting transfers between devices: 0.07 us -> 1.78 us  [swapped_between(): return lax.ppermute(value, ('tm', 'rows'), pairs)]
    ppermute x8 -> x6, waiting for transfers between devices: 3.72 us -> 3 us  [swapped(): lax.ppermute(value, axis, [(i, i ^ distance) for i in range(lax.axis_size...]
  transfers between devices with their start and end apart: 11 -> 11, of which waited for: 3 -> 3; matrix products, arithmetic and copies ran while one was open for 0% -> 0% of each run, Pallas kernels for 15% -> 16%
where the time goes in v4:
time: 26.1 us; the launch traced here: 25.6 us
  starting transfers between devices  15.8 us (61%)
  Pallas kernels  5.3 us (20%)
  waiting for transfers between devices  3.23 us (12%)
  local copies, waits for them, and re-layouts  1.16 us (4%)
    ppermute x6, starting transfers between devices, swapped(): lax.ppermute(value, axis, [(i, i ^ distance) for i in range(lax.axis_size...  9.8 us
    ppermute x2, starting transfers between devices, across_chips(): return lax.ppermute(value, ('groups', 'rows'), pairs)  4.18 us
    ppermute x6, waiting for transfers between devices, swapped(): lax.ppermute(value, axis, [(i, i ^ distance) for i in range(lax.axis_size...  3 us
    ppermute x3, starting transfers between devices, swapped_between(): return lax.ppermute(value, ('tm', 'rows'), pairs)  1.78 us
    pallas_call x1, Pallas kernels, local(): call(drive_kernel, (row_f32, middle_f32, row_f32, inside_bf16, order), [V...  1.31 us
    unnamed x12, local copies, waits for them, and re-layouts  1.16 us
    pallas_call x1, Pallas kernels, local(): call(finish_kernel, shaped(latents.shape, BF16), [VMEM] * 6, ANY, [pltpu....  1.15 us
    pallas_call x1, Pallas kernels, local(): call(mix_inside_kernel, (row_f32, shaped((frames,) + inside, BF16), row_f...  1.05 us
  transfers between devices with their start and end apart: 11, of which 3 were waited for; matrix products, arithmetic and copies ran while one was open for 0% of the time, Pallas kernels for 16%

profile of v4, /device:TPU:0, one launch (start us, length us, event | category | flops | bytes accessed | tf_op | source)
XLA Modules:
  0.0 25.6 jit_solution(4811332636829552169)
XLA Ops:
  0.0 0.0 copy-start.1
  0.0 0.0 copy-start.2
  0.0 1.1 %copy-done.2 = bf16[2,4,128,256]{3,2,1,0:T(8,128)(2,1)S(1)} copy-done((bf16[2,4,128,256]{3,2,1,0:T(8,128)(2,1)S(1)}, bf16[2,4,128,256]{3,2,1,0:T(8,128)(2,1)}, u32[]{:S(2)}) %copy-start.2) | copy-done | bytes 524312
  1.1 0.0 copy-start.4
  1.1 0.0 copy-start.5
  1.2 0.5 %collective-permute-start = (bf16[2,128,256]{2,1,0:T(8,128)(2,1)S(1)}, bf16[2,128,256]{2,1,0:T(8,128)(2,1)S(1)}, u32[]{:S(2)}, u32[]{:S(2)}) collective-permute-start(bf16[2,128,256]{2,1,0:T(8,128)(2,1)S(1)} %get-tuple-element.36), channel_id=1, source_target_pairs={{0,1},{1,0},{2,3},{3,2},{4,5},{5,4},{6,7},{7,6},{8,9},{9,8},{10,11... | collective-permute-start | bytes 393224 | tf_op jit(solution)/shard_map/ppermute | solution.py:239
  1.7 2.6 %collective-permute-start.2 = (bf16[2,128,256]{2,1,0:T(8,128)(2,1)S(1)}, bf16[2,128,256]{2,1,0:T(8,128)(2,1)S(1)}, u32[]{:S(2)}, u32[]{:S(2)}) collective-permute-start(bf16[2,128,256]{2,1,0:T(8,128)(2,1)S(1)} %get-tuple-element.41), channel_id=1, source_target_pairs={{0,16},{1,2},{2,1},{3,19},{16,0},{17,18},{18,17},{19,3},{4,20},{5,... | collective-permute-start | bytes 393224 | tf_op jit(solution)/shard_map/ppermute | solution.py:264
  4.3 0.0 copy-done.1
  4.3 0.0 copy-done.4
  4.3 0.0 copy-done.5
  4.3 1.3 %shard_map.56 = (f32[2,128,256]{2,1,0:T(8,128)S(1)}, f32[2,2,128,256]{3,2,1,0:T(8,128)S(1)}, f32[2,128,256]{2,1,0:T(8,128)S(1)}, bf16[2,128,256]{2,1,0:T(8,128)(2,1)S(1)}, f32[2,1,256]{2,1,0:T(1,128)S(1)}) custom-call(bf16[2,4,128,256]{3,2,1,0:T(8,128)(2,1)S(1)} %copy-done.2, bf16[3,3,256,256]{3,2,1,0:T(8,128)(2,1)S(1)} %copy-done.1, f32[1,16]{1,0:T(1,128)S(1)} %bitcast.3, ...), custom_call_target="tpu_custom_call" | custom-call | flops 1000 | bytes 1048576 | tf_op jit(solution)/shard_map/pallas_call | solution.py:300
  5.6 1.6 %collective-permute-start.4 = (bf16[2,128,256]{2,1,0:T(8,128)(2,1)S(1)}, bf16[2,128,256]{2,1,0:T(8,128)(2,1)S(1)}, u32[]{:S(2)}, u32[]{:S(2)}) collective-permute-start(bf16[2,128,256]{2,1,0:T(8,128)(2,1)S(1)} %get-tuple-element.45.own_ref), channel_id=1, source_target_pairs={{0,4},{1,5},{2,6},{3,7},{4,0},{5,1},{6,2},{7,3},{8,9},{9,8},{10,11... | collective-permute-start | bytes 393224 | tf_op jit(solution)/shard_map/ppermute | solution.py:251
  7.2 0.0 collective-permute-done.halo_ref
  7.2 0.3 %shard_map.57 = (f32[2,128,256]{2,1,0:T(8,128)S(1)}, bf16[128,256]{1,0:T(8,128)(2,1)S(1)}, f32[2,1,256]{2,1,0:T(1,128)S(1)}) custom-call(bf16[2,128,256]{2,1,0:T(8,128)(2,1)S(1)} %collective-permute-done.halo_ref, bf16[3,3,256,256]{3,2,1,0:T(8,128)(2,1)S(1)} %copy-done.1, f32[2,1,256]{2,1,0:T(1,128)S(1)} %get-tuple-element.37.growth_ref, ...), custom_call_target="tpu_custom_call" | custom-call | flops 1000 | bytes 1048576 | tf_op jit(solution)/shard_map/pallas_call | solution.py:311
  7.5 0.0 collective-permute-done.2.halo_ref
  7.5 0.3 %shard_map.58 = (f32[2,128,256]{2,1,0:T(8,128)S(1)}, bf16[128,256]{1,0:T(8,128)(2,1)S(1)}, f32[2,1,256]{2,1,0:T(1,128)S(1)}) custom-call(bf16[2,128,256]{2,1,0:T(8,128)(2,1)S(1)} %collective-permute-done.2.halo_ref, bf16[3,3,256,256]{3,2,1,0:T(8,128)(2,1)S(1)} %copy-done.1, f32[2,1,256]{2,1,0:T(1,128)S(1)} %get-tuple-element.42.growth_ref, ...), custom_call_target="tpu_custom_call" | custom-call | flops 1000 | bytes 1048576 | tf_op jit(solution)/shard_map/pallas_call | solution.py:311
  7.8 2.8 %collective-permute-start.3 = (bf16[128,256]{1,0:T(8,128)(2,1)S(1)}, bf16[128,256]{1,0:T(8,128)(2,1)S(1)}, u32[]{:S(2)}, u32[]{:S(2)}) collective-permute-start(bf16[128,256]{1,0:T(8,128)(2,1)S(1)} %get-tuple-element.44.own_ref), channel_id=1, source_target_pairs={{0,8},{4,12},{8,0},{12,4},{1,9},{5,13},{9,1},{13,5},{2,10},{6,14},... | collective-permute-start | bytes 196616 | tf_op jit(solution)/shard_map/ppermute | solution.py:239
  10.7 1.6 %collective-permute-start.1 = (bf16[128,256]{1,0:T(8,128)(2,1)S(1)}, bf16[128,256]{1,0:T(8,128)(2,1)S(1)}, u32[]{:S(2)}, u32[]{:S(2)}) collective-permute-start(bf16[128,256]{1,0:T(8,128)(2,1)S(1)} %get-tuple-element.40.own_ref), channel_id=1, source_target_pairs={{0,4},{4,0},{8,12},{12,8},{1,5},{5,1},{9,13},{13,9},{2,6},{6,2},{1... | collective-permute-start | bytes 196616 | tf_op jit(solution)/shard_map/ppermute | solution.py:239
  12.2 0.0 collective-permute-done.4.other_ref.first_ref
  12.2 0.1 shard_map.59
  12.3 0.1 collective-permute-start.7
  12.4 1.6 %collective-permute-done.3.far_ref = bf16[128,256]{1,0:T(8,128)(2,1)S(1)} collective-permute-done((bf16[128,256]{1,0:T(8,128)(2,1)S(1)}, bf16[128,256]{1,0:T(8,128)(2,1)S(1)}, u32[]{:S(2)}, u32[]{:S(2)}) %collective-permute-start.3) | collective-permute-done | bytes 65568 | tf_op jit(solution)/shard_map/ppermute | solution.py:239
  14.1 1.4 %collective-permute-start.6 = (bf16[128,256]{1,0:T(8,128)(2,1)S(1)}, bf16[128,256]{1,0:T(8,128)(2,1)S(1)}, u32[]{:S(2)}, u32[]{:S(2)}) collective-permute-start(bf16[128,256]{1,0:T(8,128)(2,1)S(1)} %get-tuple-element.51), channel_id=1, source_target_pairs={{0,4},{4,0},{8,12},{12,8},{1,5},{5,1},{9,13},{13,9},{2,6},{6,2},{1... | collective-permute-start | bytes 196616 | tf_op jit(solution)/shard_map/ppermute | solution.py:239
  15.5 0.0 collective-permute-done.1.other_ref.near_ref
  15.5 0.0 copy-start
  15.5 3.4 %collective-permute-start.5 = (bf16[128,256]{1,0:T(8,128)(2,1)S(1)}, bf16[128,256]{1,0:T(8,128)(2,1)S(1)}, u32[]{:S(2)}, u32[]{:S(2)}) collective-permute-start(bf16[128,256]{1,0:T(8,128)(2,1)S(1)} %get-tuple-element.49), channel_id=1, source_target_pairs={{0,8},{4,12},{8,0},{12,4},{1,9},{5,13},{9,1},{13,5},{2,10},{6,14},... | collective-permute-start | bytes 196616 | tf_op jit(solution)/shard_map/ppermute | solution.py:239
  18.9 0.0 collective-permute-done.7.before_ref.second_ref
  19.0 0.0 copy-start.3
  19.0 0.1 collective-permute-start.10
  19.1 0.0 collective-permute-done.6.near_ref
  19.1 0.1 shard_map.63
  19.1 1.6 %collective-permute-start.9 = (bf16[2,128,256]{2,1,0:T(8,128)(2,1)S(1)}, bf16[2,128,256]{2,1,0:T(8,128)(2,1)S(1)}, u32[]{:S(2)}, u32[]{:S(2)}) collective-permute-start(bf16[2,128,256]{2,1,0:T(8,128)(2,1)S(1)} %get-tuple-element.57.outer_in), channel_id=1, source_target_pairs={{0,16},{1,2},{2,1},{3,19},{16,0},{17,18},{18,17},{19,3},{4,20},{5,... | collective-permute-start | bytes 393224 | tf_op jit(solution)/shard_map/ppermute | solution.py:264
  20.7 1.4 %collective-permute-done.5.far_ref = bf16[128,256]{1,0:T(8,128)(2,1)S(1)} collective-permute-done((bf16[128,256]{1,0:T(8,128)(2,1)S(1)}, bf16[128,256]{1,0:T(8,128)(2,1)S(1)}, u32[]{:S(2)}, u32[]{:S(2)}) %collective-permute-start.5) | collective-permute-done | bytes 65568 | tf_op jit(solution)/shard_map/ppermute | solution.py:239
  22.1 0.1 shard_map.64
  22.2 0.1 collective-permute-start.8
  22.3 0.0 copy-done
  22.3 0.6 %shard_map.65 = (f32[2,128,256]{2,1,0:T(8,128)S(1)}, f32[2,2,128,256]{3,2,1,0:T(8,128)S(1)}, f32[2,128,256]{2,1,0:T(8,128)S(1)}) custom-call(bf16[2,128,256]{2,1,0:T(8,128)(2,1)S(1)} %get-tuple-element.57.outer_in, bf16[2,128,256]{2,1,0:T(8,128)(2,1)S(1)} %get-tuple-element.56.inner_in, bf16[3,3,256,256]{3,2,1,0:T(8,128)(2,1)S(1)} %copy-done), custom_call_target="tpu_custom_call" | custom-call | flops 1000 | bytes 1048576 | tf_op jit(solution)/shard_map/pallas_call | solution.py:345
  22.9 0.0 collective-permute-done.10.third_ref
  22.9 0.0 copy-done.3
  22.9 1.1 %shard_map.66 = (f32[2,128,256]{2,1,0:T(8,128)S(1)}, bf16[2,2,128,256]{3,2,1,0:T(8,128)(2,1)S(1)}, f32[2,128,256]{2,1,0:T(8,128)S(1)}) custom-call(bf16[2,128,256]{2,1,0:T(8,128)(2,1)S(1)} %collective-permute-done.4.other_ref.first_ref, bf16[2,128,256]{2,1,0:T(8,128)(2,1)S(1)} %collective-permute-done.7.before_ref.second_ref, ...), custom_call_target="tpu_custom_call" | custom-call | flops 1000 | bytes 1048576 | tf_op jit(solution)/shard_map/pallas_call | solution.py:348
  24.0 0.2 collective-permute-done.9.halo_ref
  24.2 0.3 %shard_map.67.outer_ref = f32[2,128,256]{2,1,0:T(8,128)S(1)} custom-call(bf16[2,128,256]{2,1,0:T(8,128)(2,1)S(1)} %collective-permute-done.9.halo_ref, bf16[3,3,256,256]{3,2,1,0:T(8,128)(2,1)S(1)} %copy-done, f32[2,128,256]{2,1,0:T(8,128)S(1)} %get-tuple-element.64.outer_in), custom_call_target="tpu_custom_call" | custom-call | flops 1000 | bytes 1048576 | tf_op jit(solution)/shard_map/pallas_call | solution.py:356
  24.5 0.0 collective-permute-done.8.halo_ref
  24.5 1.2 %shard_map.68 = bf16[2,4,128,256]{3,2,1,0:T(8,128)(2,1)} custom-call(bf16[2,128,256]{2,1,0:T(8,128)(2,1)S(1)} %collective-permute-done.8.halo_ref, bf16[3,3,256,256]{3,2,1,0:T(8,128)(2,1)S(1)} %copy-done, f32[2,128,256]{2,1,0:T(8,128)S(1)} %shard_map.67.outer_ref, f32[2,128,256]{2,1,0:T(8,128)S(1)} %get-tuple-element.65.inner_ref, ...), custom_call_target="tpu_custom_call" | custom-call | flops 1000 | bytes 1048576 | tf_op jit(solution)/shard_map/pallas_call | solution.py:357
  (4 shorter events, 0.1 us)
Async XLA Ops:
  0.0 4.3 %copy-start.1 = (bf16[3,3,256,256]{3,2,1,0:T(8,128)(2,1)S(1)}, bf16[3,3,256,256]{3,2,1,0:T(8,128)(2,1)}, u32[]{:S(2)}) copy-start(bf16[3,3,256,256]{3,2,1,0:T(8,128)(2,1)} %w_ref.9) | copy-start | bytes 3538948
  0.0 1.1 %copy-start.2 = (bf16[2,4,128,256]{3,2,1,0:T(8,128)(2,1)S(1)}, bf16[2,4,128,256]{3,2,1,0:T(8,128)(2,1)}, u32[]{:S(2)}) copy-start(bf16[2,4,128,256]{3,2,1,0:T(8,128)(2,1)} %x_ref.7) | copy-start | bytes 1572868
  1.1 3.1 %copy-start.4 = (s32[256]{0:T(256)S(1)}, s32[256]{0:T(256)}, u32[]{:S(2)}) copy-start(s32[256]{0:T(256)} %param.9) | copy-start | bytes 3076
  1.1 3.1 %copy-start.5 = (f32[16]{0:T(128)S(1)}, f32[16]{0:T(128)}, u32[]{:S(2)}) copy-start(f32[16]{0:T(128)} %param.8) | copy-start | bytes 196
  1.2 6.1 %collective-permute-start = (bf16[2,128,256]{2,1,0:T(8,128)(2,1)S(1)}, bf16[2,128,256]{2,1,0:T(8,128)(2,1)S(1)}, u32[]{:S(2)}, u32[]{:S(2)}) collective-permute-start(bf16[2,128,256]{2,1,0:T(8,128)(2,1)S(1)} %get-tuple-element.36), channel_id=1, source_target_pairs={{0,1},{1,0},{2,3},{3,2},{4,5},{5,4},{6,7},{7,6},{8,9},{9,8},{10,11... | collective-permute-start | bytes 393224 | tf_op jit(solution)/shard_map/ppermute | solution.py:239
  1.7 5.8 %collective-permute-start.2 = (bf16[2,128,256]{2,1,0:T(8,128)(2,1)S(1)}, bf16[2,128,256]{2,1,0:T(8,128)(2,1)S(1)}, u32[]{:S(2)}, u32[]{:S(2)}) collective-permute-start(bf16[2,128,256]{2,1,0:T(8,128)(2,1)S(1)} %get-tuple-element.41), channel_id=1, source_target_pairs={{0,16},{1,2},{2,1},{3,19},{16,0},{17,18},{18,17},{19,3},{4,20},{5,... | collective-permute-start | bytes 393224 | tf_op jit(solution)/shard_map/ppermute | solution.py:264
  5.6 6.6 %collective-permute-start.4 = (bf16[2,128,256]{2,1,0:T(8,128)(2,1)S(1)}, bf16[2,128,256]{2,1,0:T(8,128)(2,1)S(1)}, u32[]{:S(2)}, u32[]{:S(2)}) collective-permute-start(bf16[2,128,256]{2,1,0:T(8,128)(2,1)S(1)} %get-tuple-element.45.own_ref), channel_id=1, source_target_pairs={{0,4},{1,5},{2,6},{3,7},{4,0},{5,1},{6,2},{7,3},{8,9},{9,8},{10,11... | collective-permute-start | bytes 393224 | tf_op jit(solution)/shard_map/ppermute | solution.py:251
  7.8 6.2 %collective-permute-start.3 = (bf16[128,256]{1,0:T(8,128)(2,1)S(1)}, bf16[128,256]{1,0:T(8,128)(2,1)S(1)}, u32[]{:S(2)}, u32[]{:S(2)}) collective-permute-start(bf16[128,256]{1,0:T(8,128)(2,1)S(1)} %get-tuple-element.44.own_ref), channel_id=1, source_target_pairs={{0,8},{4,12},{8,0},{12,4},{1,9},{5,13},{9,1},{13,5},{2,10},{6,14},... | collective-permute-start | bytes 196616 | tf_op jit(solution)/shard_map/ppermute | solution.py:239
  10.7 4.8 %collective-permute-start.1 = (bf16[128,256]{1,0:T(8,128)(2,1)S(1)}, bf16[128,256]{1,0:T(8,128)(2,1)S(1)}, u32[]{:S(2)}, u32[]{:S(2)}) collective-permute-start(bf16[128,256]{1,0:T(8,128)(2,1)S(1)} %get-tuple-element.40.own_ref), channel_id=1, source_target_pairs={{0,4},{4,0},{8,12},{12,8},{1,5},{5,1},{9,13},{13,9},{2,6},{6,2},{1... | collective-permute-start | bytes 196616 | tf_op jit(solution)/shard_map/ppermute | solution.py:239
  12.3 6.6 %collective-permute-start.7 = (bf16[2,128,256]{2,1,0:T(8,128)(2,1)S(1)}, bf16[2,128,256]{2,1,0:T(8,128)(2,1)S(1)}, u32[]{:S(2)}, u32[]{:S(2)}) collective-permute-start(bf16[2,128,256]{2,1,0:T(8,128)(2,1)S(1)} %get-tuple-element.52), channel_id=1, source_target_pairs={{0,1},{1,0},{2,3},{3,2},{4,8},{5,9},{6,10},{7,11},{8,4},{9,5},{10,... | collective-permute-start | bytes 393224 | tf_op jit(solution)/shard_map/ppermute | solution.py:251
  14.1 5.0 %collective-permute-start.6 = (bf16[128,256]{1,0:T(8,128)(2,1)S(1)}, bf16[128,256]{1,0:T(8,128)(2,1)S(1)}, u32[]{:S(2)}, u32[]{:S(2)}) collective-permute-start(bf16[128,256]{1,0:T(8,128)(2,1)S(1)} %get-tuple-element.51), channel_id=1, source_target_pairs={{0,4},{4,0},{8,12},{12,8},{1,5},{5,1},{9,13},{13,9},{2,6},{6,2},{1... | collective-permute-start | bytes 196616 | tf_op jit(solution)/shard_map/ppermute | solution.py:239
  15.5 6.8 %copy-start = (bf16[3,3,256,256]{3,2,1,0:T(8,128)(2,1)S(1)}, bf16[3,3,256,256]{3,2,1,0:T(8,128)(2,1)}, u32[]{:S(2)}) copy-start(bf16[3,3,256,256]{3,2,1,0:T(8,128)(2,1)} %w_ref.13) | copy-start | bytes 3538948
  15.5 6.6 %collective-permute-start.5 = (bf16[128,256]{1,0:T(8,128)(2,1)S(1)}, bf16[128,256]{1,0:T(8,128)(2,1)S(1)}, u32[]{:S(2)}, u32[]{:S(2)}) collective-permute-start(bf16[128,256]{1,0:T(8,128)(2,1)S(1)} %get-tuple-element.49), channel_id=1, source_target_pairs={{0,8},{4,12},{8,0},{12,4},{1,9},{5,13},{9,1},{13,5},{2,10},{6,14},... | collective-permute-start | bytes 196616 | tf_op jit(solution)/shard_map/ppermute | solution.py:239
  19.0 3.9 %copy-start.3 = (bf16[2,4,128,256]{3,2,1,0:T(8,128)(2,1)S(1)}, bf16[2,4,128,256]{3,2,1,0:T(8,128)(2,1)}, u32[]{:S(2)}) copy-start(bf16[2,4,128,256]{3,2,1,0:T(8,128)(2,1)} %x_ref.7) | copy-start | bytes 1572868
  19.0 3.9 %collective-permute-start.10 = (bf16[2,128,256]{2,1,0:T(8,128)(2,1)S(1)}, bf16[2,128,256]{2,1,0:T(8,128)(2,1)S(1)}, u32[]{:S(2)}, u32[]{:S(2)}) collective-permute-start(bf16[2,128,256]{2,1,0:T(8,128)(2,1)S(1)} %get-tuple-element.58), channel_id=1, source_target_pairs={{0,1},{1,0},{2,3},{3,2},{4,5},{5,4},{6,7},{7,6},{8,12},{9,13},{10,... | collective-permute-start | bytes 393224 | tf_op jit(solution)/shard_map/ppermute | solution.py:251
  19.1 5.0 %collective-permute-start.9 = (bf16[2,128,256]{2,1,0:T(8,128)(2,1)S(1)}, bf16[2,128,256]{2,1,0:T(8,128)(2,1)S(1)}, u32[]{:S(2)}, u32[]{:S(2)}) collective-permute-start(bf16[2,128,256]{2,1,0:T(8,128)(2,1)S(1)} %get-tuple-element.57.outer_in), channel_id=1, source_target_pairs={{0,16},{1,2},{2,1},{3,19},{16,0},{17,18},{18,17},{19,3},{4,20},{5,... | collective-permute-start | bytes 393224 | tf_op jit(solution)/shard_map/ppermute | solution.py:264
  22.2 2.3 %collective-permute-start.8 = (bf16[2,128,256]{2,1,0:T(8,128)(2,1)S(1)}, bf16[2,128,256]{2,1,0:T(8,128)(2,1)S(1)}, u32[]{:S(2)}, u32[]{:S(2)}) collective-permute-start(bf16[2,128,256]{2,1,0:T(8,128)(2,1)S(1)} %get-tuple-element.56.inner_in), channel_id=1, source_target_pairs={{0,1},{1,0},{2,3},{3,2},{4,5},{5,4},{6,7},{7,6},{8,9},{9,8},{10,11... | collective-permute-start | bytes 393224 | tf_op jit(solution)/shard_map/ppermute | solution.py:239

commit v5 on v4

--- a/solution.py
+++ b/solution.py
@@ -119,6 +119,14 @@
     for f in range(frames):
         states_ref[f] = (row_ref[f] + growth_ref[f] * carried).astype(BF16)
     order_ref[...] = growth_ref[...]
+
+
+def by_hop(first_ref, second_ref, third_ref):
+    mine = lax.axis_index("tm")
+    carried = third_ref[...].astype(F32)
+    for hop, ref in enumerate((first_ref, second_ref)):
+        carried = jnp.where(mine == hop + 1, ref[...].astype(F32), carried)
+    return jnp.where(mine == 0, 0.0, carried)
 
 
 def far_relay_kernel(own_ref, far_ref, growth_ref, message_ref, order_ref):
@@ -312,25 +320,21 @@
 
     if lax.axis_size("tm") == 4:
         first = swapped_between(sent, 0)
+        outer, sent_outer, growth = edge(from_outside, halo_outer, outer, growth)
         inner, sent_inner, growth = edge(from_inside, halo_inner, inner, growth)
-        outer, sent_outer, growth = edge(from_outside, halo_outer, outer, growth)
         far_outer = swapped(sent_outer, "tm", 2)
         near_inner = swapped(sent_inner, "tm", 1)
-        total, growth = call(pair_kernel, (inside_bf16, order), [VMEM] * 3, (VMEM,) * 2, [], SMALL)(sent, first, growth)
+        total, growth = call(relay_kernel, (inside_bf16, order), [VMEM] * 3, (VMEM,) * 2, [], SMALL)(sent, first, growth)
         second = swapped_between(total, 1)
-        relayed, growth = call(far_relay_kernel, (last_bf16, order), [VMEM] * 3, (VMEM,) * 2, [], SMALL)(sent_outer, far_outer, growth)
-        near_outer = swapped(relayed, "tm", 1)
+        relayed_outer, growth = call(far_relay_kernel, (last_bf16, order), [VMEM] * 3, (VMEM,) * 2, [], LONG)(sent_outer, far_outer, growth)
+        near_outer = swapped(relayed_outer, "tm", 1)
         total_inner, growth = call(pair_kernel, (last_bf16, order), [VMEM] * 3, (VMEM,) * 2, [], LONG)(sent_inner, near_inner, growth)
         far_inner = swapped(total_inner, "tm", 2)
         message, growth = call(relay_kernel, (inside_bf16, order), [VMEM] * 3, (VMEM,) * 2, [], SMALL)(sent, second, growth)
         third = swapped_between(message, 2)
-        states_outer, growth = call(far_states_kernel, (row_bf16, order), [VMEM] * 4, (VMEM,) * 2, [], SMALL)(
-            outer, far_outer, near_outer, growth
-        )
+        states_outer, growth = call(far_states_kernel, (row_bf16, order), [VMEM] * 4, (VMEM,) * 2, [], SMALL)(outer, far_outer, near_outer, growth)
         halo_outer = across_chips(states_outer)
-        states_inner, growth = call(edge_states_kernel, (row_bf16, order), [VMEM] * 4, (VMEM,) * 2, [], SMALL)(
-            inner, near_inner, far_inner, growth
-        )
+        states_inner, growth = call(edge_states_kernel, (row_bf16, order), [VMEM] * 4, (VMEM,) * 2, [], SMALL)(inner, near_inner, far_inner, growth)
         halo_inner = swapped(states_inner, "rows", 1)
     else:
         inner, sent_inner, growth = edge(from_inside, halo_inner, inner, growth)

time: 26.1 us -> 25.7 us (0.985); the launches traced: 25.6 us -> 25.6 us
  starting transfers between devices: 15.8 us -> 16.6 us
  waiting for transfers between devices: 3.23 us -> 2.44 us
    ppermute x6, waiting for transfers between devices: 3 us -> 1.26 us  [swapped(): lax.ppermute(value, axis, [(i, i ^ distance) for i in range(lax.axis_size...]
    ppermute x2, waiting for transfers between devices: 0.22 us -> 1.17 us  [across_chips(): return lax.ppermute(value, ('groups', 'rows'), pairs)]
    ppermute x2, starting transfers between devices: 4.18 us -> 4.72 us  [across_chips(): return lax.ppermute(value, ('groups', 'rows'), pairs)]
    ppermute x6, starting transfers between devices: 9.8 us -> 10.1 us  [swapped(): lax.ppermute(value, axis, [(i, i ^ distance) for i in range(lax.axis_size...]
where the time goes in v5:
time: 25.7 us; the launch traced here: 25.6 us
  starting transfers between devices  16.6 us (65%)
  Pallas kernels  5.24 us (20%)
  waiting for transfers between devices  2.44 us (9%)
  local copies, waits for them, and re-layouts  1.16 us (5%)
    ppermute x6, starting transfers between devices, swapped(): lax.ppermute(value, axis, [(i, i ^ distance) for i in range(lax.axis_size...  10.1 us
    ppermute x2, starting transfers between devices, across_chips(): return lax.ppermute(value, ('groups', 'rows'), pairs)  4.72 us
    ppermute x3, starting transfers between devices, swapped_between(): return lax.ppermute(value, ('tm', 'rows'), pairs)  1.78 us
    pallas_call x1, Pallas kernels, local(): call(drive_kernel, (row_f32, middle_f32, row_f32, inside_bf16, order), [V...  1.31 us
    ppermute x6, waiting for transfers between devices, swapped(): lax.ppermute(value, axis, [(i, i ^ distance) for i in range(lax.axis_size...  1.26 us
    ppermute x2, waiting for transfers between devices, across_chips(): return lax.ppermute(value, ('groups', 'rows'), pairs)  1.17 us
    unnamed x12, local copies, waits for them, and re-layouts  1.16 us
    pallas_call x1, Pallas kernels, local(): call(finish_kernel, shaped(latents.shape, BF16), [VMEM] * 6, ANY, [pltpu....  1.15 us
  transfers between devices with their start and end apart: 11, of which 3 were waited for; matrix products, arithmetic and copies ran while one was open for 0% of the time, Pallas kernels for 16%

profile of v5, /device:TPU:0, one launch (start us, length us, event | category | flops | bytes accessed | tf_op | source)
XLA Modules:
  0.0 25.6 jit_solution(6938778096894780721)
XLA Ops:
  0.0 0.0 copy-start.1
  0.0 0.0 copy-start.2
  0.0 1.1 %copy-done.2 = bf16[2,4,128,256]{3,2,1,0:T(8,128)(2,1)S(1)} copy-done((bf16[2,4,128,256]{3,2,1,0:T(8,128)(2,1)S(1)}, bf16[2,4,128,256]{3,2,1,0:T(8,128)(2,1)}, u32[]{:S(2)}) %copy-start.2) | copy-done | bytes 524312
  1.1 0.0 copy-start.4
  1.1 0.0 copy-start.5
  1.2 3.0 %collective-permute-start.1 = (bf16[2,128,256]{2,1,0:T(8,128)(2,1)S(1)}, bf16[2,128,256]{2,1,0:T(8,128)(2,1)S(1)}, u32[]{:S(2)}, u32[]{:S(2)}) collective-permute-start(bf16[2,128,256]{2,1,0:T(8,128)(2,1)S(1)} %get-tuple-element.37), channel_id=1, source_target_pairs={{0,16},{1,2},{2,1},{3,19},{16,0},{17,18},{18,17},{19,3},{4,20},{5,... | collective-permute-start | bytes 393224 | tf_op jit(solution)/shard_map/ppermute | solution.py:272
  4.2 0.1 collective-permute-start
  4.3 0.0 copy-done.1
  4.3 0.0 copy-done.4
  4.3 0.0 copy-done.5
  4.3 1.3 %shard_map.56 = (f32[2,128,256]{2,1,0:T(8,128)S(1)}, f32[2,2,128,256]{3,2,1,0:T(8,128)S(1)}, f32[2,128,256]{2,1,0:T(8,128)S(1)}, bf16[2,128,256]{2,1,0:T(8,128)(2,1)S(1)}, f32[2,1,256]{2,1,0:T(1,128)S(1)}) custom-call(bf16[2,4,128,256]{3,2,1,0:T(8,128)(2,1)S(1)} %copy-done.2, bf16[3,3,256,256]{3,2,1,0:T(8,128)(2,1)S(1)} %copy-done.1, f32[1,16]{1,0:T(1,128)S(1)} %bitcast.3, ...), custom_call_target="tpu_custom_call" | custom-call | flops 1000 | bytes 1048576 | tf_op jit(solution)/shard_map/pallas_call | solution.py:308
  5.6 1.6 %collective-permute-start.4 = (bf16[2,128,256]{2,1,0:T(8,128)(2,1)S(1)}, bf16[2,128,256]{2,1,0:T(8,128)(2,1)S(1)}, u32[]{:S(2)}, u32[]{:S(2)}) collective-permute-start(bf16[2,128,256]{2,1,0:T(8,128)(2,1)S(1)} %get-tuple-element.45.own_ref), channel_id=1, source_target_pairs={{0,4},{1,5},{2,6},{3,7},{4,0},{5,1},{6,2},{7,3},{8,9},{9,8},{10,11... | collective-permute-start | bytes 393224 | tf_op jit(solution)/shard_map/ppermute | solution.py:259
  7.2 0.0 collective-permute-done.1.halo_ref
  7.3 0.3 %shard_map.57 = (f32[2,128,256]{2,1,0:T(8,128)S(1)}, bf16[128,256]{1,0:T(8,128)(2,1)S(1)}, f32[2,1,256]{2,1,0:T(1,128)S(1)}) custom-call(bf16[2,128,256]{2,1,0:T(8,128)(2,1)S(1)} %collective-permute-done.1.halo_ref, bf16[3,3,256,256]{3,2,1,0:T(8,128)(2,1)S(1)} %copy-done.1, f32[2,1,256]{2,1,0:T(1,128)S(1)} %get-tuple-element.38.growth_ref, ...), custom_call_target="tpu_custom_call" | custom-call | flops 1000 | bytes 1048576 | tf_op jit(solution)/shard_map/pallas_call | solution.py:319
  7.5 3.0 %collective-permute-start.3 = (bf16[128,256]{1,0:T(8,128)(2,1)S(1)}, bf16[128,256]{1,0:T(8,128)(2,1)S(1)}, u32[]{:S(2)}, u32[]{:S(2)}) collective-permute-start(bf16[128,256]{1,0:T(8,128)(2,1)S(1)} %get-tuple-element.44.own_ref), channel_id=1, source_target_pairs={{0,8},{4,12},{8,0},{12,4},{1,9},{5,13},{9,1},{13,5},{2,10},{6,14},... | collective-permute-start | bytes 196616 | tf_op jit(solution)/shard_map/ppermute | solution.py:247
  10.6 0.0 collective-permute-done.halo_ref
  10.6 0.3 %shard_map.58 = (f32[2,128,256]{2,1,0:T(8,128)S(1)}, bf16[128,256]{1,0:T(8,128)(2,1)S(1)}, f32[2,1,256]{2,1,0:T(1,128)S(1)}) custom-call(bf16[2,128,256]{2,1,0:T(8,128)(2,1)S(1)} %collective-permute-done.halo_ref, bf16[3,3,256,256]{3,2,1,0:T(8,128)(2,1)S(1)} %copy-done.1, f32[2,1,256]{2,1,0:T(1,128)S(1)} %get-tuple-element.40.growth_ref, ...), custom_call_target="tpu_custom_call" | custom-call | flops 1000 | bytes 1048576 | tf_op jit(solution)/shard_map/pallas_call | solution.py:319
  10.9 1.6 %collective-permute-start.2 = (bf16[128,256]{1,0:T(8,128)(2,1)S(1)}, bf16[128,256]{1,0:T(8,128)(2,1)S(1)}, u32[]{:S(2)}, u32[]{:S(2)}) collective-permute-start(bf16[128,256]{1,0:T(8,128)(2,1)S(1)} %get-tuple-element.43.own_ref), channel_id=1, source_target_pairs={{0,4},{4,0},{8,12},{12,8},{1,5},{5,1},{9,13},{13,9},{2,6},{6,2},{1... | collective-permute-start | bytes 196616 | tf_op jit(solution)/shard_map/ppermute | solution.py:247
  12.5 0.0 collective-permute-done.4.before_ref.first_ref
  12.6 0.1 collective-permute-start.7
  12.6 0.9 %collective-permute-done.3.far_ref = bf16[128,256]{1,0:T(8,128)(2,1)S(1)} collective-permute-done((bf16[128,256]{1,0:T(8,128)(2,1)S(1)}, bf16[128,256]{1,0:T(8,128)(2,1)S(1)}, u32[]{:S(2)}, u32[]{:S(2)}) %collective-permute-start.3) | collective-permute-done | bytes 65568 | tf_op jit(solution)/shard_map/ppermute | solution.py:247
  13.6 1.8 %collective-permute-start.6 = (bf16[128,256]{1,0:T(8,128)(2,1)S(1)}, bf16[128,256]{1,0:T(8,128)(2,1)S(1)}, u32[]{:S(2)}, u32[]{:S(2)}) collective-permute-start(bf16[128,256]{1,0:T(8,128)(2,1)S(1)} %get-tuple-element.51), channel_id=1, source_target_pairs={{0,4},{4,0},{8,12},{12,8},{1,5},{5,1},{9,13},{13,9},{2,6},{6,2},{1... | collective-permute-start | bytes 196616 | tf_op jit(solution)/shard_map/ppermute | solution.py:247
  15.4 0.0 collective-permute-done.2.other_ref.near_ref
  15.4 0.0 copy-start
  15.4 3.5 %collective-permute-start.5 = (bf16[128,256]{1,0:T(8,128)(2,1)S(1)}, bf16[128,256]{1,0:T(8,128)(2,1)S(1)}, u32[]{:S(2)}, u32[]{:S(2)}) collective-permute-start(bf16[128,256]{1,0:T(8,128)(2,1)S(1)} %get-tuple-element.49), channel_id=1, source_target_pairs={{0,8},{4,12},{8,0},{12,4},{1,9},{5,13},{9,1},{13,5},{2,10},{6,14},... | collective-permute-start | bytes 196616 | tf_op jit(solution)/shard_map/ppermute | solution.py:247
  18.9 0.0 collective-permute-done.7.before_ref.second_ref
  18.9 0.0 copy-start.3
  19.0 0.1 collective-permute-start.10
  19.0 0.0 collective-permute-done.6.near_ref
  19.0 0.1 shard_map.63
  19.1 1.7 %collective-permute-start.9 = (bf16[2,128,256]{2,1,0:T(8,128)(2,1)S(1)}, bf16[2,128,256]{2,1,0:T(8,128)(2,1)S(1)}, u32[]{:S(2)}, u32[]{:S(2)}) collective-permute-start(bf16[2,128,256]{2,1,0:T(8,128)(2,1)S(1)} %get-tuple-element.57.outer_in), channel_id=1, source_target_pairs={{0,16},{1,2},{2,1},{3,19},{16,0},{17,18},{18,17},{19,3},{4,20},{5,... | collective-permute-start | bytes 393224 | tf_op jit(solution)/shard_map/ppermute | solution.py:272
  20.8 0.3 %collective-permute-done.5.far_ref = bf16[128,256]{1,0:T(8,128)(2,1)S(1)} collective-permute-done((bf16[128,256]{1,0:T(8,128)(2,1)S(1)}, bf16[128,256]{1,0:T(8,128)(2,1)S(1)}, u32[]{:S(2)}, u32[]{:S(2)}) %collective-permute-start.5) | collective-permute-done | bytes 65568 | tf_op jit(solution)/shard_map/ppermute | solution.py:247
  21.1 0.1 shard_map.64
  21.2 0.1 collective-permute-start.8
  21.3 0.0 copy-done
  21.3 0.6 %shard_map.65 = (f32[2,128,256]{2,1,0:T(8,128)S(1)}, f32[2,2,128,256]{3,2,1,0:T(8,128)S(1)}, f32[2,128,256]{2,1,0:T(8,128)S(1)}) custom-call(bf16[2,128,256]{2,1,0:T(8,128)(2,1)S(1)} %get-tuple-element.57.outer_in, bf16[2,128,256]{2,1,0:T(8,128)(2,1)S(1)} %get-tuple-element.56.inner_in, bf16[3,3,256,256]{3,2,1,0:T(8,128)(2,1)S(1)} %copy-done), custom_call_target="tpu_custom_call" | custom-call | flops 1000 | bytes 1048576 | tf_op jit(solution)/shard_map/pallas_call | solution.py:349
  21.9 0.0 collective-permute-done.10.third_ref
  21.9 0.0 copy-done.3
  21.9 1.1 %shard_map.66 = (f32[2,128,256]{2,1,0:T(8,128)S(1)}, bf16[2,2,128,256]{3,2,1,0:T(8,128)(2,1)S(1)}, f32[2,128,256]{2,1,0:T(8,128)S(1)}) custom-call(bf16[2,128,256]{2,1,0:T(8,128)(2,1)S(1)} %collective-permute-done.4.before_ref.first_ref, bf16[2,128,256]{2,1,0:T(8,128)(2,1)S(1)} %collective-permute-done.7.before_ref.second_ref, ...), custom_call_target="tpu_custom_call" | custom-call | flops 1000 | bytes 1048576 | tf_op jit(solution)/shard_map/pallas_call | solution.py:352
  23.0 1.2 %collective-permute-done.9.halo_ref = bf16[2,128,256]{2,1,0:T(8,128)(2,1)S(1)} collective-permute-done((bf16[2,128,256]{2,1,0:T(8,128)(2,1)S(1)}, bf16[2,128,256]{2,1,0:T(8,128)(2,1)S(1)}, u32[]{:S(2)}, u32[]{:S(2)}) %collective-permute-start.9) | collective-permute-done | bytes 131104 | tf_op jit(solution)/shard_map/ppermute | solution.py:272
  24.1 0.3 %shard_map.67.outer_ref = f32[2,128,256]{2,1,0:T(8,128)S(1)} custom-call(bf16[2,128,256]{2,1,0:T(8,128)(2,1)S(1)} %collective-permute-done.9.halo_ref, bf16[3,3,256,256]{3,2,1,0:T(8,128)(2,1)S(1)} %copy-done, f32[2,128,256]{2,1,0:T(8,128)S(1)} %get-tuple-element.64.outer_in), custom_call_target="tpu_custom_call" | custom-call | flops 1000 | bytes 1048576 | tf_op jit(solution)/shard_map/pallas_call | solution.py:360
  24.4 0.0 collective-permute-done.8.halo_ref
  24.4 1.2 %shard_map.68 = bf16[2,4,128,256]{3,2,1,0:T(8,128)(2,1)} custom-call(bf16[2,128,256]{2,1,0:T(8,128)(2,1)S(1)} %collective-permute-done.8.halo_ref, bf16[3,3,256,256]{3,2,1,0:T(8,128)(2,1)S(1)} %copy-done, f32[2,128,256]{2,1,0:T(8,128)S(1)} %shard_map.67.outer_ref, f32[2,128,256]{2,1,0:T(8,128)S(1)} %get-tuple-element.65.inner_ref, ...), custom_call_target="tpu_custom_call" | custom-call | flops 1000 | bytes 1048576 | tf_op jit(solution)/shard_map/pallas_call | solution.py:361
  (5 shorter events, 0.2 us)
Async XLA Ops:
  0.0 4.3 %copy-start.1 = (bf16[3,3,256,256]{3,2,1,0:T(8,128)(2,1)S(1)}, bf16[3,3,256,256]{3,2,1,0:T(8,128)(2,1)}, u32[]{:S(2)}) copy-start(bf16[3,3,256,256]{3,2,1,0:T(8,128)(2,1)} %w_ref.9) | copy-start | bytes 3538948
  0.0 1.1 %copy-start.2 = (bf16[2,4,128,256]{3,2,1,0:T(8,128)(2,1)S(1)}, bf16[2,4,128,256]{3,2,1,0:T(8,128)(2,1)}, u32[]{:S(2)}) copy-start(bf16[2,4,128,256]{3,2,1,0:T(8,128)(2,1)} %x_ref.7) | copy-start | bytes 1572868
  1.1 3.1 %copy-start.4 = (s32[256]{0:T(256)S(1)}, s32[256]{0:T(256)}, u32[]{:S(2)}) copy-start(s32[256]{0:T(256)} %param.9) | copy-start | bytes 3076
  1.1 3.2 %copy-start.5 = (f32[16]{0:T(128)S(1)}, f32[16]{0:T(128)}, u32[]{:S(2)}) copy-start(f32[16]{0:T(128)} %param.8) | copy-start | bytes 196
  1.2 6.1 %collective-permute-start.1 = (bf16[2,128,256]{2,1,0:T(8,128)(2,1)S(1)}, bf16[2,128,256]{2,1,0:T(8,128)(2,1)S(1)}, u32[]{:S(2)}, u32[]{:S(2)}) collective-permute-start(bf16[2,128,256]{2,1,0:T(8,128)(2,1)S(1)} %get-tuple-element.37), channel_id=1, source_target_pairs={{0,16},{1,2},{2,1},{3,19},{16,0},{17,18},{18,17},{19,3},{4,20},{5,... | collective-permute-start | bytes 393224 | tf_op jit(solution)/shard_map/ppermute | solution.py:272
  4.2 6.4 %collective-permute-start = (bf16[2,128,256]{2,1,0:T(8,128)(2,1)S(1)}, bf16[2,128,256]{2,1,0:T(8,128)(2,1)S(1)}, u32[]{:S(2)}, u32[]{:S(2)}) collective-permute-start(bf16[2,128,256]{2,1,0:T(8,128)(2,1)S(1)} %get-tuple-element.36), channel_id=1, source_target_pairs={{0,1},{1,0},{2,3},{3,2},{4,5},{5,4},{6,7},{7,6},{8,9},{9,8},{10,11... | collective-permute-start | bytes 393224 | tf_op jit(solution)/shard_map/ppermute | solution.py:247
  5.6 6.9 %collective-permute-start.4 = (bf16[2,128,256]{2,1,0:T(8,128)(2,1)S(1)}, bf16[2,128,256]{2,1,0:T(8,128)(2,1)S(1)}, u32[]{:S(2)}, u32[]{:S(2)}) collective-permute-start(bf16[2,128,256]{2,1,0:T(8,128)(2,1)S(1)} %get-tuple-element.45.own_ref), channel_id=1, source_target_pairs={{0,4},{1,5},{2,6},{3,7},{4,0},{5,1},{6,2},{7,3},{8,9},{9,8},{10,11... | collective-permute-start | bytes 393224 | tf_op jit(solution)/shard_map/ppermute | solution.py:259
  7.5 6.0 %collective-permute-start.3 = (bf16[128,256]{1,0:T(8,128)(2,1)S(1)}, bf16[128,256]{1,0:T(8,128)(2,1)S(1)}, u32[]{:S(2)}, u32[]{:S(2)}) collective-permute-start(bf16[128,256]{1,0:T(8,128)(2,1)S(1)} %get-tuple-element.44.own_ref), channel_id=1, source_target_pairs={{0,8},{4,12},{8,0},{12,4},{1,9},{5,13},{9,1},{13,5},{2,10},{6,14},... | collective-permute-start | bytes 196616 | tf_op jit(solution)/shard_map/ppermute | solution.py:247
  10.9 4.5 %collective-permute-start.2 = (bf16[128,256]{1,0:T(8,128)(2,1)S(1)}, bf16[128,256]{1,0:T(8,128)(2,1)S(1)}, u32[]{:S(2)}, u32[]{:S(2)}) collective-permute-start(bf16[128,256]{1,0:T(8,128)(2,1)S(1)} %get-tuple-element.43.own_ref), channel_id=1, source_target_pairs={{0,4},{4,0},{8,12},{12,8},{1,5},{5,1},{9,13},{13,9},{2,6},{6,2},{1... | collective-permute-start | bytes 196616 | tf_op jit(solution)/shard_map/ppermute | solution.py:247
  12.6 6.3 %collective-permute-start.7 = (bf16[2,128,256]{2,1,0:T(8,128)(2,1)S(1)}, bf16[2,128,256]{2,1,0:T(8,128)(2,1)S(1)}, u32[]{:S(2)}, u32[]{:S(2)}) collective-permute-start(bf16[2,128,256]{2,1,0:T(8,128)(2,1)S(1)} %get-tuple-element.52), channel_id=1, source_target_pairs={{0,1},{1,0},{2,3},{3,2},{4,8},{5,9},{6,10},{7,11},{8,4},{9,5},{10,... | collective-permute-start | bytes 393224 | tf_op jit(solution)/shard_map/ppermute | solution.py:259
  13.6 5.4 %collective-permute-start.6 = (bf16[128,256]{1,0:T(8,128)(2,1)S(1)}, bf16[128,256]{1,0:T(8,128)(2,1)S(1)}, u32[]{:S(2)}, u32[]{:S(2)}) collective-permute-start(bf16[128,256]{1,0:T(8,128)(2,1)S(1)} %get-tuple-element.51), channel_id=1, source_target_pairs={{0,4},{4,0},{8,12},{12,8},{1,5},{5,1},{9,13},{13,9},{2,6},{6,2},{1... | collective-permute-start | bytes 196616 | tf_op jit(solution)/shard_map/ppermute | solution.py:247
  15.4 5.9 %copy-start = (bf16[3,3,256,256]{3,2,1,0:T(8,128)(2,1)S(1)}, bf16[3,3,256,256]{3,2,1,0:T(8,128)(2,1)}, u32[]{:S(2)}) copy-start(bf16[3,3,256,256]{3,2,1,0:T(8,128)(2,1)} %w_ref.13) | copy-start | bytes 3538948
  15.4 5.7 %collective-permute-start.5 = (bf16[128,256]{1,0:T(8,128)(2,1)S(1)}, bf16[128,256]{1,0:T(8,128)(2,1)S(1)}, u32[]{:S(2)}, u32[]{:S(2)}) collective-permute-start(bf16[128,256]{1,0:T(8,128)(2,1)S(1)} %get-tuple-element.49), channel_id=1, source_target_pairs={{0,8},{4,12},{8,0},{12,4},{1,9},{5,13},{9,1},{13,5},{2,10},{6,14},... | collective-permute-start | bytes 196616 | tf_op jit(solution)/shard_map/ppermute | solution.py:247
  18.9 3.0 %copy-start.3 = (bf16[2,4,128,256]{3,2,1,0:T(8,128)(2,1)S(1)}, bf16[2,4,128,256]{3,2,1,0:T(8,128)(2,1)}, u32[]{:S(2)}) copy-start(bf16[2,4,128,256]{3,2,1,0:T(8,128)(2,1)} %x_ref.7) | copy-start | bytes 1572868
  19.0 2.9 %collective-permute-start.10 = (bf16[2,128,256]{2,1,0:T(8,128)(2,1)S(1)}, bf16[2,128,256]{2,1,0:T(8,128)(2,1)S(1)}, u32[]{:S(2)}, u32[]{:S(2)}) collective-permute-start(bf16[2,128,256]{2,1,0:T(8,128)(2,1)S(1)} %get-tuple-element.58), channel_id=1, source_target_pairs={{0,1},{1,0},{2,3},{3,2},{4,5},{5,4},{6,7},{7,6},{8,12},{9,13},{10,... | collective-permute-start | bytes 393224 | tf_op jit(solution)/shard_map/ppermute | solution.py:259
  19.1 5.0 %collective-permute-start.9 = (bf16[2,128,256]{2,1,0:T(8,128)(2,1)S(1)}, bf16[2,128,256]{2,1,0:T(8,128)(2,1)S(1)}, u32[]{:S(2)}, u32[]{:S(2)}) collective-permute-start(bf16[2,128,256]{2,1,0:T(8,128)(2,1)S(1)} %get-tuple-element.57.outer_in), channel_id=1, source_target_pairs={{0,16},{1,2},{2,1},{3,19},{16,0},{17,18},{18,17},{19,3},{4,20},{5,... | collective-permute-start | bytes 393224 | tf_op jit(solution)/shard_map/ppermute | solution.py:272
  21.2 3.2 %collective-permute-start.8 = (bf16[2,128,256]{2,1,0:T(8,128)(2,1)S(1)}, bf16[2,128,256]{2,1,0:T(8,128)(2,1)S(1)}, u32[]{:S(2)}, u32[]{:S(2)}) collective-permute-start(bf16[2,128,256]{2,1,0:T(8,128)(2,1)S(1)} %get-tuple-element.56.inner_in), channel_id=1, source_target_pairs={{0,1},{1,0},{2,3},{3,2},{4,5},{5,4},{6,7},{7,6},{8,9},{9,8},{10,11... | collective-permute-start | bytes 393224 | tf_op jit(solution)/shard_map/ppermute | solution.py:247

commit v6 on v5

--- a/solution.py
+++ b/solution.py
@@ -59,9 +59,10 @@
     return join_columns(*[matmul(halo_ref[...], w_ref[place(2, 3), q]) for q in range(3)])
 
 
-def rows_kernel(x_ref, outer_ref, inner_ref):
+def rows_kernel(x_ref, outer_ref, second_ref, inner_ref):
     frames, strip = x_ref.shape[:2]
     for f in range(frames):
+        second_ref[f] = x_ref[f, place(1, strip)]
         outer_ref[f] = x_ref[f, place(0, strip)]
         inner_ref[f] = x_ref[f, place(strip - 1, strip)]
 
@@ -87,7 +88,7 @@
     sent_ref[...] = state[1 : strip - 1].astype(BF16)
 
 
-def drive_edge_kernel(beyond, halo_ref, w_ref, growth_ref, row_ref, result_ref, sent_ref, order_ref):
+def drive_edge_kernel(beyond, halo_ref, w_ref, growth_ref, row_ref, result_ref, sent_ref, order_ref, *rounded_ref):
     frames = row_ref.shape[0]
     driven = beyond(halo_ref, w_ref)
     decay = growth_ref[0]
@@ -96,7 +97,32 @@
         more = driven[f] if more is None else decay * more + driven[f]
         state = row_ref[f] + more
         result_ref[f] = state
+        for ref in rounded_ref:
+            ref[f] = state.astype(BF16)
     sent_ref[...] = state.astype(BF16)
+    order_ref[...] = growth_ref[...]
+
+
+def later_kernel(x_ref, growth_ref, out_ref):
+    out_ref[...] = x_ref[...]
+
+
+def arrived_kernel(halo_ref, growth_ref, order_ref):
+    order_ref[...] = growth_ref[...]
+
+
+def beyond_states_kernel(second_ref, halo_ref, outer_ref, w_ref, growth_ref, result_ref, order_ref):
+    above, level, below = second_ref[...], halo_ref[...], outer_ref[...]
+    driven = join_columns(
+        *[
+            matmul(above, w_ref[place(0, 3), q]) + matmul(level, w_ref[1, q]) + matmul(below, w_ref[place(2, 3), q])
+            for q in range(3)
+        ]
+    )
+    state = None
+    for f in range(driven.shape[0]):
+        state = driven[f] if state is None else growth_ref[0] * state + driven[f]
+        result_ref[f] = state
     order_ref[...] = growth_ref[...]
 
 
@@ -109,13 +135,14 @@
     order_ref[...] = growth_ref[...]
 
 
-def edge_states_kernel(row_ref, near_ref, far_ref, growth_ref, states_ref, order_ref):
+def edge_states_kernel(row_ref, near_ref, far_ref, growth_ref, states_ref, order_ref, carried_ref):
     frames = row_ref.shape[0]
     over = growth_ref[frames - 1]
     mine = lax.axis_index("tm")
     near, far = near_ref[...].astype(F32), far_ref[...].astype(F32)
     far = jnp.where(mine >= 2, far, 0.0)
     carried = jnp.where(mine % 2 == 1, over * far + near, far)
+    carried_ref[...] = carried.astype(BF16)
     for f in range(frames):
         states_ref[f] = (row_ref[f] + growth_ref[f] * carried).astype(BF16)
     order_ref[...] = growth_ref[...]
@@ -138,12 +165,13 @@
     order_ref[...] = growth_ref[...]
 
 
-def far_states_kernel(row_ref, far_ref, near_ref, growth_ref, states_ref, order_ref):
+def far_states_kernel(row_ref, far_ref, near_ref, growth_ref, states_ref, order_ref, carried_ref):
     frames = row_ref.shape[0]
     mine = lax.axis_index("tm")
     far = jnp.where(mine >= 2, far_ref[...].astype(F32), 0.0)
     near = jnp.where(mine >= 1, near_ref[...].astype(F32), 0.0)
     carried = near + growth_ref[frames - 1] * far
+    carried_ref[...] = carried.astype(BF16)
     for f in range(frames):
         states_ref[f] = (row_ref[f] + growth_ref[f] * carried).astype(BF16)
     order_ref[...] = growth_ref[...]
@@ -207,11 +235,15 @@
         middle_ref[f] = residual(x_ref[f, 1 : strip - 1], middle_in[f] + mixed[1 : strip - 1])
 
 
-def mix_beyond_kernel(halo_ref, w_ref, outer_in, outer_ref):
-    outer_ref[...] = outer_in[...] + from_outside(halo_ref, w_ref)
-
-
-def finish_kernel(halo_ref, w_ref, outer_ref, inner_ref, middle_ref, x_ref, out_ref, ready, sems):
+def carried_on(partial_ref, carried_ref, growth_ref):
+    return (partial_ref[...].astype(F32) + growth_ref[...] * carried_ref[...].astype(F32)[None]).astype(BF16)
+
+
+def mix_beyond_kernel(partial_ref, carried_ref, growth_ref, w_ref, outer_in, outer_ref):
+    outer_ref[...] = outer_in[...] + from_outside(carried_on(partial_ref, carried_ref, growth_ref), w_ref)
+
+
+def finish_kernel(partial_ref, carried_ref, growth_ref, w_ref, outer_ref, inner_ref, middle_ref, x_ref, out_ref, ready, sems):
     frames, strip = x_ref.shape[:2]
     copies = []
 
@@ -222,7 +254,7 @@
     for f in range(frames):
         send(middle_ref.at[f], out_ref.at[f, 1 : strip - 1])
     for side, row in ((0, 0), (1, strip - 1)):
-        mixed = inner_ref[...] + from_inside(halo_ref, w_ref) if side else outer_ref[...]
+        mixed = inner_ref[...] + from_inside(carried_on(partial_ref, carried_ref, growth_ref), w_ref) if side else outer_ref[...]
         for f in range(frames):
             ready[side, f] = residual(x_ref[f, place(row, strip)], mixed[f])
             send(ready.at[side, f], out_ref.at[f, place(row, strip)])
@@ -230,7 +262,7 @@
         copy.wait()
 
 
-def call(kernel, out_shape, in_specs, out_specs, scratch, flops, aliases=None):
+def call(kernel, out_shape, in_specs, out_specs, scratch, flops, aliases=None, moved=1 << 20):
     return pl.pallas_call(
         kernel,
         out_shape=out_shape,
@@ -239,7 +271,7 @@
         scratch_shapes=scratch,
         input_output_aliases=aliases or {},
         compiler_params=pltpu.CompilerParams(vmem_limit_bytes=LIMIT),
-        cost_estimate=pl.CostEstimate(flops=flops, bytes_accessed=1 << 20, transcendentals=0),
+        cost_estimate=pl.CostEstimate(flops=flops, bytes_accessed=moved, transcendentals=0),
     )
 
 
@@ -302,7 +334,7 @@
     conv_flops = 2 * 9 * frames * strip * width * channels * channels
     taps = pltpu.VMEM((3, frames, strip, width, channels), F32)
 
-    x_outer, x_inner = call(rows_kernel, (row_bf16,) * 2, [VMEM], (VMEM,) * 2, [], 2 * conv_flops)(latents)
+    x_outer, x_second, x_inner = call(rows_kernel, (row_bf16,) * 3, [VMEM], (VMEM,) * 3, [], 2 * conv_flops)(latents)
     halo_outer = across_chips(x_outer)
     halo_inner = swapped(x_inner, "rows", 1)
     outer, middle, inner, sent, growth = call(
@@ -314,15 +346,27 @@
         SMALL,
     )(latents, weight_in, decay_table[None, :], decay_index[None, :])
 
-    def edge(beyond, halo, mixed, growth):
+    def edge(beyond, halo, mixed, growth, *more):
         kernel = functools.partial(drive_edge_kernel, beyond)
-        return call(kernel, (row_f32, last_bf16, order), [VMEM] * 4, (VMEM,) * 3, [], SMALL)(halo, weight_in, growth, mixed)
+        out_shape = (row_f32, last_bf16, order) + more
+        return call(kernel, out_shape, [VMEM] * 4, (VMEM,) * len(out_shape), [], SMALL)(halo, weight_in, growth, mixed)
+
+    def arrived(halo, growth):
+        return call(arrived_kernel, order, [VMEM] * 2, VMEM, [], SMALL, moved=SMALL)(halo, growth)
+
+    def beyond_states(growth, halo_second):
+        return call(beyond_states_kernel, (row_f32, order), [VMEM] * 5, (VMEM,) * 2, [], SMALL, moved=SMALL)(
+            halo_second, halo_outer, x_outer, weight_in, growth
+        )
 
     if lax.axis_size("tm") == 4:
         first = swapped_between(sent, 0)
         outer, sent_outer, growth = edge(from_outside, halo_outer, outer, growth)
-        inner, sent_inner, growth = edge(from_inside, halo_inner, inner, growth)
+        inner, sent_inner, growth, rounded = edge(from_inside, halo_inner, inner, growth, row_bf16)
         far_outer = swapped(sent_outer, "tm", 2)
+        x_second = call(later_kernel, row_bf16, [VMEM] * 2, VMEM, [], SMALL, moved=SMALL)(x_second, growth)
+        halo_second = across_chips(x_second)
+        inner_partial = swapped(rounded, "rows", 1)
         near_inner = swapped(sent_inner, "tm", 1)
         total, growth = call(relay_kernel, (inside_bf16, order), [VMEM] * 3, (VMEM,) * 2, [], SMALL)(sent, first, growth)
         second = swapped_between(total, 1)
@@ -330,22 +374,30 @@
         near_outer = swapped(relayed_outer, "tm", 1)
         total_inner, growth = call(pair_kernel, (last_bf16, order), [VMEM] * 3, (VMEM,) * 2, [], LONG)(sent_inner, near_inner, growth)
         far_inner = swapped(total_inner, "tm", 2)
+        growth = arrived(halo_second, growth)
         message, growth = call(relay_kernel, (inside_bf16, order), [VMEM] * 3, (VMEM,) * 2, [], SMALL)(sent, second, growth)
         third = swapped_between(message, 2)
-        states_outer, growth = call(far_states_kernel, (row_bf16, order), [VMEM] * 4, (VMEM,) * 2, [], SMALL)(outer, far_outer, near_outer, growth)
-        halo_outer = across_chips(states_outer)
-        states_inner, growth = call(edge_states_kernel, (row_bf16, order), [VMEM] * 4, (VMEM,) * 2, [], SMALL)(inner, near_inner, far_inner, growth)
-        halo_inner = swapped(states_inner, "rows", 1)
+        states_outer, growth, carried_outer = call(
+            far_states_kernel, (row_bf16, order, last_bf16), [VMEM] * 4, (VMEM,) * 3, [], LONG
+        )(outer, far_outer, near_outer, growth)
+        halo_carried = across_chips(carried_outer)
+        halo_partial, growth = beyond_states(growth, halo_second)
+        states_inner, growth, carried_inner = call(
+            edge_states_kernel, (row_bf16, order, last_bf16), [VMEM] * 4, (VMEM,) * 3, [], SMALL
+        )(inner, near_inner, far_inner, growth)
+        inner_carried = swapped(carried_inner, "rows", 1)
     else:
-        inner, sent_inner, growth = edge(from_inside, halo_inner, inner, growth)
+        inner, sent_inner, growth, rounded = edge(from_inside, halo_inner, inner, growth, row_bf16)
         outer, sent_outer, growth = edge(from_outside, halo_outer, outer, growth)
         over = growth[frames - 1]
-        states_outer = (outer + growth * butterfly(sent_outer, over, "tm")[None]).astype(BF16)
-        states_inner = (inner + growth * butterfly(sent_inner, over, "tm")[None]).astype(BF16)
+        halo_partial, growth = beyond_states(growth, across_chips(x_second))
+        inner_partial = swapped(rounded, "rows", 1)
+        carried_outer, carried_inner = butterfly(sent_outer, over, "tm"), butterfly(sent_inner, over, "tm")
+        states_outer = (outer + growth * carried_outer[None]).astype(BF16)
+        states_inner = (inner + growth * carried_inner[None]).astype(BF16)
         first = second = third = butterfly(sent, over, "tm").astype(BF16)
-        halo_outer = across_chips(states_outer)
-        halo_inner = swapped(states_inner, "rows", 1)
-
+        halo_carried = across_chips(carried_outer.astype(BF16))
+        inner_carried = swapped(carried_inner.astype(BF16), "rows", 1)
     ends = call(mix_ends_kernel, (row_f32, middle_f32, row_f32), [VMEM] * 3, (VMEM,) * 3, [], SMALL)(
         states_outer, states_inner, weight_out
     )
@@ -357,15 +409,17 @@
         [taps, pltpu.VMEM((strip, width, channels), F32)],
         SMALL,
     )(first, second, third, growth, middle, weight_out, *ends, latents)
-    outer = call(mix_beyond_kernel, row_f32, [VMEM] * 3, VMEM, [], SMALL)(halo_outer, weight_out, outer)
+    outer = call(mix_beyond_kernel, row_f32, [VMEM] * 5, VMEM, [], SMALL)(
+        halo_partial, halo_carried, growth, weight_out, outer
+    )
     return call(
         finish_kernel,
         shaped(latents.shape, BF16),
-        [VMEM] * 6,
+        [VMEM] * 8,
         ANY,
         [pltpu.VMEM((2,) + row, BF16), pltpu.SemaphoreType.DMA((3 * frames,))],
         SMALL,
-    )(halo_inner, weight_out, outer, inner, middle, latents)
+    )(inner_partial, inner_carried, growth, weight_out, outer, inner, middle, latents)
 
 
 def solution(mesh):

time: 25.7 us -> 25.3 us (0.984)
  starting transfers between devices: 16.6 us -> 15.8 us
  Pallas kernels: 5.24 us -> 5.76 us
    ppermute x6 -> x7, starting transfers between devices: 10.1 us -> 8.74 us  [swapped(): lax.ppermute(value, axis, [(i, i ^ distance) for i in range(lax.axis_size...]
    ppermute x2 -> x3, waiting for transfers between devices: 1.17 us -> 0.25 us  [across_chips(): return lax.ppermute(value, ('groups', 'rows'), pairs)]
    ppermute x6 -> x7, waiting for transfers between devices: 1.26 us -> 1.94 us  [swapped(): lax.ppermute(value, axis, [(i, i ^ distance) for i in range(lax.axis_size...]
    ppermute x2 -> x3, starting transfers between devices: 4.72 us -> 5.29 us  [across_chips(): return lax.ppermute(value, ('groups', 'rows'), pairs)]
    pallas_call x7 -> x10, Pallas kernels: 2.11 us -> 2.63 us  [the longest x1 1.16 us: local(): call(finish_kernel, shaped(latents.shape, BF16), [VMEM] * 8, ANY, [pltpu....]
  transfers between devices with their start and end apart: 11 -> 13, of which waited for: 3 -> 3; matrix products, arithmetic and copies ran while one was open for 0% -> 0% of each run, Pallas kernels for 16% -> 18%
where the time goes in v6:
time: 25.3 us; the launch traced here: 25.1 us
  starting transfers between devices  15.8 us (62%)
  Pallas kernels  5.76 us (23%)
  waiting for transfers between devices  2.2 us (9%)
  local copies, waits for them, and re-layouts  1.16 us (5%)
    ppermute x7, starting transfers between devices, swapped(): lax.ppermute(value, axis, [(i, i ^ distance) for i in range(lax.axis_size...  8.74 us
    ppermute x3, starting transfers between devices, across_chips(): return lax.ppermute(value, ('groups', 'rows'), pairs)  5.29 us
    ppermute x7, waiting for transfers between devices, swapped(): lax.ppermute(value, axis, [(i, i ^ distance) for i in range(lax.axis_size...  1.94 us
    ppermute x3, starting transfers between devices, swapped_between(): return lax.ppermute(value, ('tm', 'rows'), pairs)  1.78 us
    pallas_call x1, Pallas kernels, local(): call(drive_kernel, (row_f32, middle_f32, row_f32, inside_bf16, order), [V...  1.31 us
    unnamed x12, local copies, waits for them, and re-layouts  1.16 us
    pallas_call x1, Pallas kernels, local(): call(finish_kernel, shaped(latents.shape, BF16), [VMEM] * 8, ANY, [pltpu....  1.16 us
    pallas_call x1, Pallas kernels, local(): call(mix_inside_kernel, (row_f32, shaped((frames,) + inside, BF16), row_f...  1.05 us
  transfers between devices with their start and end apart: 13, of which 3 were waited for; matrix products, arithmetic and copies ran while one was open for 0% of the time, Pallas kernels for 18%

profile of v6, /device:TPU:0, one launch (start us, length us, event | category | flops | bytes accessed | tf_op | source)
XLA Modules:
  0.0 25.1 jit_solution(10163934713871101050)
XLA Ops:
  0.0 0.0 copy-start.1
  0.0 0.0 copy-start.2
  0.0 1.1 %copy-done.2 = bf16[2,4,128,256]{3,2,1,0:T(8,128)(2,1)S(1)} copy-done((bf16[2,4,128,256]{3,2,1,0:T(8,128)(2,1)S(1)}, bf16[2,4,128,256]{3,2,1,0:T(8,128)(2,1)}, u32[]{:S(2)}) %copy-start.2) | copy-done | bytes 524312
  1.1 0.0 copy-start.4
  1.1 0.0 copy-start.5
  1.2 3.0 %collective-permute-start.1 = (bf16[2,128,256]{2,1,0:T(8,128)(2,1)S(1)}, bf16[2,128,256]{2,1,0:T(8,128)(2,1)S(1)}, u32[]{:S(2)}, u32[]{:S(2)}) collective-permute-start(bf16[2,128,256]{2,1,0:T(8,128)(2,1)S(1)} %get-tuple-element.43.outer_ref), channel_id=1, source_target_pairs={{0,16},{1,2},{2,1},{3,19},{16,0},{17,18},{18,17},{19,3},{4,20},{5,... | collective-permute-start | bytes 393224 | tf_op jit(solution)/shard_map/ppermute | solution.py:304
  4.2 0.1 collective-permute-start
  4.3 0.0 copy-done.1
  4.3 0.0 copy-done.4
  4.3 0.0 copy-done.5
  4.3 1.3 %shard_map.56 = (f32[2,128,256]{2,1,0:T(8,128)S(1)}, f32[2,2,128,256]{3,2,1,0:T(8,128)S(1)}, f32[2,128,256]{2,1,0:T(8,128)S(1)}, bf16[2,128,256]{2,1,0:T(8,128)(2,1)S(1)}, f32[2,1,256]{2,1,0:T(1,128)S(1)}) custom-call(bf16[2,4,128,256]{3,2,1,0:T(8,128)(2,1)S(1)} %copy-done.2, bf16[3,3,256,256]{3,2,1,0:T(8,128)(2,1)S(1)} %copy-done.1, f32[1,16]{1,0:T(1,128)S(1)} %bitcast.3, ...), custom_call_target="tpu_custom_call" | custom-call | flops 1000 | bytes 1048576 | tf_op jit(solution)/shard_map/pallas_call | solution.py:340
  5.6 1.6 %collective-permute-start.5 = (bf16[2,128,256]{2,1,0:T(8,128)(2,1)S(1)}, bf16[2,128,256]{2,1,0:T(8,128)(2,1)S(1)}, u32[]{:S(2)}, u32[]{:S(2)}) collective-permute-start(bf16[2,128,256]{2,1,0:T(8,128)(2,1)S(1)} %get-tuple-element.52.own_ref), channel_id=1, source_target_pairs={{0,4},{1,5},{2,6},{3,7},{4,0},{5,1},{6,2},{7,3},{8,9},{9,8},{10,11... | collective-permute-start | bytes 393224 | tf_op jit(solution)/shard_map/ppermute | solution.py:291
  7.3 0.0 collective-permute-done.1.halo_ref
  7.3 0.3 %shard_map.57 = (f32[2,128,256]{2,1,0:T(8,128)S(1)}, bf16[128,256]{1,0:T(8,128)(2,1)S(1)}, f32[2,1,256]{2,1,0:T(1,128)S(1)}) custom-call(bf16[2,128,256]{2,1,0:T(8,128)(2,1)S(1)} %collective-permute-done.1.halo_ref, bf16[3,3,256,256]{3,2,1,0:T(8,128)(2,1)S(1)} %copy-done.1, f32[2,1,256]{2,1,0:T(1,128)S(1)} %get-tuple-element.44.growth_ref, ...), custom_call_target="tpu_custom_call" | custom-call | flops 1000 | bytes 1048576 | tf_op jit(solution)/shard_map/pallas_call | solution.py:352
  7.5 3.0 %collective-permute-start.4 = (bf16[128,256]{1,0:T(8,128)(2,1)S(1)}, bf16[128,256]{1,0:T(8,128)(2,1)S(1)}, u32[]{:S(2)}, u32[]{:S(2)}) collective-permute-start(bf16[128,256]{1,0:T(8,128)(2,1)S(1)} %get-tuple-element.51.own_ref), channel_id=1, source_target_pairs={{0,8},{4,12},{8,0},{12,4},{1,9},{5,13},{9,1},{13,5},{2,10},{6,14},... | collective-permute-start | bytes 196616 | tf_op jit(solution)/shard_map/ppermute | solution.py:279
  10.6 0.0 collective-permute-done.halo_ref
  10.6 0.3 %shard_map.58 = (f32[2,128,256]{2,1,0:T(8,128)S(1)}, bf16[128,256]{1,0:T(8,128)(2,1)S(1)}, f32[2,1,256]{2,1,0:T(1,128)S(1)}, bf16[2,128,256]{2,1,0:T(8,128)(2,1)S(1)}) custom-call(bf16[2,128,256]{2,1,0:T(8,128)(2,1)S(1)} %collective-permute-done.halo_ref, bf16[3,3,256,256]{3,2,1,0:T(8,128)(2,1)S(1)} %copy-done.1, ...), custom_call_target="tpu_custom_call" | custom-call | flops 1000 | bytes 1048576 | tf_op jit(solution)/shard_map/pallas_call | solution.py:352
  10.9 1.6 %collective-permute-start.3 = (bf16[128,256]{1,0:T(8,128)(2,1)S(1)}, bf16[128,256]{1,0:T(8,128)(2,1)S(1)}, u32[]{:S(2)}, u32[]{:S(2)}) collective-permute-start(bf16[128,256]{1,0:T(8,128)(2,1)S(1)} %get-tuple-element.50.own_ref), channel_id=1, source_target_pairs={{0,4},{4,0},{8,12},{12,8},{1,5},{5,1},{9,13},{13,9},{2,6},{6,2},{1... | collective-permute-start | bytes 196616 | tf_op jit(solution)/shard_map/ppermute | solution.py:279
  12.5 0.0 collective-permute-start.2
  12.5 1.6 %collective-permute-start.7 = (bf16[2,128,256]{2,1,0:T(8,128)(2,1)S(1)}, bf16[2,128,256]{2,1,0:T(8,128)(2,1)S(1)}, u32[]{:S(2)}, u32[]{:S(2)}) collective-permute-start(bf16[2,128,256]{2,1,0:T(8,128)(2,1)S(1)} %shard_map.62), channel_id=1, source_target_pairs={{0,16},{1,2},{2,1},{3,19},{16,0},{17,18},{18,17},{19,3},{4,20},{5,... | collective-permute-start | bytes 393224 | tf_op jit(solution)/shard_map/ppermute | solution.py:304
  14.1 0.0 collective-permute-done.5.before_ref.first_ref
  14.2 0.1 collective-permute-start.9
  14.3 0.0 collective-permute-done.4.far_ref
  14.3 0.9 %collective-permute-start.8 = (bf16[128,256]{1,0:T(8,128)(2,1)S(1)}, bf16[128,256]{1,0:T(8,128)(2,1)S(1)}, u32[]{:S(2)}, u32[]{:S(2)}) collective-permute-start(bf16[128,256]{1,0:T(8,128)(2,1)S(1)} %get-tuple-element.59), channel_id=1, source_target_pairs={{0,4},{4,0},{8,12},{12,8},{1,5},{5,1},{9,13},{13,9},{2,6},{6,2},{1... | collective-permute-start | bytes 196616 | tf_op jit(solution)/shard_map/ppermute | solution.py:279
  15.3 0.0 collective-permute-done.3.other_ref.near_ref
  15.3 3.0 %collective-permute-start.6 = (bf16[128,256]{1,0:T(8,128)(2,1)S(1)}, bf16[128,256]{1,0:T(8,128)(2,1)S(1)}, u32[]{:S(2)}, u32[]{:S(2)}) collective-permute-start(bf16[128,256]{1,0:T(8,128)(2,1)S(1)} %get-tuple-element.56), channel_id=1, source_target_pairs={{0,8},{4,12},{8,0},{12,4},{1,9},{5,13},{9,1},{13,5},{2,10},{6,14},... | collective-permute-start | bytes 196616 | tf_op jit(solution)/shard_map/ppermute | solution.py:279
  18.3 0.0 collective-permute-done.7.halo_ref.second_ref
  18.3 0.0 collective-permute-done.9.before_ref.second_ref
  18.3 0.1 collective-permute-start.12
  18.4 0.8 %collective-permute-done.8.near_ref = bf16[128,256]{1,0:T(8,128)(2,1)S(1)} collective-permute-done((bf16[128,256]{1,0:T(8,128)(2,1)S(1)}, bf16[128,256]{1,0:T(8,128)(2,1)S(1)}, u32[]{:S(2)}, u32[]{:S(2)}) %collective-permute-start.8) | collective-permute-done | bytes 65568 | tf_op jit(solution)/shard_map/ppermute | solution.py:279
  19.2 0.1 shard_map.65
  19.3 0.0 copy-start
  19.3 0.7 %collective-permute-start.11 = (bf16[128,256]{1,0:T(8,128)(2,1)S(1)}, bf16[128,256]{1,0:T(8,128)(2,1)S(1)}, u32[]{:S(2)}, u32[]{:S(2)}) collective-permute-start(bf16[128,256]{1,0:T(8,128)(2,1)S(1)} %get-tuple-element.68), channel_id=1, source_target_pairs={{0,16},{1,2},{2,1},{3,19},{16,0},{17,18},{18,17},{19,3},{4,20},{5,... | collective-permute-start | bytes 196616 | tf_op jit(solution)/shard_map/ppermute | solution.py:304
  20.0 0.5 %shard_map.66 = (f32[2,128,256]{2,1,0:T(8,128)S(1)}, f32[2,1,256]{2,1,0:T(1,128)S(1)}) custom-call(bf16[2,128,256]{2,1,0:T(8,128)(2,1)S(1)} %collective-permute-done.7.halo_ref.second_ref, bf16[2,128,256]{2,1,0:T(8,128)(2,1)S(1)} %collective-permute-done.1.halo_ref, bf16[2,128,256]{2,1,0:T(8,128)(2,1)S(1)} %get-tuple-element.43.outer_ref, ...), custom_call_target="tpu_custom_call" | custom-call | flops 1000 | bytes 1000 | tf_op jit(solution)/shard_map/pallas_call | solution.py:358
  20.5 0.0 copy-start.3
  20.5 1.1 %collective-permute-done.6.far_ref = bf16[128,256]{1,0:T(8,128)(2,1)S(1)} collective-permute-done((bf16[128,256]{1,0:T(8,128)(2,1)S(1)}, bf16[128,256]{1,0:T(8,128)(2,1)S(1)}, u32[]{:S(2)}, u32[]{:S(2)}) %collective-permute-start.6) | collective-permute-done | bytes 65568 | tf_op jit(solution)/shard_map/ppermute | solution.py:279
  21.6 0.1 shard_map.67
  21.6 0.1 collective-permute-start.10
  21.7 0.0 copy-done
  21.7 0.6 %shard_map.68 = (f32[2,128,256]{2,1,0:T(8,128)S(1)}, f32[2,2,128,256]{3,2,1,0:T(8,128)S(1)}, f32[2,128,256]{2,1,0:T(8,128)S(1)}) custom-call(bf16[2,128,256]{2,1,0:T(8,128)(2,1)S(1)} %get-tuple-element.71.outer_in, bf16[2,128,256]{2,1,0:T(8,128)(2,1)S(1)} %get-tuple-element.72.inner_in, bf16[3,3,256,256]{3,2,1,0:T(8,128)(2,1)S(1)} %copy-done), custom_call_target="tpu_custom_call" | custom-call | flops 1000 | bytes 1048576 | tf_op jit(solution)/shard_map/pallas_call | solution.py:401
  22.3 0.0 collective-permute-done.12.third_ref
  22.3 0.0 copy-done.3
  22.3 1.0 %shard_map.69 = (f32[2,128,256]{2,1,0:T(8,128)S(1)}, bf16[2,2,128,256]{3,2,1,0:T(8,128)(2,1)S(1)}, f32[2,128,256]{2,1,0:T(8,128)S(1)}) custom-call(bf16[2,128,256]{2,1,0:T(8,128)(2,1)S(1)} %collective-permute-done.5.before_ref.first_ref, bf16[2,128,256]{2,1,0:T(8,128)(2,1)S(1)} %collective-permute-done.9.before_ref.second_ref, ...), custom_call_target="tpu_custom_call" | custom-call | flops 1000 | bytes 1048576 | tf_op jit(solution)/shard_map/pallas_call | solution.py:404
  23.4 0.2 collective-permute-done.11.carried_ref
  23.7 0.3 %shard_map.70.outer_ref = f32[2,128,256]{2,1,0:T(8,128)S(1)} custom-call(f32[2,128,256]{2,1,0:T(8,128)S(1)} %get-tuple-element.67.partial_ref, bf16[128,256]{1,0:T(8,128)(2,1)S(1)} %collective-permute-done.11.carried_ref, f32[2,1,256]{2,1,0:T(1,128)S(1)} %get-tuple-element.66.growth_ref, bf16[3,3,256,256]{3,2,1,0:T(8,128)(2,1)S(1)} %copy-done, ...), custom_call_target="tpu_custom_call" | custom-call | flops 1000 | bytes 1048576 | tf_op jit(solution)/shard_map/pallas_call | solution.py:412
  23.9 0.0 collective-permute-done.2.partial_ref
  24.0 0.0 collective-permute-done.10.carried_ref
  24.0 1.2 %shard_map.71 = bf16[2,4,128,256]{3,2,1,0:T(8,128)(2,1)} custom-call(bf16[2,128,256]{2,1,0:T(8,128)(2,1)S(1)} %collective-permute-done.2.partial_ref, bf16[128,256]{1,0:T(8,128)(2,1)S(1)} %collective-permute-done.10.carried_ref, f32[2,1,256]{2,1,0:T(1,128)S(1)} %get-tuple-element.66.growth_ref, bf16[3,3,256,256]{3,2,1,0:T(8,128)(2,1)S(1)} %copy-done, ...), custom_call_target="tpu_custom_call" | custom-call | flops 1000 | bytes 1048576 | tf_op jit(solution)/shard_map/pallas_call | solution.py:415
  (7 shorter events, 0.2 us)
Async XLA Ops:
  0.0 4.3 %copy-start.1 = (bf16[3,3,256,256]{3,2,1,0:T(8,128)(2,1)S(1)}, bf16[3,3,256,256]{3,2,1,0:T(8,128)(2,1)}, u32[]{:S(2)}) copy-start(bf16[3,3,256,256]{3,2,1,0:T(8,128)(2,1)} %w_ref.11) | copy-start | bytes 3538948
  0.0 1.1 %copy-start.2 = (bf16[2,4,128,256]{3,2,1,0:T(8,128)(2,1)S(1)}, bf16[2,4,128,256]{3,2,1,0:T(8,128)(2,1)}, u32[]{:S(2)}) copy-start(bf16[2,4,128,256]{3,2,1,0:T(8,128)(2,1)} %x_ref.7) | copy-start | bytes 1572868
  1.1 3.2 %copy-start.4 = (s32[256]{0:T(256)S(1)}, s32[256]{0:T(256)}, u32[]{:S(2)}) copy-start(s32[256]{0:T(256)} %param.9) | copy-start | bytes 3076
  1.1 3.2 %copy-start.5 = (f32[16]{0:T(128)S(1)}, f32[16]{0:T(128)}, u32[]{:S(2)}) copy-start(f32[16]{0:T(128)} %param.8) | copy-start | bytes 196
  1.2 6.1 %collective-permute-start.1 = (bf16[2,128,256]{2,1,0:T(8,128)(2,1)S(1)}, bf16[2,128,256]{2,1,0:T(8,128)(2,1)S(1)}, u32[]{:S(2)}, u32[]{:S(2)}) collective-permute-start(bf16[2,128,256]{2,1,0:T(8,128)(2,1)S(1)} %get-tuple-element.43.outer_ref), channel_id=1, source_target_pairs={{0,16},{1,2},{2,1},{3,19},{16,0},{17,18},{18,17},{19,3},{4,20},{5,... | collective-permute-start | bytes 393224 | tf_op jit(solution)/shard_map/ppermute | solution.py:304
  4.2 6.4 %collective-permute-start = (bf16[2,128,256]{2,1,0:T(8,128)(2,1)S(1)}, bf16[2,128,256]{2,1,0:T(8,128)(2,1)S(1)}, u32[]{:S(2)}, u32[]{:S(2)}) collective-permute-start(bf16[2,128,256]{2,1,0:T(8,128)(2,1)S(1)} %get-tuple-element.42), channel_id=1, source_target_pairs={{0,1},{1,0},{2,3},{3,2},{4,5},{5,4},{6,7},{7,6},{8,9},{9,8},{10,11... | collective-permute-start | bytes 393224 | tf_op jit(solution)/shard_map/ppermute | solution.py:279
  5.6 8.5 %collective-permute-start.5 = (bf16[2,128,256]{2,1,0:T(8,128)(2,1)S(1)}, bf16[2,128,256]{2,1,0:T(8,128)(2,1)S(1)}, u32[]{:S(2)}, u32[]{:S(2)}) collective-permute-start(bf16[2,128,256]{2,1,0:T(8,128)(2,1)S(1)} %get-tuple-element.52.own_ref), channel_id=1, source_target_pairs={{0,4},{1,5},{2,6},{3,7},{4,0},{5,1},{6,2},{7,3},{8,9},{9,8},{10,11... | collective-permute-start | bytes 393224 | tf_op jit(solution)/shard_map/ppermute | solution.py:291
  7.5 6.7 %collective-permute-start.4 = (bf16[128,256]{1,0:T(8,128)(2,1)S(1)}, bf16[128,256]{1,0:T(8,128)(2,1)S(1)}, u32[]{:S(2)}, u32[]{:S(2)}) collective-permute-start(bf16[128,256]{1,0:T(8,128)(2,1)S(1)} %get-tuple-element.51.own_ref), channel_id=1, source_target_pairs={{0,8},{4,12},{8,0},{12,4},{1,9},{5,13},{9,1},{13,5},{2,10},{6,14},... | collective-permute-start | bytes 196616 | tf_op jit(solution)/shard_map/ppermute | solution.py:279
  10.9 4.4 %collective-permute-start.3 = (bf16[128,256]{1,0:T(8,128)(2,1)S(1)}, bf16[128,256]{1,0:T(8,128)(2,1)S(1)}, u32[]{:S(2)}, u32[]{:S(2)}) collective-permute-start(bf16[128,256]{1,0:T(8,128)(2,1)S(1)} %get-tuple-element.50.own_ref), channel_id=1, source_target_pairs={{0,4},{4,0},{8,12},{12,8},{1,5},{5,1},{9,13},{13,9},{2,6},{6,2},{1... | collective-permute-start | bytes 196616 | tf_op jit(solution)/shard_map/ppermute | solution.py:279
  12.5 11.4 %collective-permute-start.2 = (bf16[2,128,256]{2,1,0:T(8,128)(2,1)S(1)}, bf16[2,128,256]{2,1,0:T(8,128)(2,1)S(1)}, u32[]{:S(2)}, u32[]{:S(2)}) collective-permute-start(bf16[2,128,256]{2,1,0:T(8,128)(2,1)S(1)} %get-tuple-element.48), channel_id=1, source_target_pairs={{0,1},{1,0},{2,3},{3,2},{4,5},{5,4},{6,7},{7,6},{8,9},{9,8},{10,11... | collective-permute-start | bytes 393224 | tf_op jit(solution)/shard_map/ppermute | solution.py:279
  12.5 5.7 %collective-permute-start.7 = (bf16[2,128,256]{2,1,0:T(8,128)(2,1)S(1)}, bf16[2,128,256]{2,1,0:T(8,128)(2,1)S(1)}, u32[]{:S(2)}, u32[]{:S(2)}) collective-permute-start(bf16[2,128,256]{2,1,0:T(8,128)(2,1)S(1)} %shard_map.62), channel_id=1, source_target_pairs={{0,16},{1,2},{2,1},{3,19},{16,0},{17,18},{18,17},{19,3},{4,20},{5,... | collective-permute-start | bytes 393224 | tf_op jit(solution)/shard_map/ppermute | solution.py:304
  14.2 4.1 %collective-permute-start.9 = (bf16[2,128,256]{2,1,0:T(8,128)(2,1)S(1)}, bf16[2,128,256]{2,1,0:T(8,128)(2,1)S(1)}, u32[]{:S(2)}, u32[]{:S(2)}) collective-permute-start(bf16[2,128,256]{2,1,0:T(8,128)(2,1)S(1)} %get-tuple-element.60), channel_id=1, source_target_pairs={{0,1},{1,0},{2,3},{3,2},{4,8},{5,9},{6,10},{7,11},{8,4},{9,5},{10,... | collective-permute-start | bytes 393224 | tf_op jit(solution)/shard_map/ppermute | solution.py:291
  14.3 4.9 %collective-permute-start.8 = (bf16[128,256]{1,0:T(8,128)(2,1)S(1)}, bf16[128,256]{1,0:T(8,128)(2,1)S(1)}, u32[]{:S(2)}, u32[]{:S(2)}) collective-permute-start(bf16[128,256]{1,0:T(8,128)(2,1)S(1)} %get-tuple-element.59), channel_id=1, source_target_pairs={{0,4},{4,0},{8,12},{12,8},{1,5},{5,1},{9,13},{13,9},{2,6},{6,2},{1... | collective-permute-start | bytes 196616 | tf_op jit(solution)/shard_map/ppermute | solution.py:279
  15.3 6.3 %collective-permute-start.6 = (bf16[128,256]{1,0:T(8,128)(2,1)S(1)}, bf16[128,256]{1,0:T(8,128)(2,1)S(1)}, u32[]{:S(2)}, u32[]{:S(2)}) collective-permute-start(bf16[128,256]{1,0:T(8,128)(2,1)S(1)} %get-tuple-element.56), channel_id=1, source_target_pairs={{0,8},{4,12},{8,0},{12,4},{1,9},{5,13},{9,1},{13,5},{2,10},{6,14},... | collective-permute-start | bytes 196616 | tf_op jit(solution)/shard_map/ppermute | solution.py:279
  18.3 4.0 %collective-permute-start.12 = (bf16[2,128,256]{2,1,0:T(8,128)(2,1)S(1)}, bf16[2,128,256]{2,1,0:T(8,128)(2,1)S(1)}, u32[]{:S(2)}, u32[]{:S(2)}) collective-permute-start(bf16[2,128,256]{2,1,0:T(8,128)(2,1)S(1)} %get-tuple-element.69), channel_id=1, source_target_pairs={{0,1},{1,0},{2,3},{3,2},{4,5},{5,4},{6,7},{7,6},{8,12},{9,13},{10,... | collective-permute-start | bytes 393224 | tf_op jit(solution)/shard_map/ppermute | solution.py:291
  19.3 2.4 %copy-start = (bf16[3,3,256,256]{3,2,1,0:T(8,128)(2,1)S(1)}, bf16[3,3,256,256]{3,2,1,0:T(8,128)(2,1)}, u32[]{:S(2)}) copy-start(bf16[3,3,256,256]{3,2,1,0:T(8,128)(2,1)} %w_ref.15) | copy-start | bytes 3538948
  19.3 4.3 %collective-permute-start.11 = (bf16[128,256]{1,0:T(8,128)(2,1)S(1)}, bf16[128,256]{1,0:T(8,128)(2,1)S(1)}, u32[]{:S(2)}, u32[]{:S(2)}) collective-permute-start(bf16[128,256]{1,0:T(8,128)(2,1)S(1)} %get-tuple-element.68), channel_id=1, source_target_pairs={{0,16},{1,2},{2,1},{3,19},{16,0},{17,18},{18,17},{19,3},{4,20},{5,... | collective-permute-start | bytes 196616 | tf_op jit(solution)/shard_map/ppermute | solution.py:304
  20.5 1.9 %copy-start.3 = (bf16[2,4,128,256]{3,2,1,0:T(8,128)(2,1)S(1)}, bf16[2,4,128,256]{3,2,1,0:T(8,128)(2,1)}, u32[]{:S(2)}) copy-start(bf16[2,4,128,256]{3,2,1,0:T(8,128)(2,1)} %x_ref.7) | copy-start | bytes 1572868
  21.6 2.3 %collective-permute-start.10 = (bf16[128,256]{1,0:T(8,128)(2,1)S(1)}, bf16[128,256]{1,0:T(8,128)(2,1)S(1)}, u32[]{:S(2)}, u32[]{:S(2)}) collective-permute-start(bf16[128,256]{1,0:T(8,128)(2,1)S(1)} %get-tuple-element.65), channel_id=1, source_target_pairs={{0,1},{1,0},{2,3},{3,2},{4,5},{5,4},{6,7},{7,6},{8,9},{9,8},{10,11... | collective-permute-start | bytes 196616 | tf_op jit(solution)/shard_map/ppermute | solution.py:279

commit v7 on v6

--- a/solution.py
+++ b/solution.py
@@ -381,11 +381,11 @@
             far_states_kernel, (row_bf16, order, last_bf16), [VMEM] * 4, (VMEM,) * 3, [], LONG
         )(outer, far_outer, near_outer, growth)
         halo_carried = across_chips(carried_outer)
-        halo_partial, growth = beyond_states(growth, halo_second)
         states_inner, growth, carried_inner = call(
             edge_states_kernel, (row_bf16, order, last_bf16), [VMEM] * 4, (VMEM,) * 3, [], SMALL
         )(inner, near_inner, far_inner, growth)
         inner_carried = swapped(carried_inner, "rows", 1)
+        halo_partial, growth = beyond_states(growth, halo_second)
     else:
         inner, sent_inner, growth, rounded = edge(from_inside, halo_inner, inner, growth, row_bf16)
         outer, sent_outer, growth = edge(from_outside, halo_outer, outer, growth)

time: 25.3 us -> 25.6 us (1.012)
    ppermute x7, waiting for transfers between devices: 1.94 us -> 2.43 us  [swapped(): lax.ppermute(value, axis, [(i, i ^ distance) for i in range(lax.axis_size...]
  transfers between devices with their start and end apart: 13 -> 13, of which waited for: 3 -> 2; matrix products, arithmetic and copies ran while one was open for 0% -> 0% of each run, Pallas kernels for 18% -> 18%
where the time goes in v7:
time: 25.6 us; the launch traced here: 25.4 us
  starting transfers between devices  15.8 us (62%)
  Pallas kernels  5.78 us (23%)
  waiting for transfers between devices  2.45 us (10%)
  local copies, waits for them, and re-layouts  1.16 us (5%)
    ppermute x7, starting transfers between devices, swapped(): lax.ppermute(value, axis, [(i, i ^ distance) for i in range(lax.axis_size...  8.74 us
    ppermute x3, starting transfers between devices, across_chips(): return lax.ppermute(value, ('groups', 'rows'), pairs)  5.31 us
    ppermute x7, waiting for transfers between devices, swapped(): lax.ppermute(value, axis, [(i, i ^ distance) for i in range(lax.axis_size...  2.43 us
    ppermute x3, starting transfers between devices, swapped_between(): return lax.ppermute(value, ('tm', 'rows'), pairs)  1.78 us
    pallas_call x1, Pallas kernels, local(): call(drive_kernel, (row_f32, middle_f32, row_f32, inside_bf16, order), [V...  1.31 us
    pallas_call x1, Pallas kernels, local(): call(finish_kernel, shaped(latents.shape, BF16), [VMEM] * 8, ANY, [pltpu....  1.16 us
    unnamed x12, local copies, waits for them, and re-layouts  1.16 us
    pallas_call x1, Pallas kernels, local(): call(mix_inside_kernel, (row_f32, shaped((frames,) + inside, BF16), row_f...  1.06 us
  transfers between devices with their start and end apart: 13, of which 2 were waited for; matrix products, arithmetic and copies ran while one was open for 0% of the time, Pallas kernels for 18%

profile of v7, /device:TPU:0, one launch (start us, length us, event | category | flops | bytes accessed | tf_op | source)
XLA Modules:
  0.0 25.4 jit_solution(4963651633945238977)
XLA Ops:
  0.0 0.0 copy-start.1
  0.0 0.0 copy-start.2
  0.0 1.1 %copy-done.2 = bf16[2,4,128,256]{3,2,1,0:T(8,128)(2,1)S(1)} copy-done((bf16[2,4,128,256]{3,2,1,0:T(8,128)(2,1)S(1)}, bf16[2,4,128,256]{3,2,1,0:T(8,128)(2,1)}, u32[]{:S(2)}) %copy-start.2) | copy-done | bytes 524312
  1.1 0.0 copy-start.4
  1.1 0.0 copy-start.5
  1.2 3.0 %collective-permute-start.1 = (bf16[2,128,256]{2,1,0:T(8,128)(2,1)S(1)}, bf16[2,128,256]{2,1,0:T(8,128)(2,1)S(1)}, u32[]{:S(2)}, u32[]{:S(2)}) collective-permute-start(bf16[2,128,256]{2,1,0:T(8,128)(2,1)S(1)} %get-tuple-element.43.outer_ref), channel_id=1, source_target_pairs={{0,16},{1,2},{2,1},{3,19},{16,0},{17,18},{18,17},{19,3},{4,20},{5,... | collective-permute-start | bytes 393224 | tf_op jit(solution)/shard_map/ppermute | solution.py:304
  4.2 0.1 collective-permute-start
  4.3 0.0 copy-done.1
  4.3 0.0 copy-done.4
  4.3 0.0 copy-done.5
  4.3 1.3 %shard_map.56 = (f32[2,128,256]{2,1,0:T(8,128)S(1)}, f32[2,2,128,256]{3,2,1,0:T(8,128)S(1)}, f32[2,128,256]{2,1,0:T(8,128)S(1)}, bf16[2,128,256]{2,1,0:T(8,128)(2,1)S(1)}, f32[2,1,256]{2,1,0:T(1,128)S(1)}) custom-call(bf16[2,4,128,256]{3,2,1,0:T(8,128)(2,1)S(1)} %copy-done.2, bf16[3,3,256,256]{3,2,1,0:T(8,128)(2,1)S(1)} %copy-done.1, f32[1,16]{1,0:T(1,128)S(1)} %bitcast.3, ...), custom_call_target="tpu_custom_call" | custom-call | flops 1000 | bytes 1048576 | tf_op jit(solution)/shard_map/pallas_call | solution.py:340
  5.6 1.6 %collective-permute-start.5 = (bf16[2,128,256]{2,1,0:T(8,128)(2,1)S(1)}, bf16[2,128,256]{2,1,0:T(8,128)(2,1)S(1)}, u32[]{:S(2)}, u32[]{:S(2)}) collective-permute-start(bf16[2,128,256]{2,1,0:T(8,128)(2,1)S(1)} %get-tuple-element.52.own_ref), channel_id=1, source_target_pairs={{0,4},{1,5},{2,6},{3,7},{4,0},{5,1},{6,2},{7,3},{8,9},{9,8},{10,11... | collective-permute-start | bytes 393224 | tf_op jit(solution)/shard_map/ppermute | solution.py:291
  7.3 0.0 collective-permute-done.1.halo_ref
  7.3 0.3 %shard_map.57 = (f32[2,128,256]{2,1,0:T(8,128)S(1)}, bf16[128,256]{1,0:T(8,128)(2,1)S(1)}, f32[2,1,256]{2,1,0:T(1,128)S(1)}) custom-call(bf16[2,128,256]{2,1,0:T(8,128)(2,1)S(1)} %collective-permute-done.1.halo_ref, bf16[3,3,256,256]{3,2,1,0:T(8,128)(2,1)S(1)} %copy-done.1, f32[2,1,256]{2,1,0:T(1,128)S(1)} %get-tuple-element.44.growth_ref, ...), custom_call_target="tpu_custom_call" | custom-call | flops 1000 | bytes 1048576 | tf_op jit(solution)/shard_map/pallas_call | solution.py:352
  7.5 3.0 %collective-permute-start.4 = (bf16[128,256]{1,0:T(8,128)(2,1)S(1)}, bf16[128,256]{1,0:T(8,128)(2,1)S(1)}, u32[]{:S(2)}, u32[]{:S(2)}) collective-permute-start(bf16[128,256]{1,0:T(8,128)(2,1)S(1)} %get-tuple-element.51.own_ref), channel_id=1, source_target_pairs={{0,8},{4,12},{8,0},{12,4},{1,9},{5,13},{9,1},{13,5},{2,10},{6,14},... | collective-permute-start | bytes 196616 | tf_op jit(solution)/shard_map/ppermute | solution.py:279
  10.6 0.0 collective-permute-done.halo_ref
  10.6 0.3 %shard_map.58 = (f32[2,128,256]{2,1,0:T(8,128)S(1)}, bf16[128,256]{1,0:T(8,128)(2,1)S(1)}, f32[2,1,256]{2,1,0:T(1,128)S(1)}, bf16[2,128,256]{2,1,0:T(8,128)(2,1)S(1)}) custom-call(bf16[2,128,256]{2,1,0:T(8,128)(2,1)S(1)} %collective-permute-done.halo_ref, bf16[3,3,256,256]{3,2,1,0:T(8,128)(2,1)S(1)} %copy-done.1, ...), custom_call_target="tpu_custom_call" | custom-call | flops 1000 | bytes 1048576 | tf_op jit(solution)/shard_map/pallas_call | solution.py:352
  10.9 1.6 %collective-permute-start.3 = (bf16[128,256]{1,0:T(8,128)(2,1)S(1)}, bf16[128,256]{1,0:T(8,128)(2,1)S(1)}, u32[]{:S(2)}, u32[]{:S(2)}) collective-permute-start(bf16[128,256]{1,0:T(8,128)(2,1)S(1)} %get-tuple-element.50.own_ref), channel_id=1, source_target_pairs={{0,4},{4,0},{8,12},{12,8},{1,5},{5,1},{9,13},{13,9},{2,6},{6,2},{1... | collective-permute-start | bytes 196616 | tf_op jit(solution)/shard_map/ppermute | solution.py:279
  12.5 0.0 collective-permute-start.2
  12.5 1.6 %collective-permute-start.9 = (bf16[2,128,256]{2,1,0:T(8,128)(2,1)S(1)}, bf16[2,128,256]{2,1,0:T(8,128)(2,1)S(1)}, u32[]{:S(2)}, u32[]{:S(2)}) collective-permute-start(bf16[2,128,256]{2,1,0:T(8,128)(2,1)S(1)} %shard_map.62), channel_id=1, source_target_pairs={{0,16},{1,2},{2,1},{3,19},{16,0},{17,18},{18,17},{19,3},{4,20},{5,... | collective-permute-start | bytes 393224 | tf_op jit(solution)/shard_map/ppermute | solution.py:304
  14.1 0.0 collective-permute-done.5.before_ref.first_ref
  14.2 0.1 collective-permute-start.8
  14.3 0.0 collective-permute-done.4.far_ref
  14.3 0.9 %collective-permute-start.7 = (bf16[128,256]{1,0:T(8,128)(2,1)S(1)}, bf16[128,256]{1,0:T(8,128)(2,1)S(1)}, u32[]{:S(2)}, u32[]{:S(2)}) collective-permute-start(bf16[128,256]{1,0:T(8,128)(2,1)S(1)} %get-tuple-element.58), channel_id=1, source_target_pairs={{0,4},{4,0},{8,12},{12,8},{1,5},{5,1},{9,13},{13,9},{2,6},{6,2},{1... | collective-permute-start | bytes 196616 | tf_op jit(solution)/shard_map/ppermute | solution.py:279
  15.3 0.0 collective-permute-done.3.other_ref.near_ref
  15.3 3.0 %collective-permute-start.6 = (bf16[128,256]{1,0:T(8,128)(2,1)S(1)}, bf16[128,256]{1,0:T(8,128)(2,1)S(1)}, u32[]{:S(2)}, u32[]{:S(2)}) collective-permute-start(bf16[128,256]{1,0:T(8,128)(2,1)S(1)} %get-tuple-element.56), channel_id=1, source_target_pairs={{0,8},{4,12},{8,0},{12,4},{1,9},{5,13},{9,1},{13,5},{2,10},{6,14},... | collective-permute-start | bytes 196616 | tf_op jit(solution)/shard_map/ppermute | solution.py:279
  18.3 0.0 collective-permute-done.9.halo_ref.second_ref
  18.3 0.0 collective-permute-done.8.before_ref.second_ref
  18.3 0.1 collective-permute-start.12
  18.4 0.8 %collective-permute-done.7.near_ref = bf16[128,256]{1,0:T(8,128)(2,1)S(1)} collective-permute-done((bf16[128,256]{1,0:T(8,128)(2,1)S(1)}, bf16[128,256]{1,0:T(8,128)(2,1)S(1)}, u32[]{:S(2)}, u32[]{:S(2)}) %collective-permute-start.7) | collective-permute-done | bytes 65568 | tf_op jit(solution)/shard_map/ppermute | solution.py:279
  19.2 0.0 copy-start
  19.2 0.1 shard_map.65
  19.3 0.7 %collective-permute-start.11 = (bf16[128,256]{1,0:T(8,128)(2,1)S(1)}, bf16[128,256]{1,0:T(8,128)(2,1)S(1)}, u32[]{:S(2)}, u32[]{:S(2)}) collective-permute-start(bf16[128,256]{1,0:T(8,128)(2,1)S(1)} %get-tuple-element.68), channel_id=1, source_target_pairs={{0,16},{1,2},{2,1},{3,19},{16,0},{17,18},{18,17},{19,3},{4,20},{5,... | collective-permute-start | bytes 196616 | tf_op jit(solution)/shard_map/ppermute | solution.py:304
  20.0 1.6 %collective-permute-done.6.far_ref = bf16[128,256]{1,0:T(8,128)(2,1)S(1)} collective-permute-done((bf16[128,256]{1,0:T(8,128)(2,1)S(1)}, bf16[128,256]{1,0:T(8,128)(2,1)S(1)}, u32[]{:S(2)}, u32[]{:S(2)}) %collective-permute-start.6) | collective-permute-done | bytes 65568 | tf_op jit(solution)/shard_map/ppermute | solution.py:279
  21.6 0.1 shard_map.66
  21.6 0.1 collective-permute-start.10
  21.7 0.0 copy-done
  21.7 0.0 copy-start.3
  21.7 0.6 %shard_map.68 = (f32[2,128,256]{2,1,0:T(8,128)S(1)}, f32[2,2,128,256]{3,2,1,0:T(8,128)S(1)}, f32[2,128,256]{2,1,0:T(8,128)S(1)}) custom-call(bf16[2,128,256]{2,1,0:T(8,128)(2,1)S(1)} %get-tuple-element.71.outer_in, bf16[2,128,256]{2,1,0:T(8,128)(2,1)S(1)} %get-tuple-element.72.inner_in, bf16[3,3,256,256]{3,2,1,0:T(8,128)(2,1)S(1)} %copy-done), custom_call_target="tpu_custom_call" | custom-call | flops 1000 | bytes 1048576 | tf_op jit(solution)/shard_map/pallas_call | solution.py:401
  22.3 0.5 %shard_map.67 = (f32[2,128,256]{2,1,0:T(8,128)S(1)}, f32[2,1,256]{2,1,0:T(1,128)S(1)}) custom-call(bf16[2,128,256]{2,1,0:T(8,128)(2,1)S(1)} %collective-permute-done.9.halo_ref.second_ref, bf16[2,128,256]{2,1,0:T(8,128)(2,1)S(1)} %collective-permute-done.1.halo_ref, bf16[2,128,256]{2,1,0:T(8,128)(2,1)S(1)} %get-tuple-element.43.outer_ref, ...), custom_call_target="tpu_custom_call" | custom-call | flops 1000 | bytes 1000 | tf_op jit(solution)/shard_map/pallas_call | solution.py:358
  22.8 0.0 collective-permute-done.12.third_ref
  22.8 0.0 copy-done.3
  22.9 1.1 %shard_map.69 = (f32[2,128,256]{2,1,0:T(8,128)S(1)}, bf16[2,2,128,256]{3,2,1,0:T(8,128)(2,1)S(1)}, f32[2,128,256]{2,1,0:T(8,128)S(1)}) custom-call(bf16[2,128,256]{2,1,0:T(8,128)(2,1)S(1)} %collective-permute-done.5.before_ref.first_ref, bf16[2,128,256]{2,1,0:T(8,128)(2,1)S(1)} %collective-permute-done.8.before_ref.second_ref, ...), custom_call_target="tpu_custom_call" | custom-call | flops 1000 | bytes 1048576 | tf_op jit(solution)/shard_map/pallas_call | solution.py:404
  23.9 0.0 collective-permute-done.11.carried_ref
  23.9 0.3 %shard_map.70.outer_ref = f32[2,128,256]{2,1,0:T(8,128)S(1)} custom-call(f32[2,128,256]{2,1,0:T(8,128)S(1)} %get-tuple-element.67.partial_ref, bf16[128,256]{1,0:T(8,128)(2,1)S(1)} %collective-permute-done.11.carried_ref, f32[2,1,256]{2,1,0:T(1,128)S(1)} %get-tuple-element.66.growth_ref, bf16[3,3,256,256]{3,2,1,0:T(8,128)(2,1)S(1)} %copy-done, ...), custom_call_target="tpu_custom_call" | custom-call | flops 1000 | bytes 1048576 | tf_op jit(solution)/shard_map/pallas_call | solution.py:412
  24.2 0.0 collective-permute-done.2.partial_ref
  24.2 0.0 collective-permute-done.10.carried_ref
  24.3 1.2 %shard_map.71 = bf16[2,4,128,256]{3,2,1,0:T(8,128)(2,1)} custom-call(bf16[2,128,256]{2,1,0:T(8,128)(2,1)S(1)} %collective-permute-done.2.partial_ref, bf16[128,256]{1,0:T(8,128)(2,1)S(1)} %collective-permute-done.10.carried_ref, f32[2,1,256]{2,1,0:T(1,128)S(1)} %get-tuple-element.66.growth_ref, bf16[3,3,256,256]{3,2,1,0:T(8,128)(2,1)S(1)} %copy-done, ...), custom_call_target="tpu_custom_call" | custom-call | flops 1000 | bytes 1048576 | tf_op jit(solution)/shard_map/pallas_call | solution.py:415
  (7 shorter events, 0.2 us)
Async XLA Ops:
  0.0 4.3 %copy-start.1 = (bf16[3,3,256,256]{3,2,1,0:T(8,128)(2,1)S(1)}, bf16[3,3,256,256]{3,2,1,0:T(8,128)(2,1)}, u32[]{:S(2)}) copy-start(bf16[3,3,256,256]{3,2,1,0:T(8,128)(2,1)} %w_ref.11) | copy-start | bytes 3538948
  0.0 1.1 %copy-start.2 = (bf16[2,4,128,256]{3,2,1,0:T(8,128)(2,1)S(1)}, bf16[2,4,128,256]{3,2,1,0:T(8,128)(2,1)}, u32[]{:S(2)}) copy-start(bf16[2,4,128,256]{3,2,1,0:T(8,128)(2,1)} %x_ref.7) | copy-start | bytes 1572868
  1.1 3.2 %copy-start.4 = (s32[256]{0:T(256)S(1)}, s32[256]{0:T(256)}, u32[]{:S(2)}) copy-start(s32[256]{0:T(256)} %param.9) | copy-start | bytes 3076
  1.1 3.2 %copy-start.5 = (f32[16]{0:T(128)S(1)}, f32[16]{0:T(128)}, u32[]{:S(2)}) copy-start(f32[16]{0:T(128)} %param.8) | copy-start | bytes 196
  1.2 6.1 %collective-permute-start.1 = (bf16[2,128,256]{2,1,0:T(8,128)(2,1)S(1)}, bf16[2,128,256]{2,1,0:T(8,128)(2,1)S(1)}, u32[]{:S(2)}, u32[]{:S(2)}) collective-permute-start(bf16[2,128,256]{2,1,0:T(8,128)(2,1)S(1)} %get-tuple-element.43.outer_ref), channel_id=1, source_target_pairs={{0,16},{1,2},{2,1},{3,19},{16,0},{17,18},{18,17},{19,3},{4,20},{5,... | collective-permute-start | bytes 393224 | tf_op jit(solution)/shard_map/ppermute | solution.py:304
  4.2 6.4 %collective-permute-start = (bf16[2,128,256]{2,1,0:T(8,128)(2,1)S(1)}, bf16[2,128,256]{2,1,0:T(8,128)(2,1)S(1)}, u32[]{:S(2)}, u32[]{:S(2)}) collective-permute-start(bf16[2,128,256]{2,1,0:T(8,128)(2,1)S(1)} %get-tuple-element.42), channel_id=1, source_target_pairs={{0,1},{1,0},{2,3},{3,2},{4,5},{5,4},{6,7},{7,6},{8,9},{9,8},{10,11... | collective-permute-start | bytes 393224 | tf_op jit(solution)/shard_map/ppermute | solution.py:279
  5.6 8.5 %collective-permute-start.5 = (bf16[2,128,256]{2,1,0:T(8,128)(2,1)S(1)}, bf16[2,128,256]{2,1,0:T(8,128)(2,1)S(1)}, u32[]{:S(2)}, u32[]{:S(2)}) collective-permute-start(bf16[2,128,256]{2,1,0:T(8,128)(2,1)S(1)} %get-tuple-element.52.own_ref), channel_id=1, source_target_pairs={{0,4},{1,5},{2,6},{3,7},{4,0},{5,1},{6,2},{7,3},{8,9},{9,8},{10,11... | collective-permute-start | bytes 393224 | tf_op jit(solution)/shard_map/ppermute | solution.py:291
  7.5 6.7 %collective-permute-start.4 = (bf16[128,256]{1,0:T(8,128)(2,1)S(1)}, bf16[128,256]{1,0:T(8,128)(2,1)S(1)}, u32[]{:S(2)}, u32[]{:S(2)}) collective-permute-start(bf16[128,256]{1,0:T(8,128)(2,1)S(1)} %get-tuple-element.51.own_ref), channel_id=1, source_target_pairs={{0,8},{4,12},{8,0},{12,4},{1,9},{5,13},{9,1},{13,5},{2,10},{6,14},... | collective-permute-start | bytes 196616 | tf_op jit(solution)/shard_map/ppermute | solution.py:279
  10.9 4.4 %collective-permute-start.3 = (bf16[128,256]{1,0:T(8,128)(2,1)S(1)}, bf16[128,256]{1,0:T(8,128)(2,1)S(1)}, u32[]{:S(2)}, u32[]{:S(2)}) collective-permute-start(bf16[128,256]{1,0:T(8,128)(2,1)S(1)} %get-tuple-element.50.own_ref), channel_id=1, source_target_pairs={{0,4},{4,0},{8,12},{12,8},{1,5},{5,1},{9,13},{13,9},{2,6},{6,2},{1... | collective-permute-start | bytes 196616 | tf_op jit(solution)/shard_map/ppermute | solution.py:279
  12.5 11.7 %collective-permute-start.2 = (bf16[2,128,256]{2,1,0:T(8,128)(2,1)S(1)}, bf16[2,128,256]{2,1,0:T(8,128)(2,1)S(1)}, u32[]{:S(2)}, u32[]{:S(2)}) collective-permute-start(bf16[2,128,256]{2,1,0:T(8,128)(2,1)S(1)} %get-tuple-element.48), channel_id=1, source_target_pairs={{0,1},{1,0},{2,3},{3,2},{4,5},{5,4},{6,7},{7,6},{8,9},{9,8},{10,11... | collective-permute-start | bytes 393224 | tf_op jit(solution)/shard_map/ppermute | solution.py:279
  12.5 5.7 %collective-permute-start.9 = (bf16[2,128,256]{2,1,0:T(8,128)(2,1)S(1)}, bf16[2,128,256]{2,1,0:T(8,128)(2,1)S(1)}, u32[]{:S(2)}, u32[]{:S(2)}) collective-permute-start(bf16[2,128,256]{2,1,0:T(8,128)(2,1)S(1)} %shard_map.62), channel_id=1, source_target_pairs={{0,16},{1,2},{2,1},{3,19},{16,0},{17,18},{18,17},{19,3},{4,20},{5,... | collective-permute-start | bytes 393224 | tf_op jit(solution)/shard_map/ppermute | solution.py:304
  14.2 4.1 %collective-permute-start.8 = (bf16[2,128,256]{2,1,0:T(8,128)(2,1)S(1)}, bf16[2,128,256]{2,1,0:T(8,128)(2,1)S(1)}, u32[]{:S(2)}, u32[]{:S(2)}) collective-permute-start(bf16[2,128,256]{2,1,0:T(8,128)(2,1)S(1)} %get-tuple-element.59), channel_id=1, source_target_pairs={{0,1},{1,0},{2,3},{3,2},{4,8},{5,9},{6,10},{7,11},{8,4},{9,5},{10,... | collective-permute-start | bytes 393224 | tf_op jit(solution)/shard_map/ppermute | solution.py:291
  14.3 4.9 %collective-permute-start.7 = (bf16[128,256]{1,0:T(8,128)(2,1)S(1)}, bf16[128,256]{1,0:T(8,128)(2,1)S(1)}, u32[]{:S(2)}, u32[]{:S(2)}) collective-permute-start(bf16[128,256]{1,0:T(8,128)(2,1)S(1)} %get-tuple-element.58), channel_id=1, source_target_pairs={{0,4},{4,0},{8,12},{12,8},{1,5},{5,1},{9,13},{13,9},{2,6},{6,2},{1... | collective-permute-start | bytes 196616 | tf_op jit(solution)/shard_map/ppermute | solution.py:279
  15.3 6.3 %collective-permute-start.6 = (bf16[128,256]{1,0:T(8,128)(2,1)S(1)}, bf16[128,256]{1,0:T(8,128)(2,1)S(1)}, u32[]{:S(2)}, u32[]{:S(2)}) collective-permute-start(bf16[128,256]{1,0:T(8,128)(2,1)S(1)} %get-tuple-element.56), channel_id=1, source_target_pairs={{0,8},{4,12},{8,0},{12,4},{1,9},{5,13},{9,1},{13,5},{2,10},{6,14},... | collective-permute-start | bytes 196616 | tf_op jit(solution)/shard_map/ppermute | solution.py:279
  18.3 4.5 %collective-permute-start.12 = (bf16[2,128,256]{2,1,0:T(8,128)(2,1)S(1)}, bf16[2,128,256]{2,1,0:T(8,128)(2,1)S(1)}, u32[]{:S(2)}, u32[]{:S(2)}) collective-permute-start(bf16[2,128,256]{2,1,0:T(8,128)(2,1)S(1)} %get-tuple-element.69), channel_id=1, source_target_pairs={{0,1},{1,0},{2,3},{3,2},{4,5},{5,4},{6,7},{7,6},{8,12},{9,13},{10,... | collective-permute-start | bytes 393224 | tf_op jit(solution)/shard_map/ppermute | solution.py:291
  19.2 2.5 %copy-start = (bf16[3,3,256,256]{3,2,1,0:T(8,128)(2,1)S(1)}, bf16[3,3,256,256]{3,2,1,0:T(8,128)(2,1)}, u32[]{:S(2)}) copy-start(bf16[3,3,256,256]{3,2,1,0:T(8,128)(2,1)} %w_ref.15) | copy-start | bytes 3538948
  19.3 4.6 %collective-permute-start.11 = (bf16[128,256]{1,0:T(8,128)(2,1)S(1)}, bf16[128,256]{1,0:T(8,128)(2,1)S(1)}, u32[]{:S(2)}, u32[]{:S(2)}) collective-permute-start(bf16[128,256]{1,0:T(8,128)(2,1)S(1)} %get-tuple-element.68), channel_id=1, source_target_pairs={{0,16},{1,2},{2,1},{3,19},{16,0},{17,18},{18,17},{19,3},{4,20},{5,... | collective-permute-start | bytes 196616 | tf_op jit(solution)/shard_map/ppermute | solution.py:304
  21.6 2.6 %collective-permute-start.10 = (bf16[128,256]{1,0:T(8,128)(2,1)S(1)}, bf16[128,256]{1,0:T(8,128)(2,1)S(1)}, u32[]{:S(2)}, u32[]{:S(2)}) collective-permute-start(bf16[128,256]{1,0:T(8,128)(2,1)S(1)} %get-tuple-element.64), channel_id=1, source_target_pairs={{0,1},{1,0},{2,3},{3,2},{4,5},{5,4},{6,7},{7,6},{8,9},{9,8},{10,11... | collective-permute-start | bytes 196616 | tf_op jit(solution)/shard_map/ppermute | solution.py:279
  21.7 1.1 %copy-start.3 = (bf16[2,4,128,256]{3,2,1,0:T(8,128)(2,1)S(1)}, bf16[2,4,128,256]{3,2,1,0:T(8,128)(2,1)}, u32[]{:S(2)}) copy-start(bf16[2,4,128,256]{3,2,1,0:T(8,128)(2,1)} %x_ref.7) | copy-start | bytes 1572868
